TPU v7x, 32 devices: a whole 2x2x4 slice. The times are simulated.
32 devices in a mesh: pose: 8 (over z, y), dom: 4 (over x, core).
Axes of the slice: x: 2, y: 2, z: 4, core: 2. Of those that a mesh axis runs over, the one named last changes fastest.
Arguments:
- particles: bfloat16 [4096, 4096], P(('pose', 'dom')), may hold values from -16 to 16
- candidates: int32 [4096, 2], P(('pose', 'dom')), may hold values from 0 to 15, all different within a row; in each aligned block of 128 rows (0 to 127, 128 to 255, ...) at most 48 rows name the same one
- ctf_ids: int32 [4096], P(('pose', 'dom')), may hold values from 0 to 15
- offsets: int32 [4096, 2, 9], P(('pose', 'dom')), may hold values from -3 to 3
- ctf_table: float32 [16, 2048], replicated, may hold values from -1 to 1
- sigma_sq: float32 [2048], replicated, may hold values from 0.5 to 2
- projections: bfloat16 [16, 256, 4096], P('pose', 'dom'), may hold values from -6 to 6
Outputs:
- class_prob: float32 [4096, 2], P(('pose', 'dom'))
- mean_shift: float32 [4096, 2], P(('pose', 'dom'))
Inputs may be any that keep to these rules, and one draw needn't show every extreme that they name: `candidates`: each particle names 2 different classes; among the rows of one device no class is named by more than 48 rows, and on some device one class is named by exactly 48.
All inputs are finite; a program needn't handle non-finite values.
Results may differ from a plain program's by a relative error of at most 0.0025.
The roundings to bfloat16 on the way count: a program that leaves them out, or rounds other values in their place, can miss the bound.
Values may be sent and summed in bfloat16 or wider, within the bound.
No kernel may reach another device: no remote copies, remote signals or barrier semaphores. Data moves between devices by JAX's collectives and lax.ppermute only.
A program may use at most 192 MiB of HBM per device.

v0:
```python
import jax
import jax.numpy as jnp
from jax import lax
from jax.sharding import PartitionSpec as P

BOX = 128


two_pi = 6.283185307179586
block_pairs = 32
piece_limit = 256
floor_score = -1e30
offset_reach = 3


def join_stats(left_stats, right_stats):
    highest = jnp.maximum(left_stats[0], right_stats[0])
    left_scale = jnp.exp(left_stats[0] - highest)
    right_scale = jnp.exp(right_stats[0] - highest)
    return (
        highest,
        left_stats[1] * left_scale + right_stats[1] * right_scale,
        left_stats[2] * left_scale + right_stats[2] * right_scale,
        left_stats[3] * left_scale + right_stats[3] * right_scale,
    )


def axis_tables(shift_values, freq_row):
    levels = jnp.arange(-offset_reach, offset_reach + 1, dtype=jnp.int32)
    angle_table = levels.astype(jnp.float32)[:, None] * freq_row[None, :]
    chooser = (shift_values[:, :, None] == levels[None, None, :]).astype(jnp.float32)
    cos_rows = jnp.einsum(
        "bto,ok->btk", chooser, jnp.cos(angle_table), precision=lax.Precision.HIGHEST
    )
    sin_rows = jnp.einsum(
        "bto,ok->btk", chooser, jnp.sin(angle_table), precision=lax.Precision.HIGHEST
    )
    return (cos_rows, sin_rows)


def block_stats(particle_rows, shifts, ctf_index, ctf_table, sigma_sq, projection, power_rows):
    pixel_count = sigma_sq.shape[0]
    rows_y = pixel_count // 64
    freq_x = (jnp.arange(64, dtype=jnp.int32) - 32).astype(jnp.float32) * (two_pi / BOX)
    freq_y = jnp.arange(rows_y, dtype=jnp.int32).astype(jnp.float32) * (two_pi / BOX)
    chooser = (
        ctf_index[:, None] == jnp.arange(ctf_table.shape[0], dtype=jnp.int32)[None, :]
    ).astype(jnp.float32)
    ctf_rows = jnp.dot(chooser, ctf_table, precision=lax.Precision.HIGHEST)
    weight = ctf_rows / sigma_sq[None, :]
    damping = weight * ctf_rows
    shift_x = shifts[:, 0, :].astype(jnp.float32)
    shift_y = shifts[:, 1, :].astype(jnp.float32)
    cos_x, sin_x = axis_tables(shifts[:, 0, :], freq_x)
    cos_y, sin_y = axis_tables(shifts[:, 1, :], freq_y)
    pair_count = particle_rows.shape[0]
    trans_count = shifts.shape[2]
    cosine = (
        cos_y[:, :, :, None] * cos_x[:, :, None, :] - sin_y[:, :, :, None] * sin_x[:, :, None, :]
    ).reshape(pair_count, trans_count, pixel_count)
    sine_part = (
        sin_y[:, :, :, None] * cos_x[:, :, None, :] + cos_y[:, :, :, None] * sin_x[:, :, None, :]
    ).reshape(pair_count, trans_count, pixel_count)
    real_part = particle_rows[:, None, :pixel_count].astype(jnp.float32)
    imag_part = particle_rows[:, None, pixel_count:].astype(jnp.float32)
    shifted = jnp.concatenate(
        [
            weight[:, None, :] * (real_part * cosine + imag_part * sine_part),
            weight[:, None, :] * (imag_part * cosine - real_part * sine_part),
        ],
        axis=2,
    ).astype(jnp.bfloat16)
    ori_count = projection.shape[0]
    width = min(piece_limit, ori_count)

    def one_piece(piece_step, running):
        scores = jnp.einsum("btk,ok->bto", shifted, projection, preferred_element_type=jnp.float32)
        penalty = -0.5 * jnp.dot(damping, power_rows.T, precision=lax.Precision.HIGHEST)
        scores = scores + penalty[:, None, :]
        highest = jnp.max(scores, axis=(1, 2))
        exp_terms = jnp.exp(scores - highest[:, None, None])
        per_shift = jnp.sum(exp_terms, axis=2)
        fresh = (
            highest,
            jnp.sum(per_shift, axis=1),
            jnp.sum(per_shift * shift_x, axis=1),
            jnp.sum(per_shift * shift_y, axis=1),
        )
        return join_stats(running, fresh)

    zeros_row = jnp.zeros((pair_count,), jnp.float32)
    initial = (jnp.full((pair_count,), floor_score, jnp.float32), zeros_row, zeros_row, zeros_row)
    return lax.fori_loop(0, ori_count // width, one_piece, initial)


def class_stats(particle_rows, shifts, ctf_index, ctf_table, sigma_sq, projection, power_rows):
    pair_count = particle_rows.shape[0]
    blocks = pair_count // block_pairs

    def one_block(pieces):
        return block_stats(
            pieces[0], pieces[1], pieces[2], ctf_table, sigma_sq, projection, power_rows
        )

    results = lax.map(
        one_block,
        (
            particle_rows.reshape((blocks, block_pairs) + particle_rows.shape[1:]),
            shifts.reshape((blocks, block_pairs) + shifts.shape[1:]),
            ctf_index.reshape(blocks, block_pairs),
        ),
    )
    return tuple((member.reshape(pair_count) for member in results))


def on_device(particles, candidates, ctf_ids, offsets, ctf_table, sigma_sq, projections):
    pose_count = lax.axis_size("pose")
    local_classes = projections.shape[0]
    class_total = local_classes * pose_count
    rows_here = particles.shape[0]
    pick_count = candidates.shape[1]
    capacity = 3 * rows_here * pick_count // class_total
    pixel_count = sigma_sq.shape[0]
    flat_class = candidates.reshape(-1)
    onehot = (flat_class[:, None] == jnp.arange(class_total, dtype=jnp.int32)[None, :]).astype(
        jnp.int32
    )
    earlier = jnp.cumsum(onehot, axis=0) - onehot
    rank_in = jnp.sum(earlier * onehot, axis=1)
    slot_index = flat_class * capacity + rank_in
    slots_all = class_total * capacity
    send_rows = (
        jnp.zeros((slots_all, particles.shape[1]), jnp.bfloat16)
        .at[slot_index]
        .set(jnp.repeat(particles, pick_count, axis=0))
    )
    send_shifts = (
        jnp.zeros((slots_all,) + offsets.shape[1:], jnp.int32)
        .at[slot_index]
        .set(jnp.repeat(offsets, pick_count, axis=0))
    )
    send_ids = (
        jnp.zeros((slots_all,), jnp.int32)
        .at[slot_index]
        .set(jnp.repeat(ctf_ids, pick_count, axis=0))
    )
    layout = (pose_count, local_classes, capacity)
    got_rows, got_shifts, got_ids = (
        lax.all_to_all(
            send_rows.reshape(layout + particles.shape[1:]),
            "pose",
            split_axis=0,
            concat_axis=2,
            tiled=True,
        ),
        lax.all_to_all(
            send_shifts.reshape(layout + offsets.shape[1:]),
            "pose",
            split_axis=0,
            concat_axis=2,
            tiled=True,
        ),
        lax.all_to_all(send_ids.reshape(layout), "pose", split_axis=0, concat_axis=2, tiled=True),
    )
    got_rows = got_rows[0]
    got_shifts = got_shifts[0]
    got_ids = got_ids[0]
    stacked = lax.all_gather(projections, "dom", axis=1, tiled=True)
    wide_real = stacked[:, :, :pixel_count].astype(jnp.float32)
    wide_imag = stacked[:, :, pixel_count:].astype(jnp.float32)
    power_all = wide_real * wide_real + wide_imag * wide_imag
    per_class = [
        class_stats(
            got_rows[index_c],
            got_shifts[index_c],
            got_ids[index_c],
            ctf_table,
            sigma_sq,
            stacked[index_c],
            power_all[index_c],
        )
        for index_c in range(local_classes)
    ]
    stats = tuple(
        (jnp.stack([entry[member] for entry in per_class], axis=0) for member in range(4))
    )
    back = lax.all_to_all(
        tuple((member.reshape((1,) + member.shape) for member in stats)),
        "pose",
        split_axis=2,
        concat_axis=0,
        tiled=True,
    )
    picked = [member.reshape(-1)[slot_index].reshape(rows_here, pick_count) for member in back]
    log_weight = picked[0] + jnp.log(picked[1])
    highest_log = jnp.max(log_weight, axis=1, keepdims=True)
    raw_weight = jnp.exp(log_weight - highest_log)
    class_prob = raw_weight / jnp.sum(raw_weight, axis=1, keepdims=True)
    mean_x = jnp.sum(class_prob * picked[2] / picked[1], axis=1)
    mean_y = jnp.sum(class_prob * picked[3] / picked[1], axis=1)
    return (class_prob, jnp.stack([mean_x, mean_y], axis=1))


def solution(mesh):
    in_specs = (
        P(("pose", "dom"), None),
        P(("pose", "dom"), None),
        P(("pose", "dom")),
        P(("pose", "dom"), None, None),
        P(),
        P(),
        P("pose", "dom", None),
    )
    out_specs = (P(("pose", "dom"), None), P(("pose", "dom"), None))
    return jax.shard_map(
        on_device, mesh=mesh, in_specs=in_specs, out_specs=out_specs, check_vma=False
    )
```

profile of v0, /device:TPU:0, one launch (start us, length us, event | category | flops | bytes accessed | tf_op | source)
XLA Modules:
  0.0 815.3 jit_solution(3255415294174277617)
XLA Ops:
  13.2 7.3 all-to-all-start
  21.8 7.0 scatter_fusion
  30.1 6.0 all-to-all-start.2
  40.4 8.2 %scatter_custom_fusion.1 = bf16[768,4096]{1,0:T(8,128)(2,1)} fusion(s32[256]{0:T(256)S(1)} %bitcast.312, bf16[256,4096]{1,0:T(8,128)(2,1)} %reshape.494, bf16[]{:T(256)} %constant.150.clone.1), kind=kCustom, calls=%fused_computation.162 | custom fusion | bytes 6291968 | tf_op jit(solution)/shard_map/scatter | solution.py:135
  48.7 6.0 all-to-all-start.1
  57.4 35.6 %all-gather.2.cloned.1.call-done = bf16[2,256,4096]{2,1,0:T(8,128)(2,1)} async-done(((bf16[2,64,4096]{2,1,0:T(8,128)(2,1)}), bf16[2,256,4096]{2,1,0:T(8,128)(2,1)}) %all-gather.2.cloned.1.call-update) | async-done | bytes 4194320 | tf_op jit(solution)/shard_map/all_gather | solution.py:168
  102.2 89.6 %all-to-all-done.1 = bf16[8,2,48,4096]{3,2,1,0:T(8,128)(2,1)} async-done(((bf16[8,2,48,4096]{3,2,1,0:T(8,128)(2,1)}), bf16[8,2,48,4096]{3,2,1,0:T(8,128)(2,1)}, u32[]{:S(2)}, u32[]{:S(2)}) %all-to-all-start.1) | async-done | bytes 6291488 | tf_op jit(solution)/shard_map/all_to_all | solution.py:149
  191.8 6.3 fusion.124
  198.1 280.4 %while.36 = (s32[]{:T(128)}, f32[12,32]{1,0:T(8,128)S(1)}, f32[12,32]{1,0:T(8,128)S(1)}, f32[12,32]{1,0:T(8,128)S(1)}, f32[12,32]{1,0:T(8,128)S(1)}, /*index=5*/...) while((s32[]{:T(128)}, f32[12,32]{1,0:T(8,128)S(1)}, ...), condition=%wide.region_12.13_spmd, body=%wide.region_6.12_spmd.sunk | while | flops 837406272 | bytes 48721008 | solution.py:105
  199.8 5.4 multiply_subtract_fusion.4
  209.1 5.1 sub.290
  223.1 5.4 multiply_subtract_fusion.4
  246.5 5.4 multiply_subtract_fusion.4
  269.9 5.4 multiply_subtract_fusion.4
  293.3 5.4 multiply_subtract_fusion.4
  302.5 5.1 sub.290
  316.6 5.4 multiply_subtract_fusion.4
  325.9 5.1 sub.290
  340.0 5.4 multiply_subtract_fusion.4
  349.3 5.1 sub.290
  363.4 5.4 multiply_subtract_fusion.4
  372.6 5.1 sub.290
  386.7 5.4 multiply_subtract_fusion.4
  396.0 5.1 sub.290
  410.1 5.4 multiply_subtract_fusion.4
  419.4 5.1 sub.290
  433.5 5.4 multiply_subtract_fusion.4
  442.7 5.1 sub.290
  456.8 5.4 multiply_subtract_fusion.4
  466.1 5.1 sub.290
  478.6 280.6 %while.37 = (s32[]{:T(128)}, f32[12,32]{1,0:T(8,128)S(1)}, f32[12,32]{1,0:T(8,128)S(1)}, f32[12,32]{1,0:T(8,128)S(1)}, f32[12,32]{1,0:T(8,128)S(1)}, /*index=5*/...) while((s32[]{:T(128)}, f32[12,32]{1,0:T(8,128)S(1)}, ...), condition=%wide.region_19.20_spmd, body=%wide.region_13.19_spmd.sunk | while | flops 837406272 | bytes 48721008 | solution.py:105
  480.5 5.4 multiply_subtract_fusion.5
  489.8 5.1 sub.297
  503.9 5.4 multiply_subtract_fusion.5
  527.3 5.4 multiply_subtract_fusion.5
  550.6 5.4 multiply_subtract_fusion.5
  574.0 5.4 multiply_subtract_fusion.5
  597.4 5.4 multiply_subtract_fusion.5
  620.7 5.4 multiply_subtract_fusion.5
  644.1 5.4 multiply_subtract_fusion.5
  667.5 5.4 multiply_subtract_fusion.5
  690.8 5.4 multiply_subtract_fusion.5
  714.2 5.4 multiply_subtract_fusion.5
  737.6 5.4 multiply_subtract_fusion.5
  746.8 5.1 sub.297
  765.1 6.8 all-to-all-done.3
  788.3 5.9 all-to-all-done.6
  799.5 5.8 all-to-all-done.5
  (816 shorter events, 425.6 us)
Async XLA Ops:
  7.2 28.9 %copy-start.5 = (bf16[128,4096]{1,0:T(8,128)(2,1)S(1)}, bf16[128,4096]{1,0:T(8,128)(2,1)}, u32[]{:S(2)}) copy-start(bf16[128,4096]{1,0:T(8,128)(2,1)} %param.11) | copy-start | bytes 3145732
  13.2 16.9 %all-to-all-start = ((s32[8,2,48]{2,1,0:T(2,128)}), s32[8,2,48]{2,1,0:T(2,128)S(1)}, u32[]{:S(2)}, u32[]{:S(2)}) async-start(s32[8,2,48]{2,1,0:T(2,128)} %reshape.433), calls=%async_computation | async-start | bytes 16384 | tf_op jit(solution)/shard_map/all_to_all | solution.py:163
  30.1 18.6 %all-to-all-start.2 = ((s32[8,1,1728]{2,1,0:T(1,128)}), s32[8,1,1728]{2,1,0:T(1,128)S(1)}, u32[]{:S(2)}, u32[]{:S(2)}) async-start(s32[8,1,1728]{2,1,0:T(1,128)} %reshape.533), calls=%async_computation.2 | async-start | bytes 114688 | tf_op jit(solution)/shard_map/all_to_all | solution.py:156
  48.7 143.1 %all-to-all-start.1 = ((bf16[8,2,48,4096]{3,2,1,0:T(8,128)(2,1)}), bf16[8,2,48,4096]{3,2,1,0:T(8,128)(2,1)}, u32[]{:S(2)}, u32[]{:S(2)}) async-start(bf16[8,2,48,4096]{3,2,1,0:T(8,128)(2,1)} %bitcast.291), calls=%async_computation.1 | async-start | bytes 12582912 | tf_op jit(solution)/shard_map/all_to_all | solution.py:149
  54.7 38.3 %all-gather.2.cloned.1.call-start = ((), (), s32[]{:S(2)}) async-start(), calls=%async_computation.7 | async-start | bytes 5242880 | tf_op jit(solution)/shard_map/all_gather | solution.py:168
  96.0 3.7 copy-start.2
  191.8 6.3 copy-start.6
  191.8 6.3 copy-start.7
  215.5 2.6 copy-start.1
  218.1 2.0 copy-start.4
  238.9 2.6 copy-start.1
  241.5 2.0 copy-start.4
  262.3 2.6 copy-start.1
  264.8 2.0 copy-start.4
  285.6 2.6 copy-start.1
  288.2 2.0 copy-start.4
  309.0 2.6 copy-start.1
  311.6 2.0 copy-start.4
  332.4 2.6 copy-start.1
  334.9 2.0 copy-start.4
  355.7 2.6 copy-start.1
  358.3 2.0 copy-start.4
  379.1 2.6 copy-start.1
  381.7 2.0 copy-start.4
  402.5 2.6 copy-start.1
  405.0 2.0 copy-start.4
  425.8 2.6 copy-start.1
  428.4 2.0 copy-start.4
  449.2 2.6 copy-start.1
  451.8 2.0 copy-start.4
  472.6 2.6 copy-start.1
  475.2 2.0 copy-start.4
  496.3 2.6 copy-start
  519.6 2.6 copy-start
  543.0 2.6 copy-start
  566.4 2.6 copy-start
  589.7 2.6 copy-start
  613.1 2.6 copy-start
  636.5 2.6 copy-start
  659.9 2.6 copy-start
  683.2 2.6 copy-start
  706.6 2.6 copy-start
  730.0 2.6 copy-start
  753.3 2.6 copy-start
  760.2 11.8 %all-to-all-start.3 = ((f32[1,2,384]{1,0,2:T(1,128)}), f32[1,2,384]{1,0,2:T(1,128)S(1)}, u32[]{:S(2)}, u32[]{:S(2)}) async-start(f32[1,2,384]{1,0,2:T(1,128)} %copy.80), calls=%async_computation.3 | async-start | bytes 393216 | tf_op jit(solution)/shard_map/all_to_all | solution.py:187
  771.9 11.1 %all-to-all-start.4 = ((f32[1,2,384]{1,0,2:T(1,128)}), f32[1,2,384]{1,0,2:T(1,128)S(1)}, u32[]{:S(2)}, u32[]{:S(2)}) async-start(f32[1,2,384]{1,0,2:T(1,128)} %copy.83), calls=%async_computation.4 | async-start | bytes 393216 | tf_op jit(solution)/shard_map/all_to_all | solution.py:187
  783.1 11.1 %all-to-all-start.6 = ((f32[1,2,384]{1,0,2:T(1,128)}), f32[1,2,384]{1,0,2:T(1,128)S(1)}, u32[]{:S(2)}, u32[]{:S(2)}) async-start(f32[1,2,384]{1,0,2:T(1,128)} %copy.89), calls=%async_computation.6 | async-start | bytes 393216 | tf_op jit(solution)/shard_map/all_to_all | solution.py:187
  794.2 11.1 %all-to-all-start.5 = ((f32[1,2,384]{1,0,2:T(1,128)}), f32[1,2,384]{1,0,2:T(1,128)S(1)}, u32[]{:S(2)}, u32[]{:S(2)}) async-start(f32[1,2,384]{1,0,2:T(1,128)} %copy.86), calls=%async_computation.5 | async-start | bytes 393216 | tf_op jit(solution)/shard_map/all_to_all | solution.py:187
  (12 other events, 23.5 us)
Sparse Core Ops, SparseCore 0:
  57.1 35.8 all-gather.1
where the time goes:
time: 820 us; the launch traced here: 815 us
  local copies, waits for them, and re-layouts  295 us (36%)
  other arithmetic  206 us (25%)
  waiting for transfers between devices  149 us (18%)
  matrix products  114 us (14%)
  starting transfers between devices  33.3 us (4%)
  between operations  14.4 us (2%)
    sub x24, other arithmetic, block_stats(): cos_y[:, :, :, None] * cos_x[:, :, None, :]  130 us
    sub x24, local copies, waits for them, and re-layouts, block_stats(): cos_y[:, :, :, None] * cos_x[:, :, None, :]  123 us
    add x24, local copies, waits for them, and re-layouts, block_stats(): sin_y[:, :, :, None] * cos_x[:, :, None, :]  92.2 us
    all_to_all x1, waiting for transfers between devices, on_device(): lax.all_to_all(send_rows.reshape(layout + particles.shape[1:]), 'pose', s...  89.6 us
    another operation x26, other arithmetic  61.9 us
    dot_general x24, matrix products, one_piece(): jnp.dot(damping, power_rows.T, precision=lax.Precision.HIGHEST)  46.3 us
    all_gather x1, waiting for transfers between devices, on_device(): stacked = lax.all_gather(projections, 'dom', axis=1, tiled=True)  35.6 us
    squeeze x24, local copies, waits for them, and re-layouts, class_stats(): lax.map(one_block, (particle_rows.reshape((blocks, block_pairs) + particl...  23.4 us
  transfers between devices with their start and end apart: 8, of which 6 were waited for; matrix products, arithmetic and copies ran while one was open for 5% of the time, Pallas kernels for 0%

commit v1 on v0

v1 whole, which is shorter than its diff:
```python
import functools

import jax
import jax.numpy as jnp
import ml_dtypes
import numpy as np
from jax import lax
from jax.experimental import pallas as pl
from jax.experimental.pallas import tpu as pltpu
from jax.sharding import PartitionSpec as P

BOX = 128
GRID_X = 64
REACH = 3
SHARE = 4
TILE = 32
CHUNK = 256
HIGHEST = lax.Precision.HIGHEST


def split_three(values):
    parts = []
    for _ in range(3):
        part = lax.reduce_precision(values, 8, 7)
        parts.append(part.astype(jnp.bfloat16))
        values = values - part
    return parts


def phase_table(pixel_count):
    levels = np.arange(-REACH, REACH + 1)
    pixel = np.arange(pixel_count)
    shift_x = np.repeat(levels, levels.size)[:, None]
    shift_y = np.tile(levels, levels.size)[:, None]
    angle = 2.0 * np.pi / BOX * (shift_x * (pixel % GRID_X - 32) + shift_y * (pixel // GRID_X))
    rest = np.concatenate([np.cos(angle), np.sin(angle)], axis=1).astype(np.float32)
    parts = []
    for _ in range(3):
        part = rest.astype(ml_dtypes.bfloat16)
        parts.append(part)
        rest = rest - part.astype(np.float32)
    rows = np.concatenate(parts, axis=0)
    count = levels.size**2
    padded = np.zeros((256, 2 * pixel_count), ml_dtypes.bfloat16)
    padded[: rows.shape[0]] = rows
    label = np.full((1, 256), -1.0, np.float32)
    label[0, : rows.shape[0]] = np.arange(rows.shape[0]) % count
    return (padded, label)


def swap(values, axis, bit):
    count = lax.axis_size(axis)
    return lax.ppermute(values, axis, [(index, index ^ bit) for index in range(count)])


def stats_kernel(share, pieces, trans, tiles_ref, rank_ref, meta_ref, label_ref, table_ref, wtab_ref,
                 pen_ref, *refs):
    x_refs = refs[:share]
    q_refs = refs[share:share + pieces]
    out_ref, parts, proj, uv, pens, info, stats = refs[share + pieces:]
    step = pl.program_id(0)
    rows_x = x_refs[0].shape[0]
    rows_q = q_refs[0].shape[1]
    slots = uv.shape[0]
    pixels = uv.shape[1] // 2
    rows_all = parts.shape[0]

    @pl.when(step == 0)
    def _():
        for index in range(share):
            parts[index * rows_x:(index + 1) * rows_x, :] = x_refs[index][...]

    for index in range(pieces):
        proj[index * rows_q:(index + 1) * rows_q, :] = q_refs[index][0]

    chosen = rank_ref[0] == lax.broadcasted_iota(jnp.int32, (slots, rows_all), 0)
    pick = jnp.where(chosen, 1.0, 0.0).astype(jnp.bfloat16)
    info[...] = jnp.dot(pick, meta_ref[...], preferred_element_type=jnp.float32)
    group = info[:, trans:trans + 1]
    lane = lax.broadcasted_iota(jnp.int32, (slots, 128), 1)
    group_hot = jnp.where(group == (lane % 16).astype(jnp.float32), 1.0, 0.0)
    group_bf = jnp.where(lane < 48, group_hot, 0.0).astype(jnp.bfloat16)
    pens[...] = jnp.dot(group_hot[:, :16], pen_ref[0], precision=HIGHEST,
                        preferred_element_type=jnp.float32)
    for first in range(0, pixels, CHUNK):
        cols = slice(first, first + CHUNK)
        icols = slice(pixels + first, pixels + first + CHUNK)
        weight = jnp.dot(group_bf, wtab_ref[:, cols], preferred_element_type=jnp.float32)
        uv[:, cols] = weight * jnp.dot(pick, parts[:, cols], preferred_element_type=jnp.float32)
        uv[:, icols] = weight * jnp.dot(pick, parts[:, icols], preferred_element_type=jnp.float32)
    stats[...] = jnp.zeros_like(stats)
    label = label_ref[...]

    @pl.loop(0, tiles_ref[step])
    def _(tile):
        rows = pl.ds(pl.multiple_of(tile * TILE, TILE), TILE)
        here = info[rows, :]
        hot = jnp.concatenate(
            [jnp.where(here[:, t:t + 1] == label, 1.0, 0.0) for t in range(trans)], axis=0
        ).astype(jnp.bfloat16)
        scores = jnp.zeros((trans * TILE, proj.shape[0]), jnp.float32)
        for first in range(0, pixels, CHUNK):
            cols = slice(first, first + CHUNK)
            icols = slice(pixels + first, pixels + first + CHUNK)
            cosine = jnp.dot(hot, table_ref[:, cols], preferred_element_type=jnp.float32)
            sine = jnp.dot(hot, table_ref[:, icols], preferred_element_type=jnp.float32)
            cosine = cosine.reshape(trans, TILE, CHUNK)
            sine = sine.reshape(trans, TILE, CHUNK)
            real = uv[rows, cols][None]
            imag = uv[rows, icols][None]
            shift_re = (real * cosine + imag * sine).astype(jnp.bfloat16)
            shift_im = (imag * cosine - real * sine).astype(jnp.bfloat16)
            contract = (((1,), (1,)), ((), ()))
            scores += lax.dot_general(shift_re.reshape(trans * TILE, CHUNK), proj[:, cols], contract,
                                      preferred_element_type=jnp.float32)
            scores += lax.dot_general(shift_im.reshape(trans * TILE, CHUNK), proj[:, icols], contract,
                                      preferred_element_type=jnp.float32)
        full = scores.reshape(trans, TILE, proj.shape[0]) + pens[rows, :][None]
        highest = jnp.max(jnp.max(full, axis=0), axis=1, keepdims=True)
        total = jnp.zeros((TILE, proj.shape[0]), jnp.float32)
        moment_x = jnp.zeros((TILE, proj.shape[0]), jnp.float32)
        moment_y = jnp.zeros((TILE, proj.shape[0]), jnp.float32)
        for t in range(trans):
            term = jnp.exp(full[t] - highest)
            total += term
            moment_x += term * here[:, trans + 1 + t:trans + 2 + t]
            moment_y += term * here[:, 2 * trans + 1 + t:2 * trans + 2 + t]
        total = jnp.sum(total, axis=1, keepdims=True)
        moment_x = jnp.sum(moment_x, axis=1, keepdims=True)
        moment_y = jnp.sum(moment_y, axis=1, keepdims=True)
        lanes = lax.broadcasted_iota(jnp.int32, (TILE, 128), 1)
        stats[rows, :] = jnp.where(
            lanes == 0, highest,
            jnp.where(lanes == 1, total, jnp.where(lanes == 2, moment_x,
                                                   jnp.where(lanes == 3, moment_y, 0.0))))

    back = lax.dot_general(stats[...], jnp.where(chosen, 1.0, 0.0), (((0,), (0,)), ((), ())),
                           precision=HIGHEST, preferred_element_type=jnp.float32)
    out_ref[0] = back[:8, :]


def class_stats(tiles, rank, meta, label, table, wtab, pen, x_parts, q_parts, trans, slots):
    classes, _, rows_all = rank.shape
    share, pieces = len(x_parts), len(q_parts)
    rows_q, width = q_parts[0].shape[1:]
    whole = lambda array: pl.BlockSpec(array.shape, lambda c, tiles: (0,) * array.ndim)
    per_class = lambda array: pl.BlockSpec((1,) + array.shape[1:], lambda c, tiles: (c, 0, 0))
    ori = rows_q * pieces
    return pl.pallas_call(
        functools.partial(stats_kernel, share, pieces, trans),
        out_shape=jax.ShapeDtypeStruct((classes, 8, rows_all), jnp.float32),
        grid_spec=pltpu.PrefetchScalarGridSpec(
            num_scalar_prefetch=1,
            grid=(classes,),
            in_specs=[per_class(rank), whole(meta), whole(label), whole(table), whole(wtab), per_class(pen)]
            + [whole(array) for array in x_parts]
            + [per_class(array) for array in q_parts],
            out_specs=pl.BlockSpec((1, 8, rows_all), lambda c, tiles: (c, 0, 0)),
            scratch_shapes=[
                pltpu.VMEM((rows_all, width), jnp.bfloat16),
                pltpu.VMEM((ori, width), jnp.bfloat16),
                pltpu.VMEM((slots, width), jnp.float32),
                pltpu.VMEM((slots, ori), jnp.float32),
                pltpu.VMEM((slots, 128), jnp.float32),
                pltpu.VMEM((slots, 128), jnp.float32),
            ],
        ),
        compiler_params=pltpu.CompilerParams(vmem_limit_bytes=56 * 1024 * 1024),
        cost_estimate=pl.CostEstimate(
            flops=classes * slots * trans * width * (ori + 256),
            bytes_accessed=(rows_all + classes * ori) * width * 2,
            transcendentals=0,
        ),
    )(tiles, rank, meta, label, table, wtab, pen, *x_parts, *q_parts)


def on_device(particles, candidates, ctf_ids, offsets, ctf_table, sigma_sq, projections):
    pose_count = lax.axis_size("pose")
    dom_count = lax.axis_size("dom")
    pose = lax.axis_index("pose")
    local = projections.shape[0]
    class_total = local * pose_count
    rows, picks = candidates.shape
    trans = offsets.shape[2]
    pixels = sigma_sq.shape[0]
    capacity = 3 * rows * picks // class_total
    share = min(SHARE, pose_count)
    share_bits = [1 << b for b in range(share.bit_length() - 1)]
    class_bits = [share << b for b in range((pose_count // share).bit_length() - 1)]
    dom_bits = [1 << b for b in range(dom_count.bit_length() - 1)][::-1]
    slots = -(-min(share * capacity, share * rows) // TILE) * TILE

    offset_f = offsets.astype(jnp.float32)
    combo = (offset_f[:, 0] + REACH) * (2 * REACH + 1) + (offset_f[:, 1] + REACH)
    meta = jnp.concatenate(
        [combo, ctf_ids[:, None].astype(jnp.float32), offset_f[:, 0], offset_f[:, 1],
         candidates.astype(jnp.float32)], axis=1)
    meta = jnp.pad(meta, ((0, 0), (0, 128 - meta.shape[1]))).astype(jnp.bfloat16)
    families = [projections]
    for bit in class_bits:
        families += [swap(member, "pose", bit) for member in families]
    x_parts, metas = [particles], meta[None]
    for bit in share_bits[::-1]:
        x_parts = x_parts + [swap(member, "pose", bit) for member in x_parts]
        metas = jnp.concatenate([metas, swap(metas, "pose", bit)], axis=0)
    order = [0]
    for bit in share_bits[::-1]:
        order = order + [member ^ bit for member in order]

    weight = ctf_table / sigma_sq[None, :]
    wide = projections.astype(jnp.float32)
    power = wide[:, :, :pixels] ** 2 + wide[:, :, pixels:] ** 2
    pen = -0.5 * jnp.einsum("gp,cop->cgo", weight * ctf_table, power, precision=HIGHEST)
    pens = pen[None]
    for bit in class_bits:
        pens = jnp.concatenate([pens, swap(pens, "pose", bit)], axis=0)
    for bit in dom_bits:
        pens = jnp.concatenate([pens, swap(pens, "dom", bit)], axis=3)
    group_count = ctf_table.shape[0]
    wtab = jnp.pad(jnp.concatenate(split_three(weight), axis=0), ((0, 128 - 3 * group_count), (0, 0)))

    meta_all = metas.reshape(share * rows, 128)
    named = meta_all[:, 3 * trans + 1:3 * trans + 1 + picks].astype(jnp.int32)
    family_count = len(families)
    owner = pose ^ (jnp.arange(family_count, dtype=jnp.int32) * share)
    class_ids = (owner[:, None] * local + jnp.arange(local, dtype=jnp.int32)[None, :]).reshape(-1)
    names = jnp.any(named.T[None, :, :] == class_ids[:, None, None], axis=1).astype(jnp.int32)
    ahead = jnp.cumsum(names, axis=1)
    rank = jnp.where(names > 0, ahead - 1, -1)[:, None, :]
    tiles = (ahead[:, -1] + (TILE - 1)) // TILE

    table, label = phase_table(pixels)
    table, label = jnp.asarray(table), jnp.asarray(label)
    results = []
    for index in range(family_count):
        q_parts = [families[index]]
        for bit in dom_bits:
            q_parts = q_parts + [swap(member, "dom", bit) for member in q_parts]
        span = slice(index * local, (index + 1) * local)
        results.append(class_stats(tiles[span], rank[span], meta_all, label, table, wtab, pens[index],
                                   x_parts, q_parts, trans, slots))
    stats = jnp.concatenate(results, axis=0)[:, :4, :]

    own = []
    for place, member in enumerate(order):
        block = stats[:, :, place * rows:(place + 1) * rows]
        own.append((member, swap(block, "pose", member) if member else block))
    cand = candidates.T
    owner = cand // local
    beyond = (owner ^ pose) // share
    within = (owner ^ pose) % share
    position = beyond * local + cand % local
    picked = jnp.zeros((picks, 4, rows), jnp.float32)
    for member, block in own:
        for spot in range(family_count * local):
            hit = (within == member) & (position == spot)
            picked = jnp.where(hit[:, None, :], block[spot][None], picked)
    log_weight = picked[:, 0] + jnp.log(picked[:, 1])
    raw_weight = jnp.exp(log_weight - jnp.max(log_weight, axis=0, keepdims=True))
    class_prob = raw_weight / jnp.sum(raw_weight, axis=0, keepdims=True)
    mean_x = jnp.sum(class_prob * picked[:, 2] / picked[:, 1], axis=0)
    mean_y = jnp.sum(class_prob * picked[:, 3] / picked[:, 1], axis=0)
    return (class_prob.T, jnp.stack([mean_x, mean_y], axis=1))


def solution(mesh):
    in_specs = (
        P(("pose", "dom"), None),
        P(("pose", "dom"), None),
        P(("pose", "dom")),
        P(("pose", "dom"), None, None),
        P(),
        P(),
        P("pose", "dom", None),
    )
    out_specs = (P(("pose", "dom"), None), P(("pose", "dom"), None))
    return jax.shard_map(
        on_device, mesh=mesh, in_specs=in_specs, out_specs=out_specs, check_vma=False
    )
```

time: 820 us -> 151 us (0.18)
  local copies, waits for them, and re-layouts: 295 us -> 7.42 us
  other arithmetic: 206 us -> 6.58 us
  matrix products: 114 us -> 1.33 us
  waiting for transfers between devices: 149 us -> 74 us
  Pallas kernels: 0 us -> 46.6 us
  starting transfers between devices: 33.3 us -> 17.2 us
  between operations: 14.4 us -> 0.91 us
    sub x24 -> x0, other arithmetic: 130 us -> none  [block_stats(): cos_y[:, :, :, None] * cos_x[:, :, None, :]]
    sub x24 -> x0, local copies, waits for them, and re-layouts: 123 us -> none  [block_stats(): cos_y[:, :, :, None] * cos_x[:, :, None, :]]
    dot_general x168 -> x1, matrix products: 114 us -> 1.33 us  [on_device(): jnp.einsum('gp,cop->cgo', weight * ctf_table, power, precision=HIGHEST)]
    all_to_all x7 -> x0, waiting for transfers between devices: 112 us -> none  [the longest x1 89.6 us: on_device(): lax.all_to_all(send_rows.reshape(layout + particles.shape[1:]), 'pose', s...]
    add x24 -> x1, local copies, waits for them, and re-layouts: 92.2 us -> 0.08 us  [on_device(): owner[:, None] * local + jnp.arange(local, dtype=jnp.int32)[None, :]]
    ppermute x0 -> x18, waiting for transfers between devices: none -> 74 us  [swap(): lax.ppermute(values, axis, [(index, index ^ bit) for index in range(count)])]
    another operation x27 -> x5, other arithmetic: 62.5 us -> 1.99 us
    pallas_call x0 -> x2, Pallas kernels: none -> 46.6 us  [class_stats(): pl.pallas_call(functools.partial(stats_kernel, share, pieces, trans), out...]
  transfers between devices with their start and end apart: 8 -> 18, of which waited for: 6 -> 9; matrix products, arithmetic and copies ran while one was open for 5% -> 7% of each run, Pallas kernels for 0% -> 15%
where the time goes in v1:
time: 151 us; the launch traced here: 154 us
  waiting for transfers between devices  74 us (49%)
  Pallas kernels  46.6 us (31%)
  starting transfers between devices  17.2 us (11%)
  local copies, waits for them, and re-layouts  7.42 us (5%)
  other arithmetic  6.58 us (4%)
    ppermute x18, waiting for transfers between devices, swap(): lax.ppermute(values, axis, [(index, index ^ bit) for index in range(count)])  74 us
    pallas_call x2, Pallas kernels, class_stats(): pl.pallas_call(functools.partial(stats_kernel, share, pieces, trans), out...  46.6 us
    ppermute x18, starting transfers between devices, swap(): lax.ppermute(values, axis, [(index, index ^ bit) for index in range(count)])  17.2 us
  transfers between devices with their start and end apart: 18, of which 9 were waited for; matrix products, arithmetic and copies ran while one was open for 7% of the time, Pallas kernels for 15%

profile of v1, /device:TPU:0, one launch (start us, length us, event | category | flops | bytes accessed | tf_op | source)
XLA Modules:
  0.0 154.1 jit_solution(4061620177253967809)
XLA Ops:
  0.7 3.1 %collective-permute-start.5 = (bf16[128,4096]{1,0:T(8,128)(2,1)}, bf16[128,4096]{1,0:T(8,128)(2,1)S(1)}, u32[]{:S(2)}, u32[]{:S(2)}) collective-permute-start(bf16[128,4096]{1,0:T(8,128)(2,1)} %refs_0_.3), channel_id=1, source_target_pairs={{0,8},{4,12},{8,0},{12,4},{16,24},{20,28},{24,16},{28,20},{1,9},{5... | collective-permute-start | bytes 3145736 | tf_op jit(solution)/shard_map/ppermute | solution.py:53
  3.8 1.5 collective-permute-start.6
  5.3 2.6 %collective-permute-start.11 = (bf16[2,64,4096]{2,1,0:T(8,128)(2,1)}, bf16[2,64,4096]{2,1,0:T(8,128)(2,1)}, u32[]{:S(2)}, u32[]{:S(2)}) collective-permute-start(bf16[2,64,4096]{2,1,0:T(8,128)(2,1)} %refs_4_.1), channel_id=1, source_target_pairs={{0,16},{4,20},{8,24},{12,28},{16,0},{20,4},{24,8},{28,12},{1,17},{... | collective-permute-start | bytes 3145736 | tf_op jit(solution)/shard_map/ppermute | solution.py:53
  7.9 1.5 collective-permute-start.8
  9.4 1.5 convert_element_type.49
  10.9 1.3 fusion
  12.2 0.4 collective-permute-start.2
  12.8 0.9 fusion.7.wtab_ref
  13.8 0.3 concatenate.27
  14.1 39.9 %collective-permute-done.2 = f32[1,2,16,64]{3,2,1,0:T(8,128)S(1)} collective-permute-done((f32[1,2,16,64]{3,2,1,0:T(8,128)S(1)}, f32[1,2,16,64]{3,2,1,0:T(8,128)S(1)}, u32[]{:S(2)}, u32[]{:S(2)}) %collective-permute-start.2) | collective-permute-done | bytes 8224 | tf_op jit(solution)/shard_map/ppermute | solution.py:53
  54.0 1.5 collective-permute-start.3
  55.5 2.3 %collective-permute-done.3 = f32[2,2,16,64]{3,2,1,0:T(8,128)S(1)} collective-permute-done((f32[2,2,16,64]{3,2,1,0:T(8,128)S(1)}, f32[2,2,16,64]{3,2,1,0:T(8,128)S(1)}, u32[]{:S(2)}, u32[]{:S(2)}) %collective-permute-start.3) | collective-permute-done | bytes 16416 | tf_op jit(solution)/shard_map/ppermute | solution.py:53
  57.9 3.8 %collective-permute-done = bf16[1,128,128]{1,2,0:T(8,128)(2,1)S(1)} collective-permute-done((bf16[1,128,128]{1,2,0:T(8,128)(2,1)S(1)}, bf16[1,128,128]{1,2,0:T(8,128)(2,1)S(1)}, u32[]{:S(2)}, u32[]{:S(2)}) %collective-permute-start) | collective-permute-done | bytes 32800 | tf_op jit(solution)/shard_map/ppermute | solution.py:53
  61.8 1.2 collective-permute-done.4
  63.0 0.5 collective-permute-start.1
  63.5 0.1 pad_maximum_fusion.2
  63.6 0.6 slice_bitcast_fusion
  64.2 3.0 %collective-permute-done.1 = bf16[2,128,128]{1,2,0:T(8,128)(2,1)S(1)} collective-permute-done((bf16[2,128,128]{1,2,0:T(8,128)(2,1)S(1)}, bf16[2,128,128]{1,2,0:T(8,128)(2,1)S(1)}, u32[]{:S(2)}, u32[]{:S(2)}) %collective-permute-start.1) | collective-permute-done | bytes 65568 | tf_op jit(solution)/shard_map/ppermute | solution.py:53
  67.3 0.1 copy.23
  67.4 0.1 convert_bitcast_fusion
  67.5 0.1 copy.24
  67.7 0.1 compare_reduce_fusion
  67.8 1.2 reduce-window.6
  69.0 1.5 collective-permute-start.12
  70.5 0.2 slice_reduce_fusion
  70.8 0.2 reduce-window.9
  70.9 0.5 collective-permute-start.7
  71.6 0.6 slice.149.rank_ref
  72.2 0.6 copy.25.rank_ref
  72.8 0.2 fusion.15
  73.0 0.6 collective-permute-start.13
  73.5 21.4 %collective-permute-done.12.refs_5_ = bf16[2,64,4096]{2,1,0:T(8,128)(2,1)} collective-permute-done((bf16[2,64,4096]{2,1,0:T(8,128)(2,1)}, bf16[2,64,4096]{2,1,0:T(8,128)(2,1)}, u32[]{:S(2)}, u32[]{:S(2)}) %collective-permute-start.12) | collective-permute-done | bytes 1048608 | tf_op jit(solution)/shard_map/ppermute | solution.py:53
  94.9 0.6 fusion.39
  95.5 0.7 collective-permute-done.7.refs_3_
  96.3 1.0 copy-done.8
  97.3 0.4 copy-done.9
  97.7 23.2 %shard_map.104 = f32[2,8,512]{2,1,0:T(8,128)} custom-call(s32[2]{0:T(128)} %get-tuple-element.61.tiles_ref, s32[2,1,512]{2,1,0:T(1,128)} %copy.25.rank_ref, bf16[512,128]{1,0:T(8,128)(2,1)} %bitcast.123, f32[1,256]{1,0:T(1,128)} %constant.101.clone.label_ref, bf16[256,4096]{1,0:T(8,128)(2,1)} %constant.100.clone.table_ref, ...), custom_call_target="tpu_custom_call" | custom-call | flops 7247757312 | bytes 8388608 | tf_op jit(solution)/shard_map/pallas_call | solution.py:149
  120.9 0.7 slice_bitcast_fusion.4
  121.6 1.0 copy-done.10
  122.6 0.3 copy-done.11
  122.9 23.4 %shard_map.105 = f32[2,8,512]{2,1,0:T(8,128)} custom-call(s32[2]{0:T(128)} %get-tuple-element.60.tiles_ref, s32[2,1,512]{2,1,0:T(1,128)} %slice.149.rank_ref, bf16[512,128]{1,0:T(8,128)(2,1)} %bitcast.124, f32[1,256]{1,0:T(1,128)} %constant.101.clone.label_ref, bf16[256,4096]{1,0:T(8,128)(2,1)} %constant.100.clone.table_ref, ...), custom_call_target="tpu_custom_call" | custom-call | flops 7247757312 | bytes 8388608 | tf_op jit(solution)/shard_map/pallas_call | solution.py:149
  146.3 0.7 pad_maximum_fusion.7
  147.0 0.7 slice_bitcast_fusion.6
  147.7 3.5 %collective-permute-start.17 = (f32[4,4,128]{2,1,0:T(4,128)S(1)}, f32[4,4,128]{2,1,0:T(4,128)S(1)}, u32[]{:S(2)}, u32[]{:S(2)}) collective-permute-start(f32[4,4,128]{2,1,0:T(4,128)S(1)} %get-tuple-element.29), channel_id=1, source_target_pairs={{0,8},{4,12},{8,0},{12,4},{16,24},{20,28},{24,16},{28,20},{1,9},{5... | collective-permute-start | bytes 24584 | tf_op jit(solution)/shard_map/ppermute | solution.py:53
  151.2 0.4 collective-permute-done.15
  151.6 1.2 collective-permute-done.17
  152.9 0.6 fusion.23
  153.5 0.6 pad_maximum_fusion.8
  (68 shorter events, 0.7 us)
Async XLA Ops:
  0.6 10.2 %copy-start.2 = (f32[16,2048]{1,0:T(8,128)S(1)}, f32[16,2048]{1,0:T(8,128)}, u32[]{:S(2)}) copy-start(f32[16,2048]{1,0:T(8,128)} %param.13) | copy-start | bytes 393220
  0.6 10.2 %copy-start.5 = (f32[2048]{0:T(1024)S(1)}, f32[2048]{0:T(1024)}, u32[]{:S(2)}) copy-start(f32[2048]{0:T(1024)} %param.14) | copy-start | bytes 24580
  0.7 11.9 %copy-start.4 = (s32[128,2,9]{0,1,2:T(2,128)S(1)}, s32[128,2,9]{0,1,2:T(2,128)}, u32[]{:S(2)}) copy-start(s32[128,2,9]{0,1,2:T(2,128)} %param.12) | copy-start | bytes 27652
  0.7 12.0 %copy-start.6 = (s32[128,2]{0,1:T(2,128)S(1)}, s32[128,2]{0,1:T(2,128)}, u32[]{:S(2)}) copy-start(s32[128,2]{0,1:T(2,128)} %param.10) | copy-start | bytes 3076
  0.7 70.3 %collective-permute-start.5 = (bf16[128,4096]{1,0:T(8,128)(2,1)}, bf16[128,4096]{1,0:T(8,128)(2,1)S(1)}, u32[]{:S(2)}, u32[]{:S(2)}) collective-permute-start(bf16[128,4096]{1,0:T(8,128)(2,1)} %refs_0_.3), channel_id=1, source_target_pairs={{0,8},{4,12},{8,0},{12,4},{16,24},{20,28},{24,16},{28,20},{1,9},{5... | collective-permute-start | bytes 3145736 | tf_op jit(solution)/shard_map/ppermute | solution.py:53
  3.8 69.2 %collective-permute-start.6 = (bf16[128,4096]{1,0:T(8,128)(2,1)}, bf16[128,4096]{1,0:T(8,128)(2,1)}, u32[]{:S(2)}, u32[]{:S(2)}) collective-permute-start(bf16[128,4096]{1,0:T(8,128)(2,1)} %refs_0_.3), channel_id=1, source_target_pairs={{0,4},{4,0},{8,12},{12,8},{16,20},{20,16},{24,28},{28,24},{1,5},{5... | collective-permute-start | bytes 3145736 | tf_op jit(solution)/shard_map/ppermute | solution.py:53
  5.3 63.7 %collective-permute-start.11 = (bf16[2,64,4096]{2,1,0:T(8,128)(2,1)}, bf16[2,64,4096]{2,1,0:T(8,128)(2,1)}, u32[]{:S(2)}, u32[]{:S(2)}) collective-permute-start(bf16[2,64,4096]{2,1,0:T(8,128)(2,1)} %refs_4_.1), channel_id=1, source_target_pairs={{0,16},{4,20},{8,24},{12,28},{16,0},{20,4},{24,8},{28,12},{1,17},{... | collective-permute-start | bytes 3145736 | tf_op jit(solution)/shard_map/ppermute | solution.py:53
  7.9 63.6 %collective-permute-start.8 = (bf16[2,64,4096]{2,1,0:T(8,128)(2,1)}, bf16[2,64,4096]{2,1,0:T(8,128)(2,1)}, u32[]{:S(2)}, u32[]{:S(2)}) collective-permute-start(bf16[2,64,4096]{2,1,0:T(8,128)(2,1)} %refs_4_.1), channel_id=1, source_target_pairs={{0,2},{1,3},{2,0},{3,1},{4,6},{5,7},{6,4},{7,5},{8,10},{9,11},{10,... | collective-permute-start | bytes 3145736 | tf_op jit(solution)/shard_map/ppermute | solution.py:53
  10.8 2.9 %copy-start.12 = (s32[128]{0:T(128)S(1)}, s32[128]{0:T(128)}, u32[]{:S(2)}) copy-start(s32[128]{0:T(128)} %param.11) | copy-start | bytes 1540
  10.9 56.4 %copy-start = (bf16[2,64,4096]{2,1,0:T(8,128)(2,1)S(1)}, bf16[2,64,4096]{2,1,0:T(8,128)(2,1)}, u32[]{:S(2)}) copy-start(bf16[2,64,4096]{2,1,0:T(8,128)(2,1)} %refs_4_.1) | copy-start | bytes 3145732
  12.2 41.7 %collective-permute-start.2 = (f32[1,2,16,64]{3,2,1,0:T(8,128)S(1)}, f32[1,2,16,64]{3,2,1,0:T(8,128)S(1)}, u32[]{:S(2)}, u32[]{:S(2)}) collective-permute-start(f32[1,2,16,64]{3,2,1,0:T(8,128)S(1)} %fusion), channel_id=1, source_target_pairs={{0,16},{4,20},{8,24},{12,28},{16,0},{20,4},{24,8},{28,12},{1,17},{... | collective-permute-start | bytes 24584 | tf_op jit(solution)/shard_map/ppermute | solution.py:53
  54.0 3.9 %collective-permute-start.3 = (f32[2,2,16,64]{3,2,1,0:T(8,128)S(1)}, f32[2,2,16,64]{3,2,1,0:T(8,128)S(1)}, u32[]{:S(2)}, u32[]{:S(2)}) collective-permute-start(f32[2,2,16,64]{3,2,1,0:T(8,128)S(1)} %pad_maximum_fusion.3), channel_id=1, source_target_pairs={{0,2},{1,3},{2,0},{3,1},{4,6},{5,7},{6,4},{7,5},{8,10},{9,11},{10,... | collective-permute-start | bytes 49160 | tf_op jit(solution)/shard_map/ppermute | solution.py:53
  57.9 3.9 %collective-permute-start = (bf16[1,128,128]{1,2,0:T(8,128)(2,1)S(1)}, bf16[1,128,128]{1,2,0:T(8,128)(2,1)S(1)}, u32[]{:S(2)}, u32[]{:S(2)}) collective-permute-start(bf16[1,128,128]{1,2,0:T(8,128)(2,1)S(1)} %pad_bitcast_fusion), channel_id=1, source_target_pairs={{0,8},{4,12},{8,0},{12,4},{16,24},{20,28},{24,16},{28,20},{1,9},{5... | collective-permute-start | bytes 98312 | tf_op jit(solution)/shard_map/ppermute | solution.py:53
  61.8 1.2 collective-permute-start.4
  63.0 4.3 %collective-permute-start.1 = (bf16[2,128,128]{1,2,0:T(8,128)(2,1)S(1)}, bf16[2,128,128]{1,2,0:T(8,128)(2,1)S(1)}, u32[]{:S(2)}, u32[]{:S(2)}) collective-permute-start(bf16[2,128,128]{1,2,0:T(8,128)(2,1)S(1)} %pad_maximum_fusion.1), channel_id=1, source_target_pairs={{0,4},{4,0},{8,12},{12,8},{16,20},{20,16},{24,28},{28,24},{1,5},{5... | collective-permute-start | bytes 196616 | tf_op jit(solution)/shard_map/ppermute | solution.py:53
  67.3 28.3 %collective-permute-start.9 = (bf16[2,64,4096]{2,1,0:T(8,128)(2,1)S(1)}, bf16[2,64,4096]{2,1,0:T(8,128)(2,1)}, u32[]{:S(2)}, u32[]{:S(2)}) collective-permute-start(bf16[2,64,4096]{2,1,0:T(8,128)(2,1)S(1)} %copy-done), channel_id=1, source_target_pairs={{0,1},{1,0},{2,3},{3,2},{4,5},{5,4},{6,7},{7,6},{8,9},{9,8},{10,11... | collective-permute-start | bytes 3145736 | tf_op jit(solution)/shard_map/ppermute | solution.py:53
  67.4 28.9 %copy-start.1 = (bf16[4,128,128]{2,1,0:T(8,128)(2,1)}, bf16[4,128,128]{2,1,0:T(8,128)(2,1)S(1)}, u32[]{:S(2)}) copy-start(bf16[4,128,128]{2,1,0:T(8,128)(2,1)S(1)} %copy.23) | copy-start | bytes 393220
  69.0 25.9 %collective-permute-start.12 = (bf16[2,64,4096]{2,1,0:T(8,128)(2,1)}, bf16[2,64,4096]{2,1,0:T(8,128)(2,1)}, u32[]{:S(2)}, u32[]{:S(2)}) collective-permute-start(bf16[2,64,4096]{2,1,0:T(8,128)(2,1)} %collective-permute-done.11.refs_4_), channel_id=1, source_target_pairs={{0,2},{1,3},{2,0},{3,1},{4,6},{5,7},{6,4},{7,5},{8,10},{9,11},{10,... | collective-permute-start | bytes 3145736 | tf_op jit(solution)/shard_map/ppermute | solution.py:53
  70.9 25.3 %copy-start.7 = (bf16[128,4096]{1,0:T(8,128)(2,1)}, bf16[128,4096]{1,0:T(8,128)(2,1)S(1)}, u32[]{:S(2)}) copy-start(bf16[128,4096]{1,0:T(8,128)(2,1)S(1)} %collective-permute-done.5.refs_1_) | copy-start | bytes 3145732
  70.9 25.3 %collective-permute-start.7 = (bf16[128,4096]{1,0:T(8,128)(2,1)S(1)}, bf16[128,4096]{1,0:T(8,128)(2,1)S(1)}, u32[]{:S(2)}, u32[]{:S(2)}) collective-permute-start(bf16[128,4096]{1,0:T(8,128)(2,1)S(1)} %collective-permute-done.5.refs_1_), channel_id=1, source_target_pairs={{0,4},{4,0},{8,12},{12,8},{16,20},{20,16},{24,28},{28,24},{1,5},{5... | collective-permute-start | bytes 3145736 | tf_op jit(solution)/shard_map/ppermute | solution.py:53
  71.5 24.8 %collective-permute-start.10 = (bf16[2,64,4096]{2,1,0:T(8,128)(2,1)}, bf16[2,64,4096]{2,1,0:T(8,128)(2,1)S(1)}, u32[]{:S(2)}, u32[]{:S(2)}) collective-permute-start(bf16[2,64,4096]{2,1,0:T(8,128)(2,1)} %collective-permute-done.8.refs_5_), channel_id=1, source_target_pairs={{0,1},{1,0},{2,3},{3,2},{4,5},{5,4},{6,7},{7,6},{8,9},{9,8},{10,11... | collective-permute-start | bytes 3145736 | tf_op jit(solution)/shard_map/ppermute | solution.py:53
  73.0 48.6 %collective-permute-start.13 = (bf16[2,64,4096]{2,1,0:T(8,128)(2,1)}, bf16[2,64,4096]{2,1,0:T(8,128)(2,1)S(1)}, u32[]{:S(2)}, u32[]{:S(2)}) collective-permute-start(bf16[2,64,4096]{2,1,0:T(8,128)(2,1)} %collective-permute-done.11.refs_4_), channel_id=1, source_target_pairs={{0,1},{1,0},{2,3},{3,2},{4,5},{5,4},{6,7},{7,6},{8,9},{9,8},{10,11... | collective-permute-start | bytes 3145736 | tf_op jit(solution)/shard_map/ppermute | solution.py:53
  94.9 26.6 %collective-permute-start.14 = (bf16[2,64,4096]{2,1,0:T(8,128)(2,1)}, bf16[2,64,4096]{2,1,0:T(8,128)(2,1)S(1)}, u32[]{:S(2)}, u32[]{:S(2)}) collective-permute-start(bf16[2,64,4096]{2,1,0:T(8,128)(2,1)} %collective-permute-done.12.refs_5_), channel_id=1, source_target_pairs={{0,1},{1,0},{2,3},{3,2},{4,5},{5,4},{6,7},{7,6},{8,9},{9,8},{10,11... | collective-permute-start | bytes 3145736 | tf_op jit(solution)/shard_map/ppermute | solution.py:53
  96.3 1.0 copy-start.8
  96.3 1.4 copy-start.9
  121.6 1.0 copy-start.10
  121.6 1.3 copy-start.11
  122.9 23.4 %copy-start.3 = (f32[2,8,512]{2,1,0:T(8,128)S(1)}, f32[2,8,512]{2,1,0:T(8,128)}, u32[]{:S(2)}) copy-start(f32[2,8,512]{2,1,0:T(8,128)} %shard_map.104) | copy-start | bytes 98308
  147.0 4.5 %collective-permute-start.15 = (f32[4,4,128]{2,1,0:T(4,128)S(1)}, f32[4,4,128]{2,1,0:T(4,128)S(1)}, u32[]{:S(2)}, u32[]{:S(2)}) collective-permute-start(f32[4,4,128]{2,1,0:T(4,128)S(1)} %get-tuple-element.27), channel_id=1, source_target_pairs={{0,12},{4,8},{8,4},{12,0},{16,28},{20,24},{24,20},{28,16},{1,13},{... | collective-permute-start | bytes 24584 | tf_op jit(solution)/shard_map/ppermute | solution.py:53
  147.7 3.9 %collective-permute-start.16 = (f32[4,4,128]{2,1,0:T(4,128)S(1)}, f32[4,4,128]{2,1,0:T(4,128)S(1)}, u32[]{:S(2)}, u32[]{:S(2)}) collective-permute-start(f32[4,4,128]{2,1,0:T(4,128)S(1)} %get-tuple-element.28), channel_id=1, source_target_pairs={{0,4},{4,0},{8,12},{12,8},{16,20},{20,16},{24,28},{28,24},{1,5},{5... | collective-permute-start | bytes 24584 | tf_op jit(solution)/shard_map/ppermute | solution.py:53
  147.7 5.1 %collective-permute-start.17 = (f32[4,4,128]{2,1,0:T(4,128)S(1)}, f32[4,4,128]{2,1,0:T(4,128)S(1)}, u32[]{:S(2)}, u32[]{:S(2)}) collective-permute-start(f32[4,4,128]{2,1,0:T(4,128)S(1)} %get-tuple-element.29), channel_id=1, source_target_pairs={{0,8},{4,12},{8,0},{12,4},{16,24},{20,28},{24,16},{28,20},{1,9},{5... | collective-permute-start | bytes 24584 | tf_op jit(solution)/shard_map/ppermute | solution.py:53

commit v2 on v1

v2 whole, which is shorter than its diff:
```python
import functools

import jax
import jax.numpy as jnp
import ml_dtypes
import numpy as np
from jax import lax
from jax.experimental import pallas as pl
from jax.experimental.pallas import tpu as pltpu
from jax.sharding import PartitionSpec as P

BOX = 128
GRID_X = 64
REACH = 3
SHARE = 4
TILE = 32
CHUNK = 512
LANES = 128
STRIDE = 4
HIGHEST = lax.Precision.HIGHEST


def split_three(values):
    parts = []
    for _ in range(3):
        part = lax.reduce_precision(values, 8, 7)
        parts.append(part.astype(jnp.bfloat16))
        values = values - part
    return parts


def phase_table(pixel_count):
    levels = np.arange(-REACH, REACH + 1)
    starts = np.arange(0, pixel_count, STRIDE * LANES)
    pixel = starts[:, None] + np.arange(LANES)[None, :]
    shift_x = np.repeat(levels, levels.size)[:, None, None]
    shift_y = np.tile(levels, levels.size)[:, None, None]
    angle = shift_x * (pixel % GRID_X - GRID_X // 2) + shift_y * (pixel // GRID_X)
    onward = np.broadcast_to(shift_y * (LANES // GRID_X), (levels.size**2, 1, LANES))
    angle = 2.0 * np.pi / BOX * np.concatenate([angle, onward], axis=1)
    rest = np.stack([np.cos(angle), np.sin(angle)], axis=2).reshape(levels.size**2, -1).astype(np.float32)
    parts = []
    for _ in range(3):
        part = rest.astype(ml_dtypes.bfloat16)
        parts.append(part)
        rest = rest - part.astype(np.float32)
    rows = np.concatenate(parts, axis=0)
    count = levels.size**2
    padded = np.zeros((256, rows.shape[1]), ml_dtypes.bfloat16)
    padded[: rows.shape[0]] = rows
    label = np.full((1, 256), -1.0, np.float32)
    label[0, : rows.shape[0]] = np.arange(rows.shape[0]) % count
    return (padded, label)


def swap(values, axis, bit):
    count = lax.axis_size(axis)
    return lax.ppermute(values, axis, [(index, index ^ bit) for index in range(count)])


def stats_kernel(trans, spots, share, tiles_ref, rank_ref, meta_ref, label_ref, table_ref, wtab_ref,
                 dtab_ref, *refs):
    x_refs = refs[:share]
    q_refs = refs[share:share + len(spots)]
    out_ref, uv, pens, info, stats, phase, shifted, moved = refs[share + len(spots):]
    rows_all = rank_ref.shape[1]
    slots = uv.shape[0]
    pixels = uv.shape[1] // 2
    ori = pens.shape[1]
    groups = dtab_ref.shape[0] // 3
    contract = (((1,), (1,)), ((), ()))

    def particles(cols):
        return jnp.concatenate([member[:, cols] for member in x_refs], axis=0)

    def views(cols):
        return jnp.concatenate([member[spot, :, cols] for member, spot in zip(q_refs, spots)], axis=0)

    def three(values):
        high = values.astype(jnp.bfloat16)
        rest = values - high.astype(jnp.float32)
        middle = rest.astype(jnp.bfloat16)
        return [high, middle, (rest - middle.astype(jnp.float32)).astype(jnp.bfloat16)]

    row = lax.broadcasted_iota(jnp.int32, (slots, rows_all), 0)
    pick = jnp.where(rank_ref[...] == row, 1.0, 0.0).astype(jnp.bfloat16)
    info[...] = jnp.dot(pick, meta_ref[...], preferred_element_type=jnp.float32)
    lane = lax.broadcasted_iota(jnp.int32, (slots, 3 * groups), 1)
    group_hot = jnp.where(info[:, trans:trans + 1] == (lane % groups).astype(jnp.float32), 1.0, 0.0)
    group_hot = group_hot.astype(jnp.bfloat16)
    stats[...] = jnp.zeros_like(stats)
    parted = jnp.zeros((3 * groups, ori), jnp.float32)
    for first in range(0, pixels, CHUNK):
        cols, icols = slice(first, first + CHUNK), slice(pixels + first, pixels + first + CHUNK)
        weight = jnp.dot(group_hot, wtab_ref[:, cols], preferred_element_type=jnp.float32)
        for span in (cols, icols):
            uv[:, span] = weight * jnp.dot(pick, particles(span), preferred_element_type=jnp.float32)
        real = views(cols).astype(jnp.float32)
        imag = views(icols).astype(jnp.float32)
        power = real * real + imag * imag
        for part in three(power)[:2]:
            parted += lax.dot_general(dtab_ref[:, cols], part, contract, preferred_element_type=jnp.float32)
    penalty = -0.5 * (parted[:groups] + parted[groups:2 * groups] + parted[2 * groups:])
    pens[...] = jnp.dot(group_hot, jnp.concatenate(three(penalty), axis=0),
                        preferred_element_type=jnp.float32)

    label = label_ref[...]
    lanes = lax.broadcasted_iota(jnp.int32, (TILE, 128), 1)
    steps = pixels // LANES

    @pl.loop(0, tiles_ref[0])
    def _(tile):
        mine = pl.ds(pl.multiple_of(tile * TILE, TILE), TILE)
        here = info[mine, :]
        moved[...] = uv[mine, :]
        penalties = pens[mine, :]
        hot = jnp.concatenate(
            [jnp.where(here[:, t:t + 1] == label, 1.0, 0.0) for t in range(trans)], axis=0
        ).astype(jnp.bfloat16)
        phase[...] = jnp.dot(hot, table_ref[...], preferred_element_type=jnp.float32)
        scores = jnp.zeros((trans * TILE, ori), jnp.float32)
        onward = 2 * LANES * (steps // STRIDE)
        for group in range(steps // STRIDE):
            for t in range(trans):
                rows = slice(t * TILE, (t + 1) * TILE)
                cosine = phase[rows, 2 * LANES * group:2 * LANES * group + LANES]
                sine = phase[rows, 2 * LANES * group + LANES:2 * LANES * (group + 1)]
                turn_c = phase[rows, onward:onward + LANES]
                turn_s = phase[rows, onward + LANES:onward + 2 * LANES]
                for step in range(STRIDE):
                    at = (group * STRIDE + step) * LANES
                    real = moved[:, at:at + LANES]
                    imag = moved[:, pixels + at:pixels + at + LANES]
                    shifted[rows, at:at + LANES] = (real * cosine + imag * sine).astype(jnp.bfloat16)
                    shifted[rows, pixels + at:pixels + at + LANES] = (
                        imag * cosine - real * sine).astype(jnp.bfloat16)
                    if step < STRIDE - 1:
                        cosine, sine = (cosine * turn_c - sine * turn_s,
                                        sine * turn_c + cosine * turn_s)
            width = STRIDE * LANES
            for at in (group * width, pixels + group * width):
                span = slice(at, at + width)
                scores += lax.dot_general(shifted[:, span], views(span), contract,
                                          preferred_element_type=jnp.float32)
        full = scores.reshape(trans, TILE, ori) + penalties[None]
        highest = jnp.max(jnp.max(full, axis=0), axis=1, keepdims=True)
        total = jnp.zeros((TILE, ori), jnp.float32)
        moment_x = jnp.zeros((TILE, ori), jnp.float32)
        moment_y = jnp.zeros((TILE, ori), jnp.float32)
        for t in range(trans):
            term = jnp.exp(full[t] - highest)
            total += term
            moment_x += term * here[:, trans + 1 + t:trans + 2 + t]
            moment_y += term * here[:, 2 * trans + 1 + t:2 * trans + 2 + t]
        total = jnp.sum(total, axis=1, keepdims=True)
        moment_x = jnp.sum(moment_x, axis=1, keepdims=True)
        moment_y = jnp.sum(moment_y, axis=1, keepdims=True)
        stats[mine, :] = jnp.where(
            lanes == 0, highest,
            jnp.where(lanes == 1, total, jnp.where(lanes == 2, moment_x,
                                                   jnp.where(lanes == 3, moment_y, 0.0))))

    back = sum(
        lax.dot_general(part, pick, (((0,), (0,)), ((), ())), preferred_element_type=jnp.float32)
        for part in three(stats[...])
    )
    out_ref[0] = back[:8, :]


def class_stats(tiles, rank, meta, label, table, wtab, dtab, x_parts, q_parts, trans, slots):
    rows_all = rank.shape[1]
    rows_q, width = q_parts[0][0].shape[1:]
    ori = rows_q * len(q_parts)
    arrays = [array for array, _ in q_parts]
    spots = [spot for _, spot in q_parts]
    vmem = pl.BlockSpec(memory_space=pltpu.VMEM)
    return pl.pallas_call(
        functools.partial(stats_kernel, trans, spots, len(x_parts)),
        out_shape=jax.ShapeDtypeStruct((1, 8, rows_all), jnp.float32),
        in_specs=[pl.BlockSpec(memory_space=pltpu.SMEM)] + [vmem] * (6 + len(x_parts) + len(arrays)),
        out_specs=vmem,
        scratch_shapes=[
            pltpu.VMEM((slots, width), jnp.float32),
            pltpu.VMEM((slots, ori), jnp.float32),
            pltpu.VMEM((slots, 128), jnp.float32),
            pltpu.VMEM((slots, 128), jnp.float32),
            pltpu.VMEM((trans * TILE, table.shape[1]), jnp.float32),
            pltpu.VMEM((trans * TILE, width), jnp.bfloat16),
            pltpu.VMEM((TILE, width), jnp.float32),
        ],
        compiler_params=pltpu.CompilerParams(vmem_limit_bytes=36 * 1024 * 1024),
        cost_estimate=pl.CostEstimate(
            flops=20 * slots * trans * width * (ori + 256),
            bytes_accessed=(rows_all + ori) * width * 2,
            transcendentals=0,
        ),
    )(tiles, rank, meta, label, table, wtab, dtab, *x_parts, *arrays)


def on_device(particles, candidates, ctf_ids, offsets, ctf_table, sigma_sq, projections):
    pose_count = lax.axis_size("pose")
    dom_count = lax.axis_size("dom")
    pose = lax.axis_index("pose")
    local = projections.shape[0]
    class_total = local * pose_count
    rows, picks = candidates.shape
    trans = offsets.shape[2]
    pixels = sigma_sq.shape[0]
    capacity = 3 * rows * picks // class_total
    share = min(SHARE, pose_count)
    share_bits = [1 << b for b in range(share.bit_length() - 1)]
    families = pose_count // share
    slots = -(-min(share * capacity, share * rows) // TILE) * TILE

    dom_bits = [1 << b for b in range(dom_count.bit_length() - 1)][::-1]

    offset_f = offsets.astype(jnp.float32)
    combo = (offset_f[:, 0] + REACH) * (2 * REACH + 1) + (offset_f[:, 1] + REACH)
    meta = jnp.concatenate(
        [combo, ctf_ids[:, None].astype(jnp.float32), offset_f[:, 0], offset_f[:, 1],
         candidates.astype(jnp.float32)], axis=1)
    meta = jnp.pad(meta, ((0, 0), (0, 128 - meta.shape[1]))).astype(jnp.bfloat16)

    order = [0]
    for bit in share_bits[::-1]:
        order = order + [member ^ bit for member in order]
    single = {bit: swap(particles, "pose", bit) for bit in share_bits[::-1]}
    own_pieces = [projections] + [swap(projections, "dom", bit) for bit in dom_bits[:1]]
    metas = [swap(meta, "pose", member) if member else meta for member in order]
    chunks = [projections[spot:spot + 1] for spot in range(local)]
    meta_all = jnp.concatenate(metas, axis=0)

    named = meta_all[:, 3 * trans + 1:3 * trans + 1 + picks].astype(jnp.int32)
    owner = pose ^ (jnp.arange(families, dtype=jnp.int32) * share)
    class_ids = (owner[:, None] * local + jnp.arange(local, dtype=jnp.int32)[None, :]).reshape(-1)
    names = jnp.any(named.T[None, :, :] == class_ids[:, None, None], axis=1).astype(jnp.int32)
    ahead = jnp.cumsum(names, axis=1)
    rank = jnp.where(names > 0, ahead - 1, -1)
    tiles = (ahead[:, -1] + (TILE - 1)) // TILE

    single, own_pieces, chunks, rank, tiles = lax.optimization_barrier(
        (single, own_pieces, chunks, rank, tiles))

    x_parts = []
    for member in order:
        bits = [bit for bit in share_bits if member & bit]
        part = single[bits[-1]] if bits else particles
        for bit in bits[:-1]:
            part = swap(part, "pose", bit)
        x_parts.append(part)

    def over_dom(members, bits):
        for bit in bits:
            members = members + [swap(member, "dom", bit) for member in members]
        return members

    far = [[swap(chunks[spot], "pose", family * share) for spot in range(local)]
           for family in range(1, families)]
    own_pieces = over_dom(own_pieces, dom_bits[1:])
    weight = ctf_table / sigma_sq[None, :]
    wtab = jnp.concatenate(split_three(weight), axis=0)
    dtab = jnp.concatenate(split_three(weight * ctf_table), axis=0)

    table, label = phase_table(pixels)
    table, label = jnp.asarray(table), jnp.asarray(label)
    results = []

    def one_class(index, members):
        turn = tiles[index:index + 1]
        if results:
            turn, results[-1] = lax.optimization_barrier((turn, results[-1]))
        results.append(class_stats(turn, rank[index:index + 1], meta_all, label, table, wtab, dtab,
                                   x_parts, members, trans, slots))

    for spot in range(local):
        one_class(spot, [(piece, spot) for piece in own_pieces])
    for family in range(1, families):
        for spot in range(local):
            pieces = [far[family - 1][spot]]
            for hop, bit in enumerate(dom_bits):
                if spot:
                    tie = -1 if hop else spot
                    pieces[hop:], results[tie] = lax.optimization_barrier((pieces[hop:], results[tie]))
                pieces = pieces + [swap(member, "dom", bit) for member in pieces]
            one_class(family * local + spot, [(member, 0) for member in pieces])
    stats = jnp.concatenate(results, axis=0)[:, :4, :]
    own = []
    for place, member in enumerate(order):
        block = stats[:, :, place * rows:(place + 1) * rows]
        block = swap(block, "pose", member) if member else block
        own += [(member, spot, block[spot]) for spot in range(families * local)]

    cand = candidates.T
    owner = cand // local
    beyond = (owner ^ pose) // share
    within = (owner ^ pose) % share
    position = beyond * local + cand % local
    picked = jnp.zeros((picks, 4, rows), jnp.float32)
    for member, spot, block in own:
        hit = (within == member) & (position == spot)
        picked = jnp.where(hit[:, None, :], block[None], picked)
    log_weight = picked[:, 0] + jnp.log(picked[:, 1])
    raw_weight = jnp.exp(log_weight - jnp.max(log_weight, axis=0, keepdims=True))
    class_prob = raw_weight / jnp.sum(raw_weight, axis=0, keepdims=True)
    mean_x = jnp.sum(class_prob * picked[:, 2] / picked[:, 1], axis=0)
    mean_y = jnp.sum(class_prob * picked[:, 3] / picked[:, 1], axis=0)
    return (class_prob.T, jnp.stack([mean_x, mean_y], axis=1))


def solution(mesh):
    in_specs = (
        P(("pose", "dom"), None),
        P(("pose", "dom"), None),
        P(("pose", "dom")),
        P(("pose", "dom"), None, None),
        P(),
        P(),
        P("pose", "dom", None),
    )
    out_specs = (P(("pose", "dom"), None), P(("pose", "dom"), None))
    return jax.shard_map(
        on_device, mesh=mesh, in_specs=in_specs, out_specs=out_specs, check_vma=False
    )
```

time: 151 us -> 147 us (0.974); the launches traced: 154 us -> 146 us
  waiting for transfers between devices: 74 us -> 58.1 us
  starting transfers between devices: 17.2 us -> 23 us
  Pallas kernels: 46.6 us -> 50.2 us
    ppermute x18 -> x20, waiting for transfers between devices: 74 us -> 58.1 us  [swap(): lax.ppermute(values, axis, [(index, index ^ bit) for index in range(count)])]
    ppermute x18 -> x20, starting transfers between devices: 17.2 us -> 23 us  [swap(): lax.ppermute(values, axis, [(index, index ^ bit) for index in range(count)])]
    pallas_call x2 -> x4, Pallas kernels: 46.6 us -> 50.2 us  [class_stats(): pl.pallas_call(functools.partial(stats_kernel, trans, spots, len(x_parts)...]
    and x3, other arithmetic: 0.05 us -> 1.74 us  [on_device(): hit = (within == member) & (position == spot)]
    slice x5 -> x4, local copies, waits for them, and re-layouts: 1.98 us -> 3.26 us  [the longest x1 2.38 us: on_device(): chunks = [projections[spot:spot + 1] for spot in range(local)]]
  transfers between devices with their start and end apart: 18 -> 20, of which waited for: 9 -> 9; matrix products, arithmetic and copies ran while one was open for 7% -> 6% of each run, Pallas kernels for 15% -> 22%
where the time goes in v2:
time: 147 us; the launch traced here: 146 us
  waiting for transfers between devices  58.1 us (40%)
  Pallas kernels  50.2 us (34%)
  starting transfers between devices  23 us (16%)
  other arithmetic  7.49 us (5%)
  local copies, waits for them, and re-layouts  6.56 us (4%)
    ppermute x20, waiting for transfers between devices, swap(): lax.ppermute(values, axis, [(index, index ^ bit) for index in range(count)])  58.1 us
    pallas_call x4, Pallas kernels, class_stats(): pl.pallas_call(functools.partial(stats_kernel, trans, spots, len(x_parts)...  50.2 us
    ppermute x20, starting transfers between devices, swap(): lax.ppermute(values, axis, [(index, index ^ bit) for index in range(count)])  23 us
  transfers between devices with their start and end apart: 20, of which 9 were waited for; matrix products, arithmetic and copies ran while one was open for 6% of the time, Pallas kernels for 22%

profile of v2, /device:TPU:0, one launch (start us, length us, event | category | flops | bytes accessed | tf_op | source)
XLA Modules:
  0.0 146.4 jit_solution(2817894318667792050)
XLA Ops:
  0.6 0.7 copy_convert_fusion
  1.4 0.6 copy-done.23
  2.0 0.7 copy-done.22
  2.7 0.3 concatenate.16
  3.0 0.1 copy.25
  3.1 3.1 %collective-permute-start.3 = (bf16[128,128]{1,0:T(8,128)(2,1)S(1)}, bf16[128,128]{1,0:T(8,128)(2,1)S(1)}, u32[]{:S(2)}, u32[]{:S(2)}) collective-permute-start(bf16[128,128]{1,0:T(8,128)(2,1)S(1)} %pad.5), channel_id=1, source_target_pairs={{0,8},{4,12},{8,0},{12,4},{16,24},{20,28},{24,16},{28,20},{1,9},{5... | collective-permute-start | bytes 98312 | tf_op jit(solution)/shard_map/ppermute | solution.py:58
  6.2 1.5 %collective-permute-start.4 = (bf16[128,128]{1,0:T(8,128)(2,1)S(1)}, bf16[128,128]{1,0:T(8,128)(2,1)S(1)}, u32[]{:S(2)}, u32[]{:S(2)}) collective-permute-start(bf16[128,128]{1,0:T(8,128)(2,1)S(1)} %pad.5), channel_id=1, source_target_pairs={{0,4},{4,0},{8,12},{12,8},{16,20},{20,16},{24,28},{28,24},{1,5},{5... | collective-permute-start | bytes 98312 | tf_op jit(solution)/shard_map/ppermute | solution.py:58
  7.8 1.9 %collective-permute-start = (bf16[128,4096]{1,0:T(8,128)(2,1)}, bf16[128,4096]{1,0:T(8,128)(2,1)S(1)}, u32[]{:S(2)}, u32[]{:S(2)}) collective-permute-start(bf16[128,4096]{1,0:T(8,128)(2,1)} %refs_0_.7), channel_id=1, source_target_pairs={{0,4},{4,0},{8,12},{12,8},{16,20},{20,16},{24,28},{28,24},{1,5},{5... | collective-permute-start | bytes 3145736 | tf_op jit(solution)/shard_map/ppermute | solution.py:58
  9.7 1.6 %collective-permute-start.1 = (bf16[128,4096]{1,0:T(8,128)(2,1)}, bf16[128,4096]{1,0:T(8,128)(2,1)}, u32[]{:S(2)}, u32[]{:S(2)}) collective-permute-start(bf16[128,4096]{1,0:T(8,128)(2,1)} %refs_0_.7), channel_id=1, source_target_pairs={{0,8},{4,12},{8,0},{12,4},{16,24},{20,28},{24,16},{28,20},{1,9},{5... | collective-permute-start | bytes 3145736 | tf_op jit(solution)/shard_map/ppermute | solution.py:58
  11.3 2.4 %fusion.30 = (bf16[1,64,4096]{2,1,0:T(8,128)(2,1)}, bf16[1,64,4096]{2,1,0:T(8,128)(2,1)}) fusion(bf16[2,64,4096]{2,1,0:T(8,128)(2,1)} %refs_4_.1), kind=kLoop, calls=%fused_computation.109 | loop fusion | bytes 2097152 | tf_op jit(solution)/shard_map/slice | solution.py:230
  13.7 0.8 reduce-precision_convert_fusion.1
  14.6 1.5 %collective-permute-start.2 = (bf16[2,64,4096]{2,1,0:T(8,128)(2,1)S(1)}, bf16[2,64,4096]{2,1,0:T(8,128)(2,1)}, u32[]{:S(2)}, u32[]{:S(2)}) collective-permute-start(bf16[2,64,4096]{2,1,0:T(8,128)(2,1)S(1)} %copy-done), channel_id=1, source_target_pairs={{0,2},{1,3},{2,0},{3,1},{4,6},{5,7},{6,4},{7,5},{8,10},{9,11},{10,... | collective-permute-start | bytes 3145736 | tf_op jit(solution)/shard_map/ppermute | solution.py:58
  16.5 1.2 reduce-window.6
  17.7 0.2 slice_reduce_fusion
  17.9 0.2 reduce-window.9
  18.2 0.2 fusion.7
  18.4 14.9 %collective-permute-done.refs_2_ = bf16[128,4096]{1,0:T(8,128)(2,1)S(1)} collective-permute-done((bf16[128,4096]{1,0:T(8,128)(2,1)}, bf16[128,4096]{1,0:T(8,128)(2,1)S(1)}, u32[]{:S(2)}, u32[]{:S(2)}) %collective-permute-start) | collective-permute-done | bytes 1048608 | tf_op jit(solution)/shard_map/ppermute | solution.py:58
  33.3 0.8 collective-permute-done.1.refs_1_
  34.1 4.1 %collective-permute-done.2.refs_5_ = bf16[2,64,4096]{2,1,0:T(8,128)(2,1)} collective-permute-done((bf16[2,64,4096]{2,1,0:T(8,128)(2,1)S(1)}, bf16[2,64,4096]{2,1,0:T(8,128)(2,1)}, u32[]{:S(2)}, u32[]{:S(2)}) %collective-permute-start.2) | collective-permute-done | bytes 1048608 | tf_op jit(solution)/shard_map/ppermute | solution.py:58
  38.2 0.5 collective-permute-start.6
  38.7 0.5 collective-permute-start.8
  39.2 0.5 fusion.22
  39.8 0.6 fusion.24
  40.4 1.0 pad_maximum_fusion
  41.4 2.7 %collective-permute-start.11 = (bf16[1,64,4096]{2,1,0:T(8,128)(2,1)}, bf16[1,64,4096]{2,1,0:T(8,128)(2,1)}, u32[]{:S(2)}, u32[]{:S(2)}) collective-permute-start(bf16[1,64,4096]{2,1,0:T(8,128)(2,1)} %get-tuple-element.33), channel_id=1, source_target_pairs={{0,16},{4,20},{8,24},{12,28},{16,0},{20,4},{24,8},{28,12},{1,17},{... | collective-permute-start | bytes 1572872 | tf_op jit(solution)/shard_map/ppermute | solution.py:58
  44.1 0.6 fusion.33
  44.7 0.3 collective-permute-start.9
  45.0 0.7 fusion.32
  45.7 33.2 %collective-permute-done.11.refs_4_ = bf16[1,64,4096]{2,1,0:T(8,128)(2,1)} collective-permute-done((bf16[1,64,4096]{2,1,0:T(8,128)(2,1)}, bf16[1,64,4096]{2,1,0:T(8,128)(2,1)}, u32[]{:S(2)}, u32[]{:S(2)}) %collective-permute-start.11) | collective-permute-done | bytes 524320 | tf_op jit(solution)/shard_map/ppermute | solution.py:58
  78.9 1.5 %collective-permute-start.12 = (bf16[1,64,4096]{2,1,0:T(8,128)(2,1)}, bf16[1,64,4096]{2,1,0:T(8,128)(2,1)S(1)}, u32[]{:S(2)}, u32[]{:S(2)}) collective-permute-start(bf16[1,64,4096]{2,1,0:T(8,128)(2,1)} %collective-permute-done.11.refs_4_), channel_id=1, source_target_pairs={{0,2},{1,3},{2,0},{3,1},{4,6},{5,7},{6,4},{7,5},{8,10},{9,11},{10,... | collective-permute-start | bytes 1572872 | tf_op jit(solution)/shard_map/ppermute | solution.py:58
  80.5 0.7 copy-done.3
  81.2 11.4 %shard_map.104 = f32[1,8,512]{2,1,0:T(8,128)S(1)} custom-call(s32[1]{0:T(128)} %get-tuple-element.99.tiles_ref, s32[1,512]{1,0:T(1,128)S(1)} %get-tuple-element.88.rank_ref, bf16[512,128]{1,0:T(8,128)(2,1)S(1)} %pad_maximum_fusion.2.meta_ref, f32[1,256]{1,0:T(1,128)S(1)} %copy-done.3, bf16[256,1280]{1,0:T(8,128)(2,1)S(1)} %copy-done.2, ...), custom_call_target="tpu_custom_call" | custom-call | flops 72477573120 | bytes 6291456 | tf_op jit(solution)/shard_map/pallas_call | solution.py:177
  92.5 0.4 collective-permute-done.12.refs_5_
  92.9 0.2 collective-permute-start.14
  93.1 11.4 %shard_map.105 = f32[1,8,512]{2,1,0:T(8,128)S(1)} custom-call(s32[1]{0:T(128)} %get-tuple-element.28.tiles_ref, s32[1,512]{1,0:T(1,128)S(1)} %get-tuple-element.87.rank_ref, bf16[512,128]{1,0:T(8,128)(2,1)S(1)} %pad_maximum_fusion.2.meta_ref, f32[1,256]{1,0:T(1,128)S(1)} %copy-done.3, bf16[256,1280]{1,0:T(8,128)(2,1)S(1)} %copy-done.2, ...), custom_call_target="tpu_custom_call" | custom-call | flops 72477573120 | bytes 6291456 | tf_op jit(solution)/shard_map/pallas_call | solution.py:177
  104.5 1.4 collective-permute-start.10
  105.9 1.3 collective-permute-start.15
  107.2 9.3 %shard_map.106 = f32[1,8,512]{2,1,0:T(8,128)S(1)} custom-call(s32[1]{0:T(128)} %get-tuple-element.32.tiles_ref, s32[1,512]{1,0:T(1,128)S(1)} %get-tuple-element.86.rank_ref, bf16[512,128]{1,0:T(8,128)(2,1)S(1)} %pad_maximum_fusion.2.meta_ref, f32[1,256]{1,0:T(1,128)S(1)} %copy-done.3, bf16[256,1280]{1,0:T(8,128)(2,1)S(1)} %copy-done.2, ...), custom_call_target="tpu_custom_call" | custom-call | flops 72477573120 | bytes 6291456 | tf_op jit(solution)/shard_map/pallas_call | solution.py:177
  116.5 1.5 %collective-permute-done.10.refs_5_ = bf16[1,64,4096]{2,1,0:T(8,128)(2,1)S(1)} collective-permute-done((bf16[1,64,4096]{2,1,0:T(8,128)(2,1)}, bf16[1,64,4096]{2,1,0:T(8,128)(2,1)S(1)}, u32[]{:S(2)}, u32[]{:S(2)}) %collective-permute-start.10) | collective-permute-done | bytes 524320 | tf_op jit(solution)/shard_map/ppermute | solution.py:58
  118.1 1.3 collective-permute-start.16
  119.4 1.5 %collective-permute-done.16.refs_7_ = bf16[1,64,4096]{2,1,0:T(8,128)(2,1)S(1)} collective-permute-done((bf16[1,64,4096]{2,1,0:T(8,128)(2,1)S(1)}, bf16[1,64,4096]{2,1,0:T(8,128)(2,1)S(1)}, u32[]{:S(2)}, u32[]{:S(2)}) %collective-permute-start.16) | collective-permute-done | bytes 524320 | tf_op jit(solution)/shard_map/ppermute | solution.py:58
  121.0 18.2 %shard_map.107 = f32[1,8,512]{2,1,0:T(8,128)S(1)} custom-call(s32[1]{0:T(128)} %get-tuple-element.36.tiles_ref, s32[1,512]{1,0:T(1,128)S(1)} %get-tuple-element.85.rank_ref, bf16[512,128]{1,0:T(8,128)(2,1)S(1)} %pad_maximum_fusion.2.meta_ref, f32[1,256]{1,0:T(1,128)S(1)} %copy-done.3, bf16[256,1280]{1,0:T(8,128)(2,1)S(1)} %copy-done.2, ...), custom_call_target="tpu_custom_call" | custom-call | flops 72477573120 | bytes 6291456 | tf_op jit(solution)/shard_map/pallas_call | solution.py:177
  139.4 3.4 %collective-permute-start.19 = (f32[4,4,128]{2,1,0:T(4,128)S(1)}, f32[4,4,128]{2,1,0:T(4,128)S(1)}, u32[]{:S(2)}, u32[]{:S(2)}) collective-permute-start(f32[4,4,128]{2,1,0:T(4,128)S(1)} %get-tuple-element.70), channel_id=1, source_target_pairs={{0,8},{4,12},{8,0},{12,4},{16,24},{20,28},{24,16},{28,20},{1,9},{5... | collective-permute-start | bytes 24584 | tf_op jit(solution)/shard_map/ppermute | solution.py:58
  142.8 1.1 collective-permute-done.17
  143.9 0.6 collective-permute-done.19
  144.6 0.5 copy-done.6
  145.2 0.6 fusion.15
  145.8 0.6 pad_maximum_fusion.8
  (90 shorter events, 1.1 us)
Async XLA Ops:
  1.3 0.7 copy-start.23
  2.0 0.7 copy-start.22
  3.1 11.5 %collective-permute-start.3 = (bf16[128,128]{1,0:T(8,128)(2,1)S(1)}, bf16[128,128]{1,0:T(8,128)(2,1)S(1)}, u32[]{:S(2)}, u32[]{:S(2)}) collective-permute-start(bf16[128,128]{1,0:T(8,128)(2,1)S(1)} %pad.5), channel_id=1, source_target_pairs={{0,8},{4,12},{8,0},{12,4},{16,24},{20,28},{24,16},{28,20},{1,9},{5... | collective-permute-start | bytes 98312 | tf_op jit(solution)/shard_map/ppermute | solution.py:58
  6.2 9.9 %collective-permute-start.4 = (bf16[128,128]{1,0:T(8,128)(2,1)S(1)}, bf16[128,128]{1,0:T(8,128)(2,1)S(1)}, u32[]{:S(2)}, u32[]{:S(2)}) collective-permute-start(bf16[128,128]{1,0:T(8,128)(2,1)S(1)} %pad.5), channel_id=1, source_target_pairs={{0,4},{4,0},{8,12},{12,8},{16,20},{20,16},{24,28},{28,24},{1,5},{5... | collective-permute-start | bytes 98312 | tf_op jit(solution)/shard_map/ppermute | solution.py:58
  7.8 8.4 %collective-permute-start.5 = (bf16[128,128]{1,0:T(8,128)(2,1)S(1)}, bf16[128,128]{1,0:T(8,128)(2,1)S(1)}, u32[]{:S(2)}, u32[]{:S(2)}) collective-permute-start(bf16[128,128]{1,0:T(8,128)(2,1)S(1)} %pad.5), channel_id=1, source_target_pairs={{0,12},{4,8},{8,4},{12,0},{16,28},{20,24},{24,20},{28,16},{1,13},{... | collective-permute-start | bytes 98312 | tf_op jit(solution)/shard_map/ppermute | solution.py:58
  7.8 25.5 %collective-permute-start = (bf16[128,4096]{1,0:T(8,128)(2,1)}, bf16[128,4096]{1,0:T(8,128)(2,1)S(1)}, u32[]{:S(2)}, u32[]{:S(2)}) collective-permute-start(bf16[128,4096]{1,0:T(8,128)(2,1)} %refs_0_.7), channel_id=1, source_target_pairs={{0,4},{4,0},{8,12},{12,8},{16,20},{20,16},{24,28},{28,24},{1,5},{5... | collective-permute-start | bytes 3145736 | tf_op jit(solution)/shard_map/ppermute | solution.py:58
  9.7 24.4 %collective-permute-start.1 = (bf16[128,4096]{1,0:T(8,128)(2,1)}, bf16[128,4096]{1,0:T(8,128)(2,1)}, u32[]{:S(2)}, u32[]{:S(2)}) collective-permute-start(bf16[128,4096]{1,0:T(8,128)(2,1)} %refs_0_.7), channel_id=1, source_target_pairs={{0,8},{4,12},{8,0},{12,4},{16,24},{20,28},{24,16},{28,20},{1,9},{5... | collective-permute-start | bytes 3145736 | tf_op jit(solution)/shard_map/ppermute | solution.py:58
  11.3 2.4 %copy-start.4 = (f32[16,2048]{1,0:T(8,128)S(1)}, f32[16,2048]{1,0:T(8,128)}, u32[]{:S(2)}) copy-start(f32[16,2048]{1,0:T(8,128)} %param.13) | copy-start | bytes 393220
  11.3 2.4 %copy-start.5 = (f32[2048]{0:T(1024)S(1)}, f32[2048]{0:T(1024)}, u32[]{:S(2)}) copy-start(f32[2048]{0:T(1024)} %param.14) | copy-start | bytes 24580
  11.3 3.4 %copy-start = (bf16[2,64,4096]{2,1,0:T(8,128)(2,1)S(1)}, bf16[2,64,4096]{2,1,0:T(8,128)(2,1)}, u32[]{:S(2)}) copy-start(bf16[2,64,4096]{2,1,0:T(8,128)(2,1)} %refs_4_.1) | copy-start | bytes 3145732
  14.4 66.0 %copy-start.1 = (bf16[128,4096]{1,0:T(8,128)(2,1)S(1)}, bf16[128,4096]{1,0:T(8,128)(2,1)}, u32[]{:S(2)}) copy-start(bf16[128,4096]{1,0:T(8,128)(2,1)} %refs_0_.7) | copy-start | bytes 3145732
  14.6 23.6 %collective-permute-start.2 = (bf16[2,64,4096]{2,1,0:T(8,128)(2,1)S(1)}, bf16[2,64,4096]{2,1,0:T(8,128)(2,1)}, u32[]{:S(2)}, u32[]{:S(2)}) collective-permute-start(bf16[2,64,4096]{2,1,0:T(8,128)(2,1)S(1)} %copy-done), channel_id=1, source_target_pairs={{0,2},{1,3},{2,0},{3,1},{4,6},{5,7},{6,4},{7,5},{8,10},{9,11},{10,... | collective-permute-start | bytes 3145736 | tf_op jit(solution)/shard_map/ppermute | solution.py:58
  18.1 62.4 %copy-start.2 = (bf16[256,1280]{1,0:T(8,128)(2,1)S(1)}, bf16[256,1280]{1,0:T(8,128)(2,1)}, u32[]{:S(2)}) copy-start(bf16[256,1280]{1,0:T(8,128)(2,1)} %constant.97.clone.table_ref) | copy-start | bytes 1966084
  38.2 42.2 %collective-permute-start.6 = (bf16[128,4096]{1,0:T(8,128)(2,1)}, bf16[128,4096]{1,0:T(8,128)(2,1)S(1)}, u32[]{:S(2)}, u32[]{:S(2)}) collective-permute-start(bf16[128,4096]{1,0:T(8,128)(2,1)} %collective-permute-done.1.refs_1_), channel_id=1, source_target_pairs={{0,4},{4,0},{8,12},{12,8},{16,20},{20,16},{24,28},{28,24},{1,5},{5... | collective-permute-start | bytes 3145736 | tf_op jit(solution)/shard_map/ppermute | solution.py:58
  38.7 41.7 %collective-permute-start.7 = (bf16[2,64,4096]{2,1,0:T(8,128)(2,1)S(1)}, bf16[2,64,4096]{2,1,0:T(8,128)(2,1)S(1)}, u32[]{:S(2)}, u32[]{:S(2)}) collective-permute-start(bf16[2,64,4096]{2,1,0:T(8,128)(2,1)S(1)} %copy-done), channel_id=1, source_target_pairs={{0,1},{1,0},{2,3},{3,2},{4,5},{5,4},{6,7},{7,6},{8,9},{9,8},{10,11... | collective-permute-start | bytes 3145736 | tf_op jit(solution)/shard_map/ppermute | solution.py:58
  38.7 41.7 %collective-permute-start.8 = (bf16[2,64,4096]{2,1,0:T(8,128)(2,1)}, bf16[2,64,4096]{2,1,0:T(8,128)(2,1)S(1)}, u32[]{:S(2)}, u32[]{:S(2)}) collective-permute-start(bf16[2,64,4096]{2,1,0:T(8,128)(2,1)} %collective-permute-done.2.refs_5_), channel_id=1, source_target_pairs={{0,1},{1,0},{2,3},{3,2},{4,5},{5,4},{6,7},{7,6},{8,9},{9,8},{10,11... | collective-permute-start | bytes 3145736 | tf_op jit(solution)/shard_map/ppermute | solution.py:58
  41.4 37.5 %collective-permute-start.11 = (bf16[1,64,4096]{2,1,0:T(8,128)(2,1)}, bf16[1,64,4096]{2,1,0:T(8,128)(2,1)}, u32[]{:S(2)}, u32[]{:S(2)}) collective-permute-start(bf16[1,64,4096]{2,1,0:T(8,128)(2,1)} %get-tuple-element.33), channel_id=1, source_target_pairs={{0,16},{4,20},{8,24},{12,28},{16,0},{20,4},{24,8},{28,12},{1,17},{... | collective-permute-start | bytes 1572872 | tf_op jit(solution)/shard_map/ppermute | solution.py:58
  44.7 59.8 %collective-permute-start.9 = (bf16[1,64,4096]{2,1,0:T(8,128)(2,1)}, bf16[1,64,4096]{2,1,0:T(8,128)(2,1)}, u32[]{:S(2)}, u32[]{:S(2)}) collective-permute-start(bf16[1,64,4096]{2,1,0:T(8,128)(2,1)} %get-tuple-element.27), channel_id=1, source_target_pairs={{0,16},{4,20},{8,24},{12,28},{16,0},{20,4},{24,8},{28,12},{1,17},{... | collective-permute-start | bytes 1572872 | tf_op jit(solution)/shard_map/ppermute | solution.py:58
  78.9 14.0 %collective-permute-start.12 = (bf16[1,64,4096]{2,1,0:T(8,128)(2,1)}, bf16[1,64,4096]{2,1,0:T(8,128)(2,1)S(1)}, u32[]{:S(2)}, u32[]{:S(2)}) collective-permute-start(bf16[1,64,4096]{2,1,0:T(8,128)(2,1)} %collective-permute-done.11.refs_4_), channel_id=1, source_target_pairs={{0,2},{1,3},{2,0},{3,1},{4,6},{5,7},{6,4},{7,5},{8,10},{9,11},{10,... | collective-permute-start | bytes 1572872 | tf_op jit(solution)/shard_map/ppermute | solution.py:58
  80.5 26.8 %collective-permute-start.13 = (bf16[1,64,4096]{2,1,0:T(8,128)(2,1)}, bf16[1,64,4096]{2,1,0:T(8,128)(2,1)}, u32[]{:S(2)}, u32[]{:S(2)}) collective-permute-start(bf16[1,64,4096]{2,1,0:T(8,128)(2,1)} %collective-permute-done.11.refs_4_), channel_id=1, source_target_pairs={{0,1},{1,0},{2,3},{3,2},{4,5},{5,4},{6,7},{7,6},{8,9},{9,8},{10,11... | collective-permute-start | bytes 1572872 | tf_op jit(solution)/shard_map/ppermute | solution.py:58
  80.5 0.7 copy-start.3
  92.9 14.4 %collective-permute-start.14 = (bf16[1,64,4096]{2,1,0:T(8,128)(2,1)S(1)}, bf16[1,64,4096]{2,1,0:T(8,128)(2,1)S(1)}, u32[]{:S(2)}, u32[]{:S(2)}) collective-permute-start(bf16[1,64,4096]{2,1,0:T(8,128)(2,1)S(1)} %collective-permute-done.12.refs_5_), channel_id=1, source_target_pairs={{0,1},{1,0},{2,3},{3,2},{4,5},{5,4},{6,7},{7,6},{8,9},{9,8},{10,11... | collective-permute-start | bytes 1572872 | tf_op jit(solution)/shard_map/ppermute | solution.py:58
  104.5 13.6 %collective-permute-start.10 = (bf16[1,64,4096]{2,1,0:T(8,128)(2,1)}, bf16[1,64,4096]{2,1,0:T(8,128)(2,1)S(1)}, u32[]{:S(2)}, u32[]{:S(2)}) collective-permute-start(bf16[1,64,4096]{2,1,0:T(8,128)(2,1)} %collective-permute-done.9.refs_4_), channel_id=1, source_target_pairs={{0,2},{1,3},{2,0},{3,1},{4,6},{5,7},{6,4},{7,5},{8,10},{9,11},{10,... | collective-permute-start | bytes 1572872 | tf_op jit(solution)/shard_map/ppermute | solution.py:58
  105.9 13.5 %collective-permute-start.15 = (bf16[1,64,4096]{2,1,0:T(8,128)(2,1)}, bf16[1,64,4096]{2,1,0:T(8,128)(2,1)S(1)}, u32[]{:S(2)}, u32[]{:S(2)}) collective-permute-start(bf16[1,64,4096]{2,1,0:T(8,128)(2,1)} %collective-permute-done.9.refs_4_), channel_id=1, source_target_pairs={{0,1},{1,0},{2,3},{3,2},{4,5},{5,4},{6,7},{7,6},{8,9},{9,8},{10,11... | collective-permute-start | bytes 1572872 | tf_op jit(solution)/shard_map/ppermute | solution.py:58
  118.1 2.9 %collective-permute-start.16 = (bf16[1,64,4096]{2,1,0:T(8,128)(2,1)S(1)}, bf16[1,64,4096]{2,1,0:T(8,128)(2,1)S(1)}, u32[]{:S(2)}, u32[]{:S(2)}) collective-permute-start(bf16[1,64,4096]{2,1,0:T(8,128)(2,1)S(1)} %collective-permute-done.10.refs_5_), channel_id=1, source_target_pairs={{0,1},{1,0},{2,3},{3,2},{4,5},{5,4},{6,7},{7,6},{8,9},{9,8},{10,11... | collective-permute-start | bytes 1572872 | tf_op jit(solution)/shard_map/ppermute | solution.py:58
  120.9 23.5 %copy-start.9 = (pred[2,128]{1,0:T(4,128)(4,1)S(1)}, pred[2,128]{1,0:T(4,128)(4,1)}, u32[]{:S(2)}) copy-start(pred[2,128]{1,0:T(4,128)(4,1)} %get-tuple-element.95) | copy-start | bytes 772
  120.9 23.5 %copy-start.10 = (pred[2,128]{1,0:T(4,128)(4,1)S(1)}, pred[2,128]{1,0:T(4,128)(4,1)}, u32[]{:S(2)}) copy-start(pred[2,128]{1,0:T(4,128)(4,1)} %get-tuple-element.110) | copy-start | bytes 772
  120.9 23.5 %copy-start.11 = (pred[2,128]{1,0:T(4,128)(4,1)S(1)}, pred[2,128]{1,0:T(4,128)(4,1)}, u32[]{:S(2)}) copy-start(pred[2,128]{1,0:T(4,128)(4,1)} %get-tuple-element.112) | copy-start | bytes 772
  120.9 23.6 %copy-start.12 = (pred[2,128]{1,0:T(4,128)(4,1)S(1)}, pred[2,128]{1,0:T(4,128)(4,1)}, u32[]{:S(2)}) copy-start(pred[2,128]{1,0:T(4,128)(4,1)} %get-tuple-element.114) | copy-start | bytes 772
  120.9 23.6 %copy-start.13 = (pred[2,128]{1,0:T(4,128)(4,1)S(1)}, pred[2,128]{1,0:T(4,128)(4,1)}, u32[]{:S(2)}) copy-start(pred[2,128]{1,0:T(4,128)(4,1)} %get-tuple-element.101) | copy-start | bytes 772
  120.9 23.6 %copy-start.14 = (pred[2,128]{1,0:T(4,128)(4,1)S(1)}, pred[2,128]{1,0:T(4,128)(4,1)}, u32[]{:S(2)}) copy-start(pred[2,128]{1,0:T(4,128)(4,1)} %get-tuple-element.102) | copy-start | bytes 772
  121.0 23.6 %copy-start.15 = (pred[2,128]{1,0:T(4,128)(4,1)S(1)}, pred[2,128]{1,0:T(4,128)(4,1)}, u32[]{:S(2)}) copy-start(pred[2,128]{1,0:T(4,128)(4,1)} %get-tuple-element.103) | copy-start | bytes 772
  121.0 23.6 %copy-start.16 = (pred[2,128]{1,0:T(4,128)(4,1)S(1)}, pred[2,128]{1,0:T(4,128)(4,1)}, u32[]{:S(2)}) copy-start(pred[2,128]{1,0:T(4,128)(4,1)} %get-tuple-element.104) | copy-start | bytes 772
  121.0 23.6 %copy-start.17 = (pred[2,128]{1,0:T(4,128)(4,1)S(1)}, pred[2,128]{1,0:T(4,128)(4,1)}, u32[]{:S(2)}) copy-start(pred[2,128]{1,0:T(4,128)(4,1)} %get-tuple-element.105) | copy-start | bytes 772
  121.0 23.6 %copy-start.18 = (pred[2,128]{1,0:T(4,128)(4,1)S(1)}, pred[2,128]{1,0:T(4,128)(4,1)}, u32[]{:S(2)}) copy-start(pred[2,128]{1,0:T(4,128)(4,1)} %get-tuple-element.106) | copy-start | bytes 772
  121.0 23.6 %copy-start.19 = (pred[2,128]{1,0:T(4,128)(4,1)S(1)}, pred[2,128]{1,0:T(4,128)(4,1)}, u32[]{:S(2)}) copy-start(pred[2,128]{1,0:T(4,128)(4,1)} %get-tuple-element.107) | copy-start | bytes 772
  121.0 23.6 %copy-start.20 = (pred[2,128]{1,0:T(4,128)(4,1)S(1)}, pred[2,128]{1,0:T(4,128)(4,1)}, u32[]{:S(2)}) copy-start(pred[2,128]{1,0:T(4,128)(4,1)} %get-tuple-element.108) | copy-start | bytes 772
  121.0 23.6 %copy-start.21 = (pred[2,128]{1,0:T(4,128)(4,1)S(1)}, pred[2,128]{1,0:T(4,128)(4,1)}, u32[]{:S(2)}) copy-start(pred[2,128]{1,0:T(4,128)(4,1)} %get-tuple-element.109) | copy-start | bytes 772
  139.2 4.6 %collective-permute-start.17 = (f32[4,4,128]{2,1,0:T(4,128)S(1)}, f32[4,4,128]{2,1,0:T(4,128)S(1)}, u32[]{:S(2)}, u32[]{:S(2)}) collective-permute-start(f32[4,4,128]{2,1,0:T(4,128)S(1)} %get-tuple-element.68), channel_id=1, source_target_pairs={{0,12},{4,8},{8,4},{12,0},{16,28},{20,24},{24,20},{28,16},{1,13},{... | collective-permute-start | bytes 24584 | tf_op jit(solution)/shard_map/ppermute | solution.py:58
  139.3 4.6 %collective-permute-start.18 = (f32[4,4,128]{2,1,0:T(4,128)S(1)}, f32[4,4,128]{2,1,0:T(4,128)S(1)}, u32[]{:S(2)}, u32[]{:S(2)}) collective-permute-start(f32[4,4,128]{2,1,0:T(4,128)S(1)} %get-tuple-element.69), channel_id=1, source_target_pairs={{0,4},{4,0},{8,12},{12,8},{16,20},{20,16},{24,28},{28,24},{1,5},{5... | collective-permute-start | bytes 24584 | tf_op jit(solution)/shard_map/ppermute | solution.py:58
  139.4 5.0 %collective-permute-start.19 = (f32[4,4,128]{2,1,0:T(4,128)S(1)}, f32[4,4,128]{2,1,0:T(4,128)S(1)}, u32[]{:S(2)}, u32[]{:S(2)}) collective-permute-start(f32[4,4,128]{2,1,0:T(4,128)S(1)} %get-tuple-element.70), channel_id=1, source_target_pairs={{0,8},{4,12},{8,0},{12,4},{16,24},{20,28},{24,16},{28,20},{1,9},{5... | collective-permute-start | bytes 24584 | tf_op jit(solution)/shard_map/ppermute | solution.py:58
  144.5 0.7 copy-start.6
  144.5 0.7 copy-start.7
  144.5 0.7 copy-start.8

commit v3 on v2

v3 whole, which is shorter than its diff:
```python
import functools

import jax
import jax.numpy as jnp
import ml_dtypes
import numpy as np
from jax import lax
from jax.experimental import pallas as pl
from jax.experimental.pallas import tpu as pltpu
from jax.sharding import PartitionSpec as P

BOX = 128
GRID_X = 64
REACH = 3
SHARE = 4
TILE = 32
HALF = 16
CHUNK = 512
PIECE = 256
HIGHEST = lax.Precision.HIGHEST


def split_three(values):
    parts = []
    for _ in range(3):
        part = lax.reduce_precision(values, 8, 7)
        parts.append(part.astype(jnp.bfloat16))
        values = values - part
    return parts


def phase_table(pixel_count):
    levels = np.arange(-REACH, REACH + 1)
    pixel = np.arange(pixel_count).reshape(-1, PIECE)
    shift_x = np.repeat(levels, levels.size)[:, None, None]
    shift_y = np.tile(levels, levels.size)[:, None, None]
    angle = 2.0 * np.pi / BOX * (
        shift_x * (pixel % GRID_X - GRID_X // 2) + shift_y * (pixel // GRID_X))
    rest = np.stack([np.cos(angle), np.sin(angle)], axis=2).reshape(levels.size**2, -1).astype(np.float32)
    parts = []
    for _ in range(3):
        part = rest.astype(ml_dtypes.bfloat16)
        parts.append(part)
        rest = rest - part.astype(np.float32)
    rows = np.concatenate(parts, axis=0)
    count = levels.size**2
    padded = np.zeros((256, rows.shape[1]), ml_dtypes.bfloat16)
    padded[: rows.shape[0]] = rows
    label = np.full((1, 256), -1.0, np.float32)
    label[0, : rows.shape[0]] = np.arange(rows.shape[0]) % count
    return (padded, label)


def swap(values, axis, bit):
    count = lax.axis_size(axis)
    return lax.ppermute(values, axis, [(index, index ^ bit) for index in range(count)])


def three(values):
    high = values.astype(jnp.bfloat16)
    rest = values - high.astype(jnp.float32)
    middle = rest.astype(jnp.bfloat16)
    return [high, middle, (rest - middle.astype(jnp.float32)).astype(jnp.bfloat16)]


contract_last = (((1,), (1,)), ((), ()))


def penalties_of(views, dtab_ref, ori, pixels):
    groups = dtab_ref.shape[0] // 3
    parted = jnp.zeros((3 * groups, ori), jnp.float32)
    for first in range(0, pixels, CHUNK):
        real = views(slice(first, first + CHUNK)).astype(jnp.float32)
        imag = views(slice(pixels + first, pixels + first + CHUNK)).astype(jnp.float32)
        for part in three(real * real + imag * imag)[:2]:
            parted += lax.dot_general(dtab_ref[:, first:first + CHUNK], part, contract_last,
                                      preferred_element_type=jnp.float32)
    return -0.5 * (parted[:groups] + parted[groups:2 * groups] + parted[2 * groups:])


def views_of(q_refs, spots):
    def views(cols):
        return jnp.concatenate([member[spot, :, cols] for member, spot in zip(q_refs, spots)], axis=0)
    return views


def penalty_kernel(pieces, dtab_ref, *refs):
    out_ref = refs[pieces]
    for place in range(out_ref.shape[0]):
        views = views_of(refs[:pieces], [place] * pieces)
        out_ref[place] = penalties_of(views, dtab_ref, out_ref.shape[2], dtab_ref.shape[1])


def own_penalties(dtab, pieces):
    classes, rows_q, width = pieces[0].shape
    ori = rows_q * len(pieces)
    vmem = pl.BlockSpec(memory_space=pltpu.VMEM)
    return pl.pallas_call(
        functools.partial(penalty_kernel, len(pieces)),
        out_shape=jax.ShapeDtypeStruct((classes, dtab.shape[0] // 3, ori), jnp.float32),
        in_specs=[vmem] * (1 + len(pieces)),
        out_specs=vmem,
        compiler_params=pltpu.CompilerParams(vmem_limit_bytes=24 * 1024 * 1024),
    )(dtab, *pieces)


def stats_kernel(trans, spots, share, have_penalty, tiles_ref, rank_ref, meta_ref, label_ref, table_ref,
                 wtab_ref, dtab_ref, *refs):
    if have_penalty:
        penalty_ref, refs = refs[0], refs[1:]
    x_refs = refs[:share]
    q_refs = refs[share:share + len(spots)]
    out_ref, uv, pens, info, stats, shifted = refs[share + len(spots):]
    rows_all = rank_ref.shape[1]
    slots = uv.shape[0]
    pixels = uv.shape[1] // 2
    ori = pens.shape[1]
    groups = dtab_ref.shape[0] // 3
    views = views_of(q_refs, spots)

    def particles(cols):
        return jnp.concatenate([member[:, cols] for member in x_refs], axis=0)

    row = lax.broadcasted_iota(jnp.int32, (slots, rows_all), 0)
    pick = jnp.where(rank_ref[...] == row, 1.0, 0.0).astype(jnp.bfloat16)
    info[...] = jnp.dot(pick, meta_ref[...], preferred_element_type=jnp.float32)
    lane = lax.broadcasted_iota(jnp.int32, (slots, 3 * groups), 1)
    group_hot = jnp.where(info[:, trans:trans + 1] == (lane % groups).astype(jnp.float32), 1.0, 0.0)
    group_hot = group_hot.astype(jnp.bfloat16)
    stats[...] = jnp.zeros_like(stats)
    for first in range(0, pixels, CHUNK):
        weight = jnp.dot(group_hot, wtab_ref[:, first:first + CHUNK], preferred_element_type=jnp.float32)
        for start in (first, pixels + first):
            span = slice(start, start + CHUNK)
            uv[:, span] = weight * jnp.dot(pick, particles(span), preferred_element_type=jnp.float32)
    penalty = penalty_ref[spots[0]] if have_penalty else penalties_of(views, dtab_ref, ori, pixels)
    pens[...] = jnp.dot(group_hot, jnp.concatenate(three(penalty), axis=0),
                        preferred_element_type=jnp.float32)
    label = label_ref[...]

    def one_tile(start, size):
        mine = pl.ds(pl.multiple_of(start, HALF), size)
        here = info[mine, :]
        hot = jnp.concatenate(
            [jnp.where(here[:, t:t + 1] == label, 1.0, 0.0) for t in range(trans)], axis=0
        ).astype(jnp.bfloat16)
        for first in range(0, pixels, PIECE):
            phase = jnp.dot(hot, table_ref[:, 2 * first:2 * (first + PIECE)],
                            preferred_element_type=jnp.float32)
            real = uv[mine, first:first + PIECE]
            imag = uv[mine, pixels + first:pixels + first + PIECE]
            for t in range(trans):
                rows = slice(t * size, (t + 1) * size)
                cosine = phase[rows, :PIECE]
                sine = phase[rows, PIECE:]
                shifted[rows, first:first + PIECE] = (real * cosine + imag * sine).astype(jnp.bfloat16)
                shifted[rows, pixels + first:pixels + first + PIECE] = (
                    imag * cosine - real * sine).astype(jnp.bfloat16)
        scores = lax.dot_general(shifted[:trans * size, :], views(slice(0, 2 * pixels)), contract_last,
                                 preferred_element_type=jnp.float32)
        full = scores.reshape(trans, size, ori) + pens[mine, :][None]
        highest = jnp.max(jnp.max(full, axis=0), axis=1, keepdims=True)
        total = jnp.zeros((size, ori), jnp.float32)
        moment_x = jnp.zeros((size, ori), jnp.float32)
        moment_y = jnp.zeros((size, ori), jnp.float32)
        for t in range(trans):
            term = jnp.exp(full[t] - highest)
            total += term
            moment_x += term * here[:, trans + 1 + t:trans + 2 + t]
            moment_y += term * here[:, 2 * trans + 1 + t:2 * trans + 2 + t]
        total = jnp.sum(total, axis=1, keepdims=True)
        moment_x = jnp.sum(moment_x, axis=1, keepdims=True)
        moment_y = jnp.sum(moment_y, axis=1, keepdims=True)
        lanes = lax.broadcasted_iota(jnp.int32, (size, 128), 1)
        stats[mine, :] = jnp.where(
            lanes == 0, highest,
            jnp.where(lanes == 1, total, jnp.where(lanes == 2, moment_x,
                                                   jnp.where(lanes == 3, moment_y, 0.0))))

    halves = tiles_ref[0]

    @pl.loop(0, halves // 2)
    def _(tile):
        one_tile(tile * TILE, TILE)

    @pl.when(halves % 2 == 1)
    def _():
        one_tile((halves - 1) * HALF, HALF)

    back = sum(
        lax.dot_general(part, pick, (((0,), (0,)), ((), ())), preferred_element_type=jnp.float32)
        for part in three(stats[...])
    )
    out_ref[0] = back[:8, :]


def class_stats(tiles, rank, meta, label, table, wtab, dtab, penalty, x_parts, q_parts, trans, slots):
    rows_all = rank.shape[1]
    rows_q, width = q_parts[0][0].shape[1:]
    ori = rows_q * len(q_parts)
    arrays = [array for array, _ in q_parts]
    spots = [spot for _, spot in q_parts]
    extra = [] if penalty is None else [penalty]
    vmem = pl.BlockSpec(memory_space=pltpu.VMEM)
    return pl.pallas_call(
        functools.partial(stats_kernel, trans, spots, len(x_parts), penalty is not None),
        out_shape=jax.ShapeDtypeStruct((1, 8, rows_all), jnp.float32),
        in_specs=[pl.BlockSpec(memory_space=pltpu.SMEM)]
        + [vmem] * (6 + len(extra) + len(x_parts) + len(arrays)),
        out_specs=vmem,
        scratch_shapes=[
            pltpu.VMEM((slots, width), jnp.float32),
            pltpu.VMEM((slots, ori), jnp.float32),
            pltpu.VMEM((slots, 128), jnp.float32),
            pltpu.VMEM((slots, 128), jnp.float32),
            pltpu.VMEM((trans * TILE, width), jnp.bfloat16),
        ],
        compiler_params=pltpu.CompilerParams(vmem_limit_bytes=36 * 1024 * 1024),
        cost_estimate=pl.CostEstimate(
            flops=20 * slots * trans * width * (ori + 256),
            bytes_accessed=(rows_all + ori) * width * 2,
            transcendentals=0,
        ),
    )(tiles, rank, meta, label, table, wtab, dtab, *extra, *x_parts, *arrays)


def on_device(particles, candidates, ctf_ids, offsets, ctf_table, sigma_sq, projections):
    pose_count = lax.axis_size("pose")
    dom_count = lax.axis_size("dom")
    pose = lax.axis_index("pose")
    local = projections.shape[0]
    class_total = local * pose_count
    rows, picks = candidates.shape
    trans = offsets.shape[2]
    pixels = sigma_sq.shape[0]
    capacity = 3 * rows * picks // class_total
    share = min(SHARE, pose_count)
    share_bits = [1 << b for b in range(share.bit_length() - 1)]
    families = pose_count // share
    slots = -(-min(share * capacity, share * rows) // TILE) * TILE

    dom_bits = [1 << b for b in range(dom_count.bit_length() - 1)][::-1]

    order = [0]
    for bit in share_bits[::-1]:
        order = order + [member ^ bit for member in order]

    single = {bit: swap(particles, "pose", bit) for bit in share_bits[::-1]}
    own_pieces = [projections] + [swap(projections, "dom", bit) for bit in dom_bits]
    chunks = [projections[spot:spot + 1] for spot in range(local)]

    offsets, *_ = lax.optimization_barrier((offsets, own_pieces[-1]))
    offset_f = offsets.astype(jnp.float32)
    combo = (offset_f[:, 0] + REACH) * (2 * REACH + 1) + (offset_f[:, 1] + REACH)
    meta = jnp.concatenate(
        [combo, ctf_ids[:, None].astype(jnp.float32), offset_f[:, 0], offset_f[:, 1],
         candidates.astype(jnp.float32)], axis=1)
    meta = jnp.pad(meta, ((0, 0), (0, 128 - meta.shape[1]))).astype(jnp.bfloat16)
    metas = [swap(meta, "pose", member) if member else meta for member in order]
    meta_all = jnp.concatenate(metas, axis=0)

    single, own_pieces, chunks = lax.optimization_barrier((single, own_pieces, chunks))

    x_parts = []
    for member in order:
        bits = [bit for bit in share_bits if member & bit]
        part = single[bits[-1]] if bits else particles
        for bit in bits[:-1]:
            part = swap(part, "pose", bit)
        x_parts.append(part)

    far = []
    for family in range(1, families):
        members = []
        for spot in range(local):
            if members:
                chunks[spot], members[-1] = lax.optimization_barrier((chunks[spot], members[-1]))
            members.append(swap(chunks[spot], "pose", family * share))
        far.append(members)
    own_pieces = own_pieces + [swap(own_pieces[1], "dom", bit) for bit in dom_bits[1:]]

    named = meta_all[:, 3 * trans + 1:3 * trans + 1 + picks].astype(jnp.int32)
    owner = pose ^ (jnp.arange(families, dtype=jnp.int32) * share)
    class_ids = (owner[:, None] * local + jnp.arange(local, dtype=jnp.int32)[None, :]).reshape(-1)
    names = jnp.any(named.T[None, :, :] == class_ids[:, None, None], axis=1).astype(jnp.int32)
    ahead = jnp.cumsum(names, axis=1)
    rank = jnp.where(names > 0, ahead - 1, -1)
    tiles = (ahead[:, -1] + (HALF - 1)) // HALF

    weight = ctf_table / sigma_sq[None, :]
    wtab = jnp.concatenate(split_three(weight), axis=0)
    dtab = jnp.concatenate(split_three(weight * ctf_table), axis=0)

    table, label = phase_table(pixels)
    table, label = jnp.asarray(table), jnp.asarray(label)
    own_penalty = own_penalties(dtab, own_pieces)
    results = []

    def one_class(index, members, penalty):
        turn = tiles[index:index + 1]
        if results:
            turn, results[-1] = lax.optimization_barrier((turn, results[-1]))
        results.append(class_stats(turn, rank[index:index + 1], meta_all, label, table, wtab, dtab, penalty,
                                   x_parts, members, trans, slots))

    for spot in range(local):
        one_class(spot, [(piece, spot) for piece in own_pieces], own_penalty)
    for family in range(1, families):
        for spot in range(local):
            pieces = [far[family - 1][spot]]
            for hop, bit in enumerate(dom_bits):
                if spot:
                    tie = -1 if hop else spot
                    pieces[hop:], results[tie] = lax.optimization_barrier((pieces[hop:], results[tie]))
                pieces = pieces + [swap(member, "dom", bit) for member in pieces]
            one_class(family * local + spot, [(member, 0) for member in pieces], None)
    stats = jnp.concatenate(results, axis=0)[:, :4, :]
    own = []
    for place, member in enumerate(order):
        block = stats[:, :, place * rows:(place + 1) * rows]
        block = swap(block, "pose", member) if member else block
        own += [(member, spot, block[spot]) for spot in range(families * local)]

    cand = candidates.T
    owner = cand // local
    beyond = (owner ^ pose) // share
    within = (owner ^ pose) % share
    position = beyond * local + cand % local
    picked = jnp.zeros((picks, 4, rows), jnp.float32)
    for member, spot, block in own:
        hit = (within == member) & (position == spot)
        picked = jnp.where(hit[:, None, :], block[None], picked)
    log_weight = picked[:, 0] + jnp.log(picked[:, 1])
    raw_weight = jnp.exp(log_weight - jnp.max(log_weight, axis=0, keepdims=True))
    class_prob = raw_weight / jnp.sum(raw_weight, axis=0, keepdims=True)
    mean_x = jnp.sum(class_prob * picked[:, 2] / picked[:, 1], axis=0)
    mean_y = jnp.sum(class_prob * picked[:, 3] / picked[:, 1], axis=0)
    return (class_prob.T, jnp.stack([mean_x, mean_y], axis=1))


def solution(mesh):
    in_specs = (
        P(("pose", "dom"), None),
        P(("pose", "dom"), None),
        P(("pose", "dom")),
        P(("pose", "dom"), None, None),
        P(),
        P(),
        P("pose", "dom", None),
    )
    out_specs = (P(("pose", "dom"), None), P(("pose", "dom"), None))
    return jax.shard_map(
        on_device, mesh=mesh, in_specs=in_specs, out_specs=out_specs, check_vma=False
    )
```

time: 147 us -> 127 us (0.86)
  waiting for transfers between devices: 58.1 us -> 41.6 us
  starting transfers between devices: 23 us -> 20.8 us
    ppermute x20, waiting for transfers between devices: 58.1 us -> 41.6 us  [swap(): lax.ppermute(values, axis, [(index, index ^ bit) for index in range(count)])]
    pallas_call x4, Pallas kernels: 50.2 us -> 46.4 us  [class_stats(): pl.pallas_call(functools.partial(stats_kernel, trans, spots, len(x_parts)...]
    pallas_call x0 -> x1, Pallas kernels: none -> 2.8 us  [own_penalties(): pl.pallas_call(functools.partial(penalty_kernel, len(pieces)), out_shape=...]
    ppermute x20, starting transfers between devices: 23 us -> 20.8 us  [swap(): lax.ppermute(values, axis, [(index, index ^ bit) for index in range(count)])]
    unnamed x49, local copies, waits for them, and re-layouts: 2.61 us -> 0.74 us
  transfers between devices with their start and end apart: 20 -> 20, of which waited for: 9 -> 7; matrix products, arithmetic and copies ran while one was open for 6% -> 8% of each run, Pallas kernels for 22% -> 33%
where the time goes in v3:
time: 127 us; the launch traced here: 125 us
  Pallas kernels  49.2 us (39%)
  waiting for transfers between devices  41.6 us (33%)
  starting transfers between devices  20.8 us (16%)
  other arithmetic  6.71 us (5%)
  local copies, waits for them, and re-layouts  5.66 us (4%)
    pallas_call x4, Pallas kernels, class_stats(): pl.pallas_call(functools.partial(stats_kernel, trans, spots, len(x_parts)...  46.4 us
    ppermute x20, waiting for transfers between devices, swap(): lax.ppermute(values, axis, [(index, index ^ bit) for index in range(count)])  41.6 us
    ppermute x20, starting transfers between devices, swap(): lax.ppermute(values, axis, [(index, index ^ bit) for index in range(count)])  20.8 us
    pallas_call x1, Pallas kernels, own_penalties(): pl.pallas_call(functools.partial(penalty_kernel, len(pieces)), out_shape=...  2.8 us
  transfers between devices with their start and end apart: 20, of which 7 were waited for; matrix products, arithmetic and copies ran while one was open for 8% of the time, Pallas kernels for 33%

profile of v3, /device:TPU:0, one launch (start us, length us, event | category | flops | bytes accessed | tf_op | source)
XLA Modules:
  0.0 125.2 jit_solution(14837757700543682248)
XLA Ops:
  0.7 3.0 %collective-permute-start.4 = (bf16[128,4096]{1,0:T(8,128)(2,1)}, bf16[128,4096]{1,0:T(8,128)(2,1)}, u32[]{:S(2)}, u32[]{:S(2)}) collective-permute-start(bf16[128,4096]{1,0:T(8,128)(2,1)} %refs_0_.4), channel_id=1, source_target_pairs={{0,4},{4,0},{8,12},{12,8},{16,20},{20,16},{24,28},{28,24},{1,5},{5... | collective-permute-start | bytes 3145736 | tf_op jit(solution)/shard_map/ppermute | solution.py:56
  3.7 1.6 %collective-permute-start.5 = (bf16[128,4096]{1,0:T(8,128)(2,1)}, bf16[128,4096]{1,0:T(8,128)(2,1)}, u32[]{:S(2)}, u32[]{:S(2)}) collective-permute-start(bf16[128,4096]{1,0:T(8,128)(2,1)} %refs_0_.4), channel_id=1, source_target_pairs={{0,8},{4,12},{8,0},{12,4},{16,24},{20,28},{24,16},{28,20},{1,9},{5... | collective-permute-start | bytes 3145736 | tf_op jit(solution)/shard_map/ppermute | solution.py:56
  5.3 1.5 %collective-permute-start.6 = (bf16[2,64,4096]{2,1,0:T(8,128)(2,1)}, bf16[2,64,4096]{2,1,0:T(8,128)(2,1)S(1)}, u32[]{:S(2)}, u32[]{:S(2)}) collective-permute-start(bf16[2,64,4096]{2,1,0:T(8,128)(2,1)} %refs_5_.1), channel_id=1, source_target_pairs={{0,2},{1,3},{2,0},{3,1},{4,6},{5,7},{6,4},{7,5},{8,10},{9,11},{10,... | collective-permute-start | bytes 3145736 | tf_op jit(solution)/shard_map/ppermute | solution.py:56
  6.8 2.4 %fusion.30 = (bf16[1,64,4096]{2,1,0:T(8,128)(2,1)}, bf16[1,64,4096]{2,1,0:T(8,128)(2,1)}) fusion(bf16[2,64,4096]{2,1,0:T(8,128)(2,1)} %refs_5_.1), kind=kLoop, calls=%fused_computation.109 | loop fusion | bytes 2097152 | tf_op jit(solution)/shard_map/slice | solution.py:250
  9.2 0.1 reduce-precision_convert_fusion.1
  9.3 0.5 fusion.22
  9.8 0.6 fusion.24
  10.5 0.7 pad_maximum_fusion.wtab_ref
  11.2 0.3 concatenate.16
  11.6 0.1 copy.25
  11.7 0.5 collective-permute-start.1
  12.2 0.5 collective-permute-start.2
  12.7 14.8 %collective-permute-done.4.refs_3_.refs_2_ = bf16[128,4096]{1,0:T(8,128)(2,1)} collective-permute-done((bf16[128,4096]{1,0:T(8,128)(2,1)}, bf16[128,4096]{1,0:T(8,128)(2,1)}, u32[]{:S(2)}, u32[]{:S(2)}) %collective-permute-start.4) | collective-permute-done | bytes 1048608 | tf_op jit(solution)/shard_map/ppermute | solution.py:56
  27.5 2.7 %collective-permute-start.3 = (bf16[128,128]{1,0:T(8,128)(2,1)S(1)}, bf16[128,128]{1,0:T(8,128)(2,1)}, u32[]{:S(2)}, u32[]{:S(2)}) collective-permute-start(bf16[128,128]{1,0:T(8,128)(2,1)S(1)} %pad.5), channel_id=1, source_target_pairs={{0,12},{4,8},{8,4},{12,0},{16,28},{20,24},{24,20},{28,16},{1,13},{... | collective-permute-start | bytes 98312 | tf_op jit(solution)/shard_map/ppermute | solution.py:56
  30.3 0.1 iota_add_fusion
  30.4 0.1 add.66
  30.5 0.6 collective-permute-done.6.refs_1_.refs_6_
  31.1 0.5 collective-permute-start.8
  31.6 2.6 %collective-permute-start.9 = (bf16[1,64,4096]{2,1,0:T(8,128)(2,1)}, bf16[1,64,4096]{2,1,0:T(8,128)(2,1)}, u32[]{:S(2)}, u32[]{:S(2)}) collective-permute-start(bf16[1,64,4096]{2,1,0:T(8,128)(2,1)} %get-tuple-element.30), channel_id=1, source_target_pairs={{0,16},{4,20},{8,24},{12,28},{16,0},{20,4},{24,8},{28,12},{1,17},{... | collective-permute-start | bytes 1572872 | tf_op jit(solution)/shard_map/ppermute | solution.py:56
  34.2 0.6 copy-done.6
  34.8 0.8 pad_maximum_fusion.2.meta_ref
  35.6 0.8 convert_bitcast_fusion
  36.4 1.1 copy.26
  37.5 0.1 compare_reduce_fusion
  37.6 1.2 reduce-window.6
  38.8 0.2 slice_reduce_fusion
  39.0 0.2 reduce-window.9
  39.2 0.1 add_bitcast_fusion
  39.3 0.2 fusion.7
  39.5 0.7 fusion.32
  40.2 17.7 %collective-permute-done.9.refs_4_ = bf16[1,64,4096]{2,1,0:T(8,128)(2,1)} collective-permute-done((bf16[1,64,4096]{2,1,0:T(8,128)(2,1)}, bf16[1,64,4096]{2,1,0:T(8,128)(2,1)}, u32[]{:S(2)}, u32[]{:S(2)}) %collective-permute-start.9) | collective-permute-done | bytes 524320 | tf_op jit(solution)/shard_map/ppermute | solution.py:56
  57.9 1.5 %collective-permute-start.12 = (bf16[1,64,4096]{2,1,0:T(8,128)(2,1)}, bf16[1,64,4096]{2,1,0:T(8,128)(2,1)S(1)}, u32[]{:S(2)}, u32[]{:S(2)}) collective-permute-start(bf16[1,64,4096]{2,1,0:T(8,128)(2,1)} %collective-permute-done.9.refs_4_), channel_id=1, source_target_pairs={{0,2},{1,3},{2,0},{3,1},{4,6},{5,7},{6,4},{7,5},{8,10},{9,11},{10,... | collective-permute-start | bytes 1572872 | tf_op jit(solution)/shard_map/ppermute | solution.py:56
  59.5 2.8 %shard_map.104.refs_0_ = f32[2,16,256]{2,1,0:T(8,128)S(1)} custom-call(bf16[48,2048]{1,0:T(8,128)(2,1)S(1)} %pad_maximum_fusion.1.dtab_ref, bf16[2,64,4096]{2,1,0:T(8,128)(2,1)S(1)} %copy-done, bf16[2,64,4096]{2,1,0:T(8,128)(2,1)S(1)} %collective-permute-done.6.refs_1_.refs_6_, bf16[2,64,4096]{2,1,0:T(8,128)(2,1)S(1)} %collective-permute-done.refs_2_.refs_7_, ...), custom_call_target="tpu_custom_call" | custom-call | tf_op jit(solution)/shard_map/pallas_call | solution.py:98
  62.4 18.3 %shard_map.105 = f32[1,8,512]{2,1,0:T(8,128)S(1)} custom-call(s32[1]{0:T(128)} %get-tuple-element.103.tiles_ref, s32[1,512]{1,0:T(1,128)S(1)} %get-tuple-element.92.rank_ref, bf16[512,128]{1,0:T(8,128)(2,1)S(1)} %pad_maximum_fusion.2.meta_ref, f32[1,256]{1,0:T(1,128)S(1)} %copy-done.4, bf16[256,4096]{1,0:T(8,128)(2,1)S(1)} %copy-done.3, ...), custom_call_target="tpu_custom_call" | custom-call | flops 72477573120 | bytes 6291456 | tf_op jit(solution)/shard_map/pallas_call | solution.py:205
  80.7 0.6 collective-permute-start.14
  81.2 11.0 %shard_map.106 = f32[1,8,512]{2,1,0:T(8,128)S(1)} custom-call(s32[1]{0:T(128)} %get-tuple-element.32.tiles_ref, s32[1,512]{1,0:T(1,128)S(1)} %get-tuple-element.91.rank_ref, bf16[512,128]{1,0:T(8,128)(2,1)S(1)} %pad_maximum_fusion.2.meta_ref, f32[1,256]{1,0:T(1,128)S(1)} %copy-done.4, bf16[256,4096]{1,0:T(8,128)(2,1)S(1)} %copy-done.3, ...), custom_call_target="tpu_custom_call" | custom-call | flops 72477573120 | bytes 6291456 | tf_op jit(solution)/shard_map/pallas_call | solution.py:205
  92.3 0.1 collective-permute-start.11
  92.4 0.1 collective-permute-start.15
  92.5 9.4 %shard_map.107 = f32[1,8,512]{2,1,0:T(8,128)S(1)} custom-call(s32[1]{0:T(128)} %get-tuple-element.36.tiles_ref, s32[1,512]{1,0:T(1,128)S(1)} %get-tuple-element.90.rank_ref, bf16[512,128]{1,0:T(8,128)(2,1)S(1)} %pad_maximum_fusion.2.meta_ref, f32[1,256]{1,0:T(1,128)S(1)} %copy-done.4, bf16[256,4096]{1,0:T(8,128)(2,1)S(1)} %copy-done.3, ...), custom_call_target="tpu_custom_call" | custom-call | flops 72477573120 | bytes 6291456 | tf_op jit(solution)/shard_map/pallas_call | solution.py:205
  102.0 3.0 %collective-permute-done.11.refs_5_ = bf16[1,64,4096]{2,1,0:T(8,128)(2,1)S(1)} collective-permute-done((bf16[1,64,4096]{2,1,0:T(8,128)(2,1)}, bf16[1,64,4096]{2,1,0:T(8,128)(2,1)S(1)}, u32[]{:S(2)}, u32[]{:S(2)}) %collective-permute-start.11) | collective-permute-done | bytes 524320 | tf_op jit(solution)/shard_map/ppermute | solution.py:56
  105.1 1.8 %collective-permute-done.16.refs_7_ = bf16[1,64,4096]{2,1,0:T(8,128)(2,1)S(1)} collective-permute-done((bf16[1,64,4096]{2,1,0:T(8,128)(2,1)S(1)}, bf16[1,64,4096]{2,1,0:T(8,128)(2,1)S(1)}, u32[]{:S(2)}, u32[]{:S(2)}) %collective-permute-start.16) | collective-permute-done | bytes 524320 | tf_op jit(solution)/shard_map/ppermute | solution.py:56
  106.9 7.7 %shard_map.108 = f32[1,8,512]{2,1,0:T(8,128)S(1)} custom-call(s32[1]{0:T(128)} %get-tuple-element.40.tiles_ref, s32[1,512]{1,0:T(1,128)S(1)} %get-tuple-element.89.rank_ref, bf16[512,128]{1,0:T(8,128)(2,1)S(1)} %pad_maximum_fusion.2.meta_ref, f32[1,256]{1,0:T(1,128)S(1)} %copy-done.4, bf16[256,4096]{1,0:T(8,128)(2,1)S(1)} %copy-done.3, ...), custom_call_target="tpu_custom_call" | custom-call | flops 72477573120 | bytes 6291456 | tf_op jit(solution)/shard_map/pallas_call | solution.py:205
  114.6 0.1 collective-permute-start.17
  114.7 5.5 %collective-permute-start.18 = (f32[4,4,128]{2,1,0:T(4,128)S(1)}, f32[4,4,128]{2,1,0:T(4,128)S(1)}, u32[]{:S(2)}, u32[]{:S(2)}) collective-permute-start(f32[4,4,128]{2,1,0:T(4,128)S(1)} %get-tuple-element.73), channel_id=1, source_target_pairs={{0,4},{4,0},{8,12},{12,8},{16,20},{20,16},{24,28},{28,24},{1,5},{5... | collective-permute-start | bytes 24584 | tf_op jit(solution)/shard_map/ppermute | solution.py:56
  120.2 1.6 %collective-permute-done.18 = f32[4,4,128]{2,1,0:T(4,128)S(1)} collective-permute-done((f32[4,4,128]{2,1,0:T(4,128)S(1)}, f32[4,4,128]{2,1,0:T(4,128)S(1)}, u32[]{:S(2)}, u32[]{:S(2)}) %collective-permute-start.18) | collective-permute-done | bytes 8224 | tf_op jit(solution)/shard_map/ppermute | solution.py:56
  121.9 2.0 %collective-permute-done.19 = f32[4,4,128]{2,1,0:T(4,128)S(1)} collective-permute-done((f32[4,4,128]{2,1,0:T(4,128)S(1)}, f32[4,4,128]{2,1,0:T(4,128)S(1)}, u32[]{:S(2)}, u32[]{:S(2)}) %collective-permute-start.19) | collective-permute-done | bytes 8224 | tf_op jit(solution)/shard_map/ppermute | solution.py:56
  124.1 0.6 fusion.15
  124.6 0.6 pad_maximum_fusion.8
  (91 shorter events, 0.4 us)
Async XLA Ops:
  0.6 8.6 %copy-start.5 = (f32[16,2048]{1,0:T(8,128)S(1)}, f32[16,2048]{1,0:T(8,128)}, u32[]{:S(2)}) copy-start(f32[16,2048]{1,0:T(8,128)} %param.13) | copy-start | bytes 393220
  0.6 8.5 %copy-start.8 = (f32[2048]{0:T(1024)S(1)}, f32[2048]{0:T(1024)}, u32[]{:S(2)}) copy-start(f32[2048]{0:T(1024)} %param.14) | copy-start | bytes 24580
  0.7 8.6 %copy-start.22 = (s32[128,2]{0,1:T(2,128)S(1)}, s32[128,2]{0,1:T(2,128)}, u32[]{:S(2)}) copy-start(s32[128,2]{0,1:T(2,128)} %param.10) | copy-start | bytes 3076
  0.7 10.5 %copy-start.23 = (s32[128]{0:T(128)S(1)}, s32[128]{0:T(128)}, u32[]{:S(2)}) copy-start(s32[128]{0:T(128)} %param.11) | copy-start | bytes 1540
  0.7 10.5 %copy-start.7 = (s32[128,2,9]{0,1,2:T(2,128)S(1)}, s32[128,2,9]{0,1,2:T(2,128)}, u32[]{:S(2)}) copy-start(s32[128,2,9]{0,1,2:T(2,128)} %param.12) | copy-start | bytes 27652
  0.7 26.9 %collective-permute-start.4 = (bf16[128,4096]{1,0:T(8,128)(2,1)}, bf16[128,4096]{1,0:T(8,128)(2,1)}, u32[]{:S(2)}, u32[]{:S(2)}) collective-permute-start(bf16[128,4096]{1,0:T(8,128)(2,1)} %refs_0_.4), channel_id=1, source_target_pairs={{0,4},{4,0},{8,12},{12,8},{16,20},{20,16},{24,28},{28,24},{1,5},{5... | collective-permute-start | bytes 3145736 | tf_op jit(solution)/shard_map/ppermute | solution.py:56
  3.7 26.7 %collective-permute-start.5 = (bf16[128,4096]{1,0:T(8,128)(2,1)}, bf16[128,4096]{1,0:T(8,128)(2,1)}, u32[]{:S(2)}, u32[]{:S(2)}) collective-permute-start(bf16[128,4096]{1,0:T(8,128)(2,1)} %refs_0_.4), channel_id=1, source_target_pairs={{0,8},{4,12},{8,0},{12,4},{16,24},{20,28},{24,16},{28,20},{1,9},{5... | collective-permute-start | bytes 3145736 | tf_op jit(solution)/shard_map/ppermute | solution.py:56
  5.3 5.9 %collective-permute-start = (bf16[2,64,4096]{2,1,0:T(8,128)(2,1)}, bf16[2,64,4096]{2,1,0:T(8,128)(2,1)S(1)}, u32[]{:S(2)}, u32[]{:S(2)}) collective-permute-start(bf16[2,64,4096]{2,1,0:T(8,128)(2,1)} %refs_5_.1), channel_id=1, source_target_pairs={{0,1},{1,0},{2,3},{3,2},{4,5},{5,4},{6,7},{7,6},{8,9},{9,8},{10,11... | collective-permute-start | bytes 3145736 | tf_op jit(solution)/shard_map/ppermute | solution.py:56
  5.3 25.8 %collective-permute-start.6 = (bf16[2,64,4096]{2,1,0:T(8,128)(2,1)}, bf16[2,64,4096]{2,1,0:T(8,128)(2,1)S(1)}, u32[]{:S(2)}, u32[]{:S(2)}) collective-permute-start(bf16[2,64,4096]{2,1,0:T(8,128)(2,1)} %refs_5_.1), channel_id=1, source_target_pairs={{0,2},{1,3},{2,0},{3,1},{4,6},{5,7},{6,4},{7,5},{8,10},{9,11},{10,... | collective-permute-start | bytes 3145736 | tf_op jit(solution)/shard_map/ppermute | solution.py:56
  6.8 52.7 %copy-start = (bf16[2,64,4096]{2,1,0:T(8,128)(2,1)S(1)}, bf16[2,64,4096]{2,1,0:T(8,128)(2,1)}, u32[]{:S(2)}) copy-start(bf16[2,64,4096]{2,1,0:T(8,128)(2,1)} %refs_5_.1) | copy-start | bytes 3145732
  11.7 19.9 %collective-permute-start.1 = (bf16[128,128]{1,0:T(8,128)(2,1)S(1)}, bf16[128,128]{1,0:T(8,128)(2,1)S(1)}, u32[]{:S(2)}, u32[]{:S(2)}) collective-permute-start(bf16[128,128]{1,0:T(8,128)(2,1)S(1)} %pad.5), channel_id=1, source_target_pairs={{0,8},{4,12},{8,0},{12,4},{16,24},{20,28},{24,16},{28,20},{1,9},{5... | collective-permute-start | bytes 98312 | tf_op jit(solution)/shard_map/ppermute | solution.py:56
  12.2 22.0 %collective-permute-start.2 = (bf16[128,128]{1,0:T(8,128)(2,1)S(1)}, bf16[128,128]{1,0:T(8,128)(2,1)S(1)}, u32[]{:S(2)}, u32[]{:S(2)}) collective-permute-start(bf16[128,128]{1,0:T(8,128)(2,1)S(1)} %pad.5), channel_id=1, source_target_pairs={{0,4},{4,0},{8,12},{12,8},{16,20},{20,16},{24,28},{28,24},{1,5},{5... | collective-permute-start | bytes 98312 | tf_op jit(solution)/shard_map/ppermute | solution.py:56
  27.5 7.3 %collective-permute-start.3 = (bf16[128,128]{1,0:T(8,128)(2,1)S(1)}, bf16[128,128]{1,0:T(8,128)(2,1)}, u32[]{:S(2)}, u32[]{:S(2)}) collective-permute-start(bf16[128,128]{1,0:T(8,128)(2,1)S(1)} %pad.5), channel_id=1, source_target_pairs={{0,12},{4,8},{8,4},{12,0},{16,28},{20,24},{24,20},{28,16},{1,13},{... | collective-permute-start | bytes 98312 | tf_op jit(solution)/shard_map/ppermute | solution.py:56
  31.1 28.4 %collective-permute-start.7 = (bf16[2,64,4096]{2,1,0:T(8,128)(2,1)S(1)}, bf16[2,64,4096]{2,1,0:T(8,128)(2,1)}, u32[]{:S(2)}, u32[]{:S(2)}) collective-permute-start(bf16[2,64,4096]{2,1,0:T(8,128)(2,1)S(1)} %collective-permute-done.6.refs_1_.refs_6_), channel_id=1, source_target_pairs={{0,1},{1,0},{2,3},{3,2},{4,5},{5,4},{6,7},{7,6},{8,9},{9,8},{10,11... | collective-permute-start | bytes 3145736 | tf_op jit(solution)/shard_map/ppermute | solution.py:56
  31.1 31.2 %collective-permute-start.8 = (bf16[128,4096]{1,0:T(8,128)(2,1)}, bf16[128,4096]{1,0:T(8,128)(2,1)}, u32[]{:S(2)}, u32[]{:S(2)}) collective-permute-start(bf16[128,4096]{1,0:T(8,128)(2,1)} %collective-permute-done.5.refs_2_.refs_1_), channel_id=1, source_target_pairs={{0,4},{4,0},{8,12},{12,8},{16,20},{20,16},{24,28},{28,24},{1,5},{5... | collective-permute-start | bytes 3145736 | tf_op jit(solution)/shard_map/ppermute | solution.py:56
  31.6 26.3 %collective-permute-start.9 = (bf16[1,64,4096]{2,1,0:T(8,128)(2,1)}, bf16[1,64,4096]{2,1,0:T(8,128)(2,1)}, u32[]{:S(2)}, u32[]{:S(2)}) collective-permute-start(bf16[1,64,4096]{2,1,0:T(8,128)(2,1)} %get-tuple-element.30), channel_id=1, source_target_pairs={{0,16},{4,20},{8,24},{12,28},{16,0},{20,4},{24,8},{28,12},{1,17},{... | collective-permute-start | bytes 1572872 | tf_op jit(solution)/shard_map/ppermute | solution.py:56
  34.2 0.6 copy-start.6
  40.2 22.1 %copy-start.1 = (bf16[48,2048]{1,0:T(8,128)(2,1)S(1)}, bf16[48,2048]{1,0:T(8,128)(2,1)}, u32[]{:S(2)}) copy-start(bf16[48,2048]{1,0:T(8,128)(2,1)} %pad_maximum_fusion.wtab_ref) | copy-start | bytes 589828
  40.2 22.1 %copy-start.2 = (bf16[128,4096]{1,0:T(8,128)(2,1)S(1)}, bf16[128,4096]{1,0:T(8,128)(2,1)}, u32[]{:S(2)}) copy-start(bf16[128,4096]{1,0:T(8,128)(2,1)} %refs_0_.4) | copy-start | bytes 3145732
  40.2 22.1 %copy-start.3 = (bf16[256,4096]{1,0:T(8,128)(2,1)S(1)}, bf16[256,4096]{1,0:T(8,128)(2,1)}, u32[]{:S(2)}) copy-start(bf16[256,4096]{1,0:T(8,128)(2,1)} %constant.96.clone.table_ref) | copy-start | bytes 6291460
  40.2 22.1 %copy-start.4 = (f32[1,256]{1,0:T(1,128)S(1)}, f32[1,256]{1,0:T(1,128)}, u32[]{:S(2)}) copy-start(f32[1,256]{1,0:T(1,128)} %constant.97.clone.label_ref) | copy-start | bytes 3076
  57.9 22.7 %collective-permute-start.12 = (bf16[1,64,4096]{2,1,0:T(8,128)(2,1)}, bf16[1,64,4096]{2,1,0:T(8,128)(2,1)S(1)}, u32[]{:S(2)}, u32[]{:S(2)}) collective-permute-start(bf16[1,64,4096]{2,1,0:T(8,128)(2,1)} %collective-permute-done.9.refs_4_), channel_id=1, source_target_pairs={{0,2},{1,3},{2,0},{3,1},{4,6},{5,7},{6,4},{7,5},{8,10},{9,11},{10,... | collective-permute-start | bytes 1572872 | tf_op jit(solution)/shard_map/ppermute | solution.py:56
  59.5 33.0 %collective-permute-start.13 = (bf16[1,64,4096]{2,1,0:T(8,128)(2,1)}, bf16[1,64,4096]{2,1,0:T(8,128)(2,1)}, u32[]{:S(2)}, u32[]{:S(2)}) collective-permute-start(bf16[1,64,4096]{2,1,0:T(8,128)(2,1)} %collective-permute-done.9.refs_4_), channel_id=1, source_target_pairs={{0,1},{1,0},{2,3},{3,2},{4,5},{5,4},{6,7},{7,6},{8,9},{9,8},{10,11... | collective-permute-start | bytes 1572872 | tf_op jit(solution)/shard_map/ppermute | solution.py:56
  59.5 32.8 %collective-permute-start.10 = (bf16[1,64,4096]{2,1,0:T(8,128)(2,1)}, bf16[1,64,4096]{2,1,0:T(8,128)(2,1)}, u32[]{:S(2)}, u32[]{:S(2)}) collective-permute-start(bf16[1,64,4096]{2,1,0:T(8,128)(2,1)} %get-tuple-element.31), channel_id=1, source_target_pairs={{0,16},{4,20},{8,24},{12,28},{16,0},{20,4},{24,8},{28,12},{1,17},{... | collective-permute-start | bytes 1572872 | tf_op jit(solution)/shard_map/ppermute | solution.py:56
  80.7 11.8 %collective-permute-start.14 = (bf16[1,64,4096]{2,1,0:T(8,128)(2,1)S(1)}, bf16[1,64,4096]{2,1,0:T(8,128)(2,1)S(1)}, u32[]{:S(2)}, u32[]{:S(2)}) collective-permute-start(bf16[1,64,4096]{2,1,0:T(8,128)(2,1)S(1)} %collective-permute-done.12.refs_5_), channel_id=1, source_target_pairs={{0,1},{1,0},{2,3},{3,2},{4,5},{5,4},{6,7},{7,6},{8,9},{9,8},{10,11... | collective-permute-start | bytes 1572872 | tf_op jit(solution)/shard_map/ppermute | solution.py:56
  92.3 12.7 %collective-permute-start.11 = (bf16[1,64,4096]{2,1,0:T(8,128)(2,1)}, bf16[1,64,4096]{2,1,0:T(8,128)(2,1)S(1)}, u32[]{:S(2)}, u32[]{:S(2)}) collective-permute-start(bf16[1,64,4096]{2,1,0:T(8,128)(2,1)} %collective-permute-done.10.refs_4_), channel_id=1, source_target_pairs={{0,2},{1,3},{2,0},{3,1},{4,6},{5,7},{6,4},{7,5},{8,10},{9,11},{10,... | collective-permute-start | bytes 1572872 | tf_op jit(solution)/shard_map/ppermute | solution.py:56
  92.4 12.7 %collective-permute-start.15 = (bf16[1,64,4096]{2,1,0:T(8,128)(2,1)}, bf16[1,64,4096]{2,1,0:T(8,128)(2,1)S(1)}, u32[]{:S(2)}, u32[]{:S(2)}) collective-permute-start(bf16[1,64,4096]{2,1,0:T(8,128)(2,1)} %collective-permute-done.10.refs_4_), channel_id=1, source_target_pairs={{0,1},{1,0},{2,3},{3,2},{4,5},{5,4},{6,7},{7,6},{8,9},{9,8},{10,11... | collective-permute-start | bytes 1572872 | tf_op jit(solution)/shard_map/ppermute | solution.py:56
  92.5 12.5 %copy-start.16 = (pred[2,128]{1,0:T(4,128)(4,1)S(1)}, pred[2,128]{1,0:T(4,128)(4,1)}, u32[]{:S(2)}) copy-start(pred[2,128]{1,0:T(4,128)(4,1)} %get-tuple-element.53) | copy-start | bytes 772
  92.5 12.5 %copy-start.17 = (pred[2,128]{1,0:T(4,128)(4,1)S(1)}, pred[2,128]{1,0:T(4,128)(4,1)}, u32[]{:S(2)}) copy-start(pred[2,128]{1,0:T(4,128)(4,1)} %get-tuple-element.98) | copy-start | bytes 772
  92.5 12.5 %copy-start.18 = (pred[2,128]{1,0:T(4,128)(4,1)S(1)}, pred[2,128]{1,0:T(4,128)(4,1)}, u32[]{:S(2)}) copy-start(pred[2,128]{1,0:T(4,128)(4,1)} %get-tuple-element.100) | copy-start | bytes 772
  92.5 12.5 %copy-start.19 = (pred[2,128]{1,0:T(4,128)(4,1)S(1)}, pred[2,128]{1,0:T(4,128)(4,1)}, u32[]{:S(2)}) copy-start(pred[2,128]{1,0:T(4,128)(4,1)} %get-tuple-element.115) | copy-start | bytes 772
  92.5 12.5 %copy-start.20 = (pred[2,128]{1,0:T(4,128)(4,1)S(1)}, pred[2,128]{1,0:T(4,128)(4,1)}, u32[]{:S(2)}) copy-start(pred[2,128]{1,0:T(4,128)(4,1)} %get-tuple-element.117) | copy-start | bytes 772
  92.5 12.5 %copy-start.21 = (pred[2,128]{1,0:T(4,128)(4,1)S(1)}, pred[2,128]{1,0:T(4,128)(4,1)}, u32[]{:S(2)}) copy-start(pred[2,128]{1,0:T(4,128)(4,1)} %get-tuple-element.119) | copy-start | bytes 772
  105.0 1.9 %collective-permute-start.16 = (bf16[1,64,4096]{2,1,0:T(8,128)(2,1)S(1)}, bf16[1,64,4096]{2,1,0:T(8,128)(2,1)S(1)}, u32[]{:S(2)}, u32[]{:S(2)}) collective-permute-start(bf16[1,64,4096]{2,1,0:T(8,128)(2,1)S(1)} %collective-permute-done.11.refs_5_), channel_id=1, source_target_pairs={{0,1},{1,0},{2,3},{3,2},{4,5},{5,4},{6,7},{7,6},{8,9},{9,8},{10,11... | collective-permute-start | bytes 1572872 | tf_op jit(solution)/shard_map/ppermute | solution.py:56
  106.9 17.0 %copy-start.9 = (pred[2,128]{1,0:T(4,128)(4,1)S(1)}, pred[2,128]{1,0:T(4,128)(4,1)}, u32[]{:S(2)}) copy-start(pred[2,128]{1,0:T(4,128)(4,1)} %get-tuple-element.47) | copy-start | bytes 772
  106.9 17.0 %copy-start.10 = (pred[2,128]{1,0:T(4,128)(4,1)S(1)}, pred[2,128]{1,0:T(4,128)(4,1)}, u32[]{:S(2)}) copy-start(pred[2,128]{1,0:T(4,128)(4,1)} %get-tuple-element.52) | copy-start | bytes 772
  106.9 17.0 %copy-start.11 = (pred[2,128]{1,0:T(4,128)(4,1)S(1)}, pred[2,128]{1,0:T(4,128)(4,1)}, u32[]{:S(2)}) copy-start(pred[2,128]{1,0:T(4,128)(4,1)} %get-tuple-element.97) | copy-start | bytes 772
  106.9 17.0 %copy-start.12 = (pred[2,128]{1,0:T(4,128)(4,1)S(1)}, pred[2,128]{1,0:T(4,128)(4,1)}, u32[]{:S(2)}) copy-start(pred[2,128]{1,0:T(4,128)(4,1)} %get-tuple-element.99) | copy-start | bytes 772
  106.9 17.0 %copy-start.13 = (pred[2,128]{1,0:T(4,128)(4,1)S(1)}, pred[2,128]{1,0:T(4,128)(4,1)}, u32[]{:S(2)}) copy-start(pred[2,128]{1,0:T(4,128)(4,1)} %get-tuple-element.114) | copy-start | bytes 772
  106.9 17.0 %copy-start.14 = (pred[2,128]{1,0:T(4,128)(4,1)S(1)}, pred[2,128]{1,0:T(4,128)(4,1)}, u32[]{:S(2)}) copy-start(pred[2,128]{1,0:T(4,128)(4,1)} %get-tuple-element.116) | copy-start | bytes 772
  106.9 17.0 %copy-start.15 = (pred[2,128]{1,0:T(4,128)(4,1)S(1)}, pred[2,128]{1,0:T(4,128)(4,1)}, u32[]{:S(2)}) copy-start(pred[2,128]{1,0:T(4,128)(4,1)} %get-tuple-element.118) | copy-start | bytes 772
  114.6 5.6 %collective-permute-start.17 = (f32[4,4,128]{2,1,0:T(4,128)S(1)}, f32[4,4,128]{2,1,0:T(4,128)S(1)}, u32[]{:S(2)}, u32[]{:S(2)}) collective-permute-start(f32[4,4,128]{2,1,0:T(4,128)S(1)} %get-tuple-element.72), channel_id=1, source_target_pairs={{0,12},{4,8},{8,4},{12,0},{16,28},{20,24},{24,20},{28,16},{1,13},{... | collective-permute-start | bytes 24584 | tf_op jit(solution)/shard_map/ppermute | solution.py:56
  114.7 7.1 %collective-permute-start.18 = (f32[4,4,128]{2,1,0:T(4,128)S(1)}, f32[4,4,128]{2,1,0:T(4,128)S(1)}, u32[]{:S(2)}, u32[]{:S(2)}) collective-permute-start(f32[4,4,128]{2,1,0:T(4,128)S(1)} %get-tuple-element.73), channel_id=1, source_target_pairs={{0,4},{4,0},{8,12},{12,8},{16,20},{20,16},{24,28},{28,24},{1,5},{5... | collective-permute-start | bytes 24584 | tf_op jit(solution)/shard_map/ppermute | solution.py:56
  120.2 3.7 %collective-permute-start.19 = (f32[4,4,128]{2,1,0:T(4,128)S(1)}, f32[4,4,128]{2,1,0:T(4,128)S(1)}, u32[]{:S(2)}, u32[]{:S(2)}) collective-permute-start(f32[4,4,128]{2,1,0:T(4,128)S(1)} %get-tuple-element.74), channel_id=1, source_target_pairs={{0,8},{4,12},{8,0},{12,4},{16,24},{20,28},{24,16},{28,20},{1,9},{5... | collective-permute-start | bytes 24584 | tf_op jit(solution)/shard_map/ppermute | solution.py:56

commit v4 on v3

v4 whole, which is shorter than its diff:
```python
import functools

import jax
import jax.numpy as jnp
import ml_dtypes
import numpy as np
from jax import lax
from jax.experimental import pallas as pl
from jax.experimental.pallas import tpu as pltpu
from jax.sharding import PartitionSpec as P

BOX = 128
GRID_X = 64
REACH = 3
SHARE = 4
TILE = 32
CHUNK = 512
PIECE = 256
HIGHEST = lax.Precision.HIGHEST


def split_three(values):
    parts = []
    for _ in range(3):
        part = lax.reduce_precision(values, 8, 7)
        parts.append(part.astype(jnp.bfloat16))
        values = values - part
    return parts


def phase_table(pixel_count):
    levels = np.arange(-REACH, REACH + 1)
    pixel = np.arange(pixel_count)
    shift_x = np.repeat(levels, levels.size)[:, None]
    shift_y = np.tile(levels, levels.size)[:, None]
    angle = 2.0 * np.pi / BOX * (shift_x * (pixel % GRID_X - 32) + shift_y * (pixel // GRID_X))
    rest = np.concatenate([np.cos(angle), np.sin(angle)], axis=1).astype(np.float32)
    parts = []
    for _ in range(3):
        part = rest.astype(ml_dtypes.bfloat16)
        parts.append(part)
        rest = rest - part.astype(np.float32)
    rows = np.concatenate(parts, axis=0)
    count = levels.size**2
    padded = np.zeros((256, 2 * pixel_count), ml_dtypes.bfloat16)
    padded[: rows.shape[0]] = rows
    label = np.full((1, 256), -1.0, np.float32)
    label[0, : rows.shape[0]] = np.arange(rows.shape[0]) % count
    return (padded, label)


def swap(values, axis, bit):
    count = lax.axis_size(axis)
    return lax.ppermute(values, axis, [(index, index ^ bit) for index in range(count)])


def three(values):
    high = values.astype(jnp.bfloat16)
    rest = values - high.astype(jnp.float32)
    middle = rest.astype(jnp.bfloat16)
    return [high, middle, (rest - middle.astype(jnp.float32)).astype(jnp.bfloat16)]


contract_last = (((1,), (1,)), ((), ()))


def penalties_of(views, dtab_ref, ori, pixels):
    groups = dtab_ref.shape[0] // 3
    parted = jnp.zeros((3 * groups, ori), jnp.float32)
    for first in range(0, pixels, CHUNK):
        real = views(slice(first, first + CHUNK)).astype(jnp.float32)
        imag = views(slice(pixels + first, pixels + first + CHUNK)).astype(jnp.float32)
        for part in three(real * real + imag * imag)[:2]:
            parted += lax.dot_general(dtab_ref[:, first:first + CHUNK], part, contract_last,
                                      preferred_element_type=jnp.float32)
    return -0.5 * (parted[:groups] + parted[groups:2 * groups] + parted[2 * groups:])


def views_of(q_refs, spots):
    def views(cols):
        return jnp.concatenate([member[spot, :, cols] for member, spot in zip(q_refs, spots)], axis=0)
    return views


def penalty_kernel(pieces, dtab_ref, *refs):
    out_ref = refs[pieces]
    for place in range(out_ref.shape[0]):
        views = views_of(refs[:pieces], [place] * pieces)
        out_ref[place] = penalties_of(views, dtab_ref, out_ref.shape[2], dtab_ref.shape[1])


def own_penalties(dtab, pieces):
    classes, rows_q, width = pieces[0].shape
    ori = rows_q * len(pieces)
    vmem = pl.BlockSpec(memory_space=pltpu.VMEM)
    return pl.pallas_call(
        functools.partial(penalty_kernel, len(pieces)),
        out_shape=jax.ShapeDtypeStruct((classes, dtab.shape[0] // 3, ori), jnp.float32),
        in_specs=[vmem] * (1 + len(pieces)),
        out_specs=vmem,
        compiler_params=pltpu.CompilerParams(vmem_limit_bytes=24 * 1024 * 1024),
    )(dtab, *pieces)


def stats_kernel(trans, index, spots, share, have_penalty, ids_ref, label_ref, table_ref, wtab_ref,
                 dtab_ref, *refs):
    if have_penalty:
        penalty_ref, refs = refs[0], refs[1:]
    meta_refs, refs = refs[:share], refs[share:]
    x_refs, refs = refs[:share], refs[share:]
    q_refs = refs[:len(spots)]
    out_ref, uv, pens, info, stats = refs[len(spots):]
    rows_all = out_ref.shape[2]
    slots = uv.shape[0]
    pixels = uv.shape[1] // 2
    ori = pens.shape[1]
    groups = dtab_ref.shape[0] // 3
    views = views_of(q_refs, spots)

    def particles(cols):
        return jnp.concatenate([member[:, cols] for member in x_refs], axis=0)

    meta = jnp.concatenate([member[...] for member in meta_refs], axis=1)
    named = meta[3 * trans + 1:, :].astype(jnp.float32)
    wanted = ids_ref[index].astype(jnp.float32)
    names = jnp.max(jnp.where(named == wanted, 1.0, 0.0), axis=0, keepdims=True)
    before = lax.broadcasted_iota(jnp.int32, (rows_all, rows_all), 0)
    after = lax.broadcasted_iota(jnp.int32, (rows_all, rows_all), 1)
    upper = jnp.where(before <= after, 1.0, 0.0).astype(jnp.bfloat16)
    ahead = jnp.dot(jnp.broadcast_to(names, (16, rows_all)).astype(jnp.bfloat16), upper,
                    preferred_element_type=jnp.float32)[:1]
    rank = jnp.where(names > 0.0, ahead - 1.0, -1.0).astype(jnp.int32)
    tiles = (jnp.max(ahead).astype(jnp.int32) + (TILE - 1)) // TILE

    row = lax.broadcasted_iota(jnp.int32, (slots, rows_all), 0)
    pick = jnp.where(rank == row, 1.0, 0.0).astype(jnp.bfloat16)
    info[...] = lax.dot_general(pick, meta, contract_last, preferred_element_type=jnp.float32)
    lane = lax.broadcasted_iota(jnp.int32, (slots, 3 * groups), 1)
    group_hot = jnp.where(info[:, trans:trans + 1] == (lane % groups).astype(jnp.float32), 1.0, 0.0)
    group_hot = group_hot.astype(jnp.bfloat16)
    stats[...] = jnp.zeros_like(stats)
    for first in range(0, pixels, CHUNK):
        weight = jnp.dot(group_hot, wtab_ref[:, first:first + CHUNK], preferred_element_type=jnp.float32)
        for start in (first, pixels + first):
            span = slice(start, start + CHUNK)
            uv[:, span] = weight * jnp.dot(pick, particles(span), preferred_element_type=jnp.float32)
    penalty = penalty_ref[spots[0]] if have_penalty else penalties_of(views, dtab_ref, ori, pixels)
    pens[...] = jnp.dot(group_hot, jnp.concatenate(three(penalty), axis=0),
                        preferred_element_type=jnp.float32)
    label = label_ref[...]

    @pl.loop(0, tiles)
    def _(tile):
        mine = pl.ds(pl.multiple_of(tile * TILE, TILE), TILE)
        here = info[mine, :]
        hot = jnp.concatenate(
            [jnp.where(here[:, t:t + 1] == label, 1.0, 0.0) for t in range(trans)], axis=0
        ).astype(jnp.bfloat16)
        scores = jnp.zeros((trans * TILE, ori), jnp.float32)
        for first in range(0, pixels, PIECE):
            cols = slice(first, first + PIECE)
            icols = slice(pixels + first, pixels + first + PIECE)
            cosine = jnp.dot(hot, table_ref[:, cols], preferred_element_type=jnp.float32)
            sine = jnp.dot(hot, table_ref[:, icols], preferred_element_type=jnp.float32)
            cosine = cosine.reshape(trans, TILE, PIECE)
            sine = sine.reshape(trans, TILE, PIECE)
            real = uv[mine, cols][None]
            imag = uv[mine, icols][None]
            shift_re = (real * cosine + imag * sine).astype(jnp.bfloat16)
            shift_im = (imag * cosine - real * sine).astype(jnp.bfloat16)
            scores += lax.dot_general(shift_re.reshape(trans * TILE, PIECE), views(cols), contract_last,
                                      preferred_element_type=jnp.float32)
            scores += lax.dot_general(shift_im.reshape(trans * TILE, PIECE), views(icols), contract_last,
                                      preferred_element_type=jnp.float32)
        full = scores.reshape(trans, TILE, ori) + pens[mine, :][None]
        highest = jnp.max(jnp.max(full, axis=0), axis=1, keepdims=True)
        total = jnp.zeros((TILE, ori), jnp.float32)
        moment_x = jnp.zeros((TILE, ori), jnp.float32)
        moment_y = jnp.zeros((TILE, ori), jnp.float32)
        for t in range(trans):
            term = jnp.exp(full[t] - highest)
            total += term
            moment_x += term * here[:, trans + 1 + t:trans + 2 + t]
            moment_y += term * here[:, 2 * trans + 1 + t:2 * trans + 2 + t]
        total = jnp.sum(total, axis=1, keepdims=True)
        moment_x = jnp.sum(moment_x, axis=1, keepdims=True)
        moment_y = jnp.sum(moment_y, axis=1, keepdims=True)
        lanes = lax.broadcasted_iota(jnp.int32, (TILE, 128), 1)
        stats[mine, :] = jnp.where(
            lanes == 0, highest,
            jnp.where(lanes == 1, total, jnp.where(lanes == 2, moment_x,
                                                   jnp.where(lanes == 3, moment_y, 0.0))))

    back = sum(
        lax.dot_general(part, pick, (((0,), (0,)), ((), ())), preferred_element_type=jnp.float32)
        for part in three(stats[...])
    )
    out_ref[0] = back[:8, :]


def class_stats(index, ids, label, table, wtab, dtab, penalty, metas, x_parts, q_parts, trans, slots):
    rows_all = sum(part.shape[0] for part in x_parts)
    rows_q, width = q_parts[0][0].shape[1:]
    ori = rows_q * len(q_parts)
    arrays = [array for array, _ in q_parts]
    spots = [spot for _, spot in q_parts]
    extra = [] if penalty is None else [penalty]
    vmem = pl.BlockSpec(memory_space=pltpu.VMEM)
    return pl.pallas_call(
        functools.partial(stats_kernel, trans, index, spots, len(x_parts), penalty is not None),
        out_shape=jax.ShapeDtypeStruct((1, 8, rows_all), jnp.float32),
        in_specs=[pl.BlockSpec(memory_space=pltpu.SMEM)]
        + [vmem] * (4 + len(extra) + 2 * len(x_parts) + len(arrays)),
        out_specs=vmem,
        scratch_shapes=[
            pltpu.VMEM((slots, width), jnp.float32),
            pltpu.VMEM((slots, ori), jnp.float32),
            pltpu.VMEM((slots, metas[0].shape[0]), jnp.float32),
            pltpu.VMEM((slots, 128), jnp.float32),
        ],
        compiler_params=pltpu.CompilerParams(vmem_limit_bytes=28 * 1024 * 1024),
        cost_estimate=pl.CostEstimate(
            flops=20 * slots * trans * width * (ori + 256),
            bytes_accessed=(rows_all + ori) * width * 2,
            transcendentals=0,
        ),
    )(ids, label, table, wtab, dtab, *extra, *metas, *x_parts, *arrays)


def on_device(particles, candidates, ctf_ids, offsets, ctf_table, sigma_sq, projections):
    pose_count = lax.axis_size("pose")
    dom_count = lax.axis_size("dom")
    pose = lax.axis_index("pose")
    local = projections.shape[0]
    class_total = local * pose_count
    rows, picks = candidates.shape
    trans = offsets.shape[2]
    pixels = sigma_sq.shape[0]
    capacity = 3 * rows * picks // class_total
    share = min(SHARE, pose_count)
    share_bits = [1 << b for b in range(share.bit_length() - 1)]
    families = pose_count // share

    def slots_for(blocks):
        return -(-min(blocks * capacity, blocks * rows) // TILE) * TILE

    dom_bits = [1 << b for b in range(dom_count.bit_length() - 1)][::-1]

    order = [0]
    for bit in share_bits[::-1]:
        order = order + [member ^ bit for member in order]

    near = len([member for member in order if bin(member).count("1") < 2])

    single = {bit: swap(particles, "pose", bit) for bit in share_bits[::-1]}
    own_pieces = [projections] + [swap(projections, "dom", bit) for bit in dom_bits]
    chunks = [projections[spot:spot + 1] for spot in range(local)]
    far = [[swap(chunks[0], "pose", family * share)] for family in range(1, families)]

    offsets, *_ = lax.optimization_barrier((offsets, own_pieces[-1]))
    offset_t = offsets.transpose(1, 2, 0).astype(jnp.float32)
    combo = (offset_t[0] + REACH) * (2 * REACH + 1) + (offset_t[1] + REACH)
    meta = jnp.concatenate(
        [combo, ctf_ids[None, :].astype(jnp.float32), offset_t[0], offset_t[1],
         candidates.T.astype(jnp.float32)], axis=0)
    meta = jnp.pad(meta, ((0, -meta.shape[0] % 16), (0, 0)), constant_values=-1.0).astype(jnp.bfloat16)
    metas = [swap(meta, "pose", member) if member else meta for member in order]

    single, own_pieces, chunks, far = lax.optimization_barrier((single, own_pieces, chunks, far))

    x_parts = []
    for member in order:
        bits = [bit for bit in share_bits if member & bit]
        part = single[bits[-1]] if bits else particles
        for bit in bits[:-1]:
            part = swap(part, "pose", bit)
        x_parts.append(part)
    for family in range(1, families):
        far[family - 1] += [swap(chunk, "pose", family * share) for chunk in chunks[1:]]
    own_pieces = own_pieces + [swap(own_pieces[1], "dom", bit) for bit in dom_bits[1:]]

    weight = ctf_table / sigma_sq[None, :]
    wtab = jnp.concatenate(split_three(weight), axis=0)
    dtab = jnp.concatenate(split_three(weight * ctf_table), axis=0)
    own_penalty = own_penalties(dtab, own_pieces)
    owner = pose ^ (jnp.arange(families, dtype=jnp.int32) * share)
    ids = (owner[:, None] * local + jnp.arange(local, dtype=jnp.int32)[None, :]).reshape(-1)
    table, label = phase_table(pixels)
    table, label = jnp.asarray(table), jnp.asarray(label)
    results = {}
    latest = []

    def one_class(index, members, penalty, first, last):
        turn = ids
        if latest:
            turn, results[latest[-1]] = lax.optimization_barrier((turn, results[latest[-1]]))
        results[(index, first)] = class_stats(
            index, turn, label, table, wtab, dtab, penalty, metas[first:last], x_parts[first:last], members,
            trans, slots_for(last - first))
        latest.append((index, first))

    own = [[(piece, spot) for piece in own_pieces] for spot in range(local)]
    for spot in range(local):
        one_class(spot, own[spot], own_penalty, 0, near)
    for family in range(1, families):
        for spot in range(local):
            pieces = [far[family - 1][spot]]
            for hop, bit in enumerate(dom_bits):
                if spot:
                    key = latest[-1] if hop else (spot, 0)
                    pieces[hop:], results[key] = lax.optimization_barrier((pieces[hop:], results[key]))
                pieces = pieces + [swap(member, "dom", bit) for member in pieces]
            one_class(family * local + spot, [(member, 0) for member in pieces], None, 0, share)
            if family == 1 and near < share:
                one_class(spot, own[spot], own_penalty, near, share)

    own = []
    for place, member in enumerate(order):
        block = []
        for spot in range(families * local):
            first = near if spot < local and place >= near else 0
            start = (place - first) * rows
            block.append(results[(spot, first)][:, :4, start:start + rows])
        block = jnp.concatenate(block, axis=0)
        block = swap(block, "pose", member) if member else block
        own += [(member, spot, block[spot]) for spot in range(families * local)]

    cand = candidates.T
    owner = cand // local
    beyond = (owner ^ pose) // share
    within = (owner ^ pose) % share
    position = beyond * local + cand % local
    picked = jnp.zeros((picks, 4, rows), jnp.float32)
    for member, spot, block in own:
        hit = (within == member) & (position == spot)
        picked = jnp.where(hit[:, None, :], block[None], picked)
    log_weight = picked[:, 0] + jnp.log(picked[:, 1])
    raw_weight = jnp.exp(log_weight - jnp.max(log_weight, axis=0, keepdims=True))
    class_prob = raw_weight / jnp.sum(raw_weight, axis=0, keepdims=True)
    mean_x = jnp.sum(class_prob * picked[:, 2] / picked[:, 1], axis=0)
    mean_y = jnp.sum(class_prob * picked[:, 3] / picked[:, 1], axis=0)
    return (class_prob.T, jnp.stack([mean_x, mean_y], axis=1))


def solution(mesh):
    in_specs = (
        P(("pose", "dom"), None),
        P(("pose", "dom"), None),
        P(("pose", "dom")),
        P(("pose", "dom"), None, None),
        P(),
        P(),
        P("pose", "dom", None),
    )
    out_specs = (P(("pose", "dom"), None), P(("pose", "dom"), None))
    return jax.shard_map(
        on_device, mesh=mesh, in_specs=in_specs, out_specs=out_specs, check_vma=False
    )
```

time: 127 us -> 126 us (level); the launches traced: 125 us -> 127 us
  starting transfers between devices: 20.8 us -> 32.9 us
  Pallas kernels: 49.2 us -> 40.6 us
  waiting for transfers between devices: 41.6 us -> 40.2 us
    ppermute x20, starting transfers between devices: 20.8 us -> 32.9 us  [swap(): lax.ppermute(values, axis, [(index, index ^ bit) for index in range(count)])]
    pallas_call x4 -> x6, Pallas kernels: 46.4 us -> 37.8 us  [class_stats(): pl.pallas_call(functools.partial(stats_kernel, trans, index, spots, len(x...]
    concatenate x2 -> x1, local copies, waits for them, and re-layouts: 0.45 us -> 2.29 us  [on_device(): jnp.concatenate([combo, ctf_ids[None, :].astype(jnp.float32), offset_t[0]...]
    ppermute x20, waiting for transfers between devices: 41.6 us -> 40.2 us  [swap(): lax.ppermute(values, axis, [(index, index ^ bit) for index in range(count)])]
  transfers between devices with their start and end apart: 20 -> 20, of which waited for: 7 -> 6; matrix products, arithmetic and copies ran while one was open for 8% -> 8% of each run, Pallas kernels for 33% -> 27%
where the time goes in v4:
time: 126 us; the launch traced here: 127 us
  Pallas kernels  40.6 us (32%)
  waiting for transfers between devices  40.2 us (32%)
  starting transfers between devices  32.9 us (26%)
  local copies, waits for them, and re-layouts  6.61 us (5%)
  other arithmetic  5.48 us (4%)
    ppermute x20, waiting for transfers between devices, swap(): lax.ppermute(values, axis, [(index, index ^ bit) for index in range(count)])  40.2 us
    pallas_call x6, Pallas kernels, class_stats(): pl.pallas_call(functools.partial(stats_kernel, trans, index, spots, len(x...  37.8 us
    ppermute x20, starting transfers between devices, swap(): lax.ppermute(values, axis, [(index, index ^ bit) for index in range(count)])  32.9 us
    pallas_call x1, Pallas kernels, own_penalties(): pl.pallas_call(functools.partial(penalty_kernel, len(pieces)), out_shape=...  2.81 us
  transfers between devices with their start and end apart: 20, of which 6 were waited for; matrix products, arithmetic and copies ran while one was open for 8% of the time, Pallas kernels for 27%

profile of v4, /device:TPU:0, one launch (start us, length us, event | category | flops | bytes accessed | tf_op | source)
XLA Modules:
  0.0 126.9 jit_solution(15272385087643329706)
XLA Ops:
  0.7 3.0 %collective-permute-start = (bf16[128,4096]{1,0:T(8,128)(2,1)}, bf16[128,4096]{1,0:T(8,128)(2,1)}, u32[]{:S(2)}, u32[]{:S(2)}) collective-permute-start(bf16[128,4096]{1,0:T(8,128)(2,1)} %refs_4_.7), channel_id=1, source_target_pairs={{0,4},{4,0},{8,12},{12,8},{16,20},{20,16},{24,28},{28,24},{1,5},{5... | collective-permute-start | bytes 3145736 | tf_op jit(solution)/shard_map/ppermute | solution.py:54
  3.7 1.6 %collective-permute-start.1 = (bf16[128,4096]{1,0:T(8,128)(2,1)}, bf16[128,4096]{1,0:T(8,128)(2,1)}, u32[]{:S(2)}, u32[]{:S(2)}) collective-permute-start(bf16[128,4096]{1,0:T(8,128)(2,1)} %refs_4_.7), channel_id=1, source_target_pairs={{0,8},{4,12},{8,0},{12,4},{16,24},{20,28},{24,16},{28,20},{1,9},{5... | collective-permute-start | bytes 3145736 | tf_op jit(solution)/shard_map/ppermute | solution.py:54
  5.3 1.5 %collective-permute-start.2 = (bf16[2,64,4096]{2,1,0:T(8,128)(2,1)}, bf16[2,64,4096]{2,1,0:T(8,128)(2,1)S(1)}, u32[]{:S(2)}, u32[]{:S(2)}) collective-permute-start(bf16[2,64,4096]{2,1,0:T(8,128)(2,1)} %refs_3_.1), channel_id=1, source_target_pairs={{0,2},{1,3},{2,0},{3,1},{4,6},{5,7},{6,4},{7,5},{8,10},{9,11},{10,... | collective-permute-start | bytes 3145736 | tf_op jit(solution)/shard_map/ppermute | solution.py:54
  6.8 0.0 collective-permute-start.3
  6.8 2.3 %fusion.31 = (bf16[1,64,4096]{2,1,0:T(8,128)(2,1)}, bf16[1,64,4096]{2,1,0:T(8,128)(2,1)}) fusion(bf16[2,64,4096]{2,1,0:T(8,128)(2,1)} %refs_3_.1), kind=kLoop, calls=%fused_computation.96 | loop fusion | bytes 2097152 | tf_op jit(solution)/shard_map/slice | solution.py:257
  9.1 2.6 %collective-permute-start.4 = (bf16[1,64,4096]{2,1,0:T(8,128)(2,1)}, bf16[1,64,4096]{2,1,0:T(8,128)(2,1)}, u32[]{:S(2)}, u32[]{:S(2)}) collective-permute-start(bf16[1,64,4096]{2,1,0:T(8,128)(2,1)} %get-tuple-element.69), channel_id=1, source_target_pairs={{0,16},{4,20},{8,24},{12,28},{16,0},{20,4},{24,8},{28,12},{1,17},{... | collective-permute-start | bytes 1572872 | tf_op jit(solution)/shard_map/ppermute | solution.py:54
  11.7 0.5 fusion.23
  12.2 0.6 fusion.25
  12.8 0.1 reduce-precision_convert_fusion.1
  12.9 0.6 fusion.14
  13.6 25.4 %collective-permute-done.4.refs_8_ = bf16[1,64,4096]{2,1,0:T(8,128)(2,1)} collective-permute-done((bf16[1,64,4096]{2,1,0:T(8,128)(2,1)}, bf16[1,64,4096]{2,1,0:T(8,128)(2,1)}, u32[]{:S(2)}, u32[]{:S(2)}) %collective-permute-start.4) | collective-permute-done | bytes 524320 | tf_op jit(solution)/shard_map/ppermute | solution.py:54
  39.0 0.9 collective-permute-done.1.refs_5_
  39.9 0.0 collective-permute-done.2.refs_1_.refs_8_.refs_4_
  39.9 0.0 collective-permute-done.3.refs_2_.refs_9_.refs_5_
  39.9 0.0 collective-permute-start.6
  39.9 0.5 convert_bitcast_fusion
  40.4 0.5 xor_multiply_fusion
  41.0 1.5 %collective-permute-start.12 = (bf16[1,64,4096]{2,1,0:T(8,128)(2,1)}, bf16[1,64,4096]{2,1,0:T(8,128)(2,1)}, u32[]{:S(2)}, u32[]{:S(2)}) collective-permute-start(bf16[1,64,4096]{2,1,0:T(8,128)(2,1)} %collective-permute-done.4.refs_8_), channel_id=1, source_target_pairs={{0,2},{1,3},{2,0},{3,1},{4,6},{5,7},{6,4},{7,5},{8,10},{9,11},{10,... | collective-permute-start | bytes 1572872 | tf_op jit(solution)/shard_map/ppermute | solution.py:54
  42.5 0.6 fusion.6
  43.1 2.3 %concatenate.21 = bf16[30,128]{1,0:T(8,128)(2,1)S(1)} concatenate(bf16[9,128]{1,0:T(8,128)(2,1)S(1)} %fusion.7, bf16[1,128]{1,0:T(2,128)(2,1)} %convert_bitcast_fusion, bf16[9,128]{1,0:T(8,128)(2,1)} %get-tuple-element.85, bf16[9,128]{1,0:T(8,128)(2,1)S(1)} %get-tuple-element.84, bf16[2,128]{1,0:T(2,128)(2,1)} %fusion.14), dimensions={0} | concatenate | bytes 15360 | tf_op jit(solution)/shard_map/concatenate | solution.py:263
  45.4 2.7 %collective-permute-start.7 = (bf16[32,128]{1,0:T(8,128)(2,1)S(1)}, bf16[32,128]{1,0:T(8,128)(2,1)S(1)}, u32[]{:S(2)}, u32[]{:S(2)}) collective-permute-start(bf16[32,128]{1,0:T(8,128)(2,1)S(1)} %pad.5.refs_1_.refs_0_), channel_id=1, source_target_pairs={{0,8},{4,12},{8,0},{12,4},{16,24},{20,28},{24,16},{28,20},{1,9},{5... | collective-permute-start | bytes 24584 | tf_op jit(solution)/shard_map/ppermute | solution.py:54
  48.1 0.5 collective-permute-start.8
  48.6 1.3 iota_add_fusion
  49.9 1.3 %add.52.ids_ref = s32[4]{0:T(128)} reshape(s32[2,2]{1,0:T(2,128)} %iota_add_fusion) | data formatting | bytes 32 | tf_op jit(solution)/shard_map/add | solution.py:287
  51.2 0.0 copy-start.5
  51.2 1.1 collective-permute-start.10
  52.3 2.8 %shard_map.104.refs_0_ = f32[2,16,256]{2,1,0:T(8,128)S(1)} custom-call(bf16[48,2048]{1,0:T(8,128)(2,1)S(1)} %pad_maximum_fusion.1.dtab_ref, bf16[2,64,4096]{2,1,0:T(8,128)(2,1)S(1)} %copy-done, bf16[2,64,4096]{2,1,0:T(8,128)(2,1)S(1)} %collective-permute-done.2.refs_1_.refs_8_.refs_4_, ...), custom_call_target="tpu_custom_call" | custom-call | tf_op jit(solution)/shard_map/pallas_call | solution.py:96
  55.1 0.0 copy-done.6
  55.1 1.9 %collective-permute-start.5 = (bf16[1,64,4096]{2,1,0:T(8,128)(2,1)S(1)}, bf16[1,64,4096]{2,1,0:T(8,128)(2,1)S(1)}, u32[]{:S(2)}, u32[]{:S(2)}) collective-permute-start(bf16[1,64,4096]{2,1,0:T(8,128)(2,1)S(1)} %copy-done.6), channel_id=1, source_target_pairs={{0,16},{4,20},{8,24},{12,28},{16,0},{20,4},{24,8},{28,12},{1,17},{... | collective-permute-start | bytes 1572872 | tf_op jit(solution)/shard_map/ppermute | solution.py:54
  57.0 0.7 collective-permute-start.11
  57.8 7.5 %shard_map.105 = f32[1,8,384]{2,1,0:T(8,128)S(1)} custom-call(s32[4]{0:T(128)S(1)} %copy-done.4, f32[1,256]{1,0:T(1,128)S(1)} %copy-done.5, bf16[256,4096]{1,0:T(8,128)(2,1)S(1)} %copy-done.3, bf16[48,2048]{1,0:T(8,128)(2,1)S(1)} %pad_maximum_fusion.wtab_ref, bf16[48,2048]{1,0:T(8,128)(2,1)S(1)} %pad_maximum_fusion.1.dtab_ref, ...), custom_call_target="tpu_custom_call" | custom-call | flops 60397977600 | bytes 5242880 | tf_op jit(solution)/shard_map/pallas_call | solution.py:209
  65.3 7.5 %shard_map.106 = f32[1,8,384]{2,1,0:T(8,128)S(1)} custom-call(s32[4]{0:T(128)S(1)} %copy-done.4, f32[1,256]{1,0:T(1,128)S(1)} %copy-done.5, bf16[256,4096]{1,0:T(8,128)(2,1)S(1)} %copy-done.3, bf16[48,2048]{1,0:T(8,128)(2,1)S(1)} %pad_maximum_fusion.wtab_ref, bf16[48,2048]{1,0:T(8,128)(2,1)S(1)} %pad_maximum_fusion.1.dtab_ref, ...), custom_call_target="tpu_custom_call" | custom-call | flops 60397977600 | bytes 5242880 | tf_op jit(solution)/shard_map/pallas_call | solution.py:209
  72.8 8.8 %collective-permute-done.5.refs_8_ = bf16[1,64,4096]{2,1,0:T(8,128)(2,1)S(1)} collective-permute-done((bf16[1,64,4096]{2,1,0:T(8,128)(2,1)S(1)}, bf16[1,64,4096]{2,1,0:T(8,128)(2,1)S(1)}, u32[]{:S(2)}, u32[]{:S(2)}) %collective-permute-start.5) | collective-permute-done | bytes 524320 | tf_op jit(solution)/shard_map/ppermute | solution.py:54
  81.7 0.5 collective-permute-start.9
  82.2 0.3 collective-permute-done.11.refs_7_.refs_2_
  82.5 8.5 %shard_map.107 = f32[1,8,512]{2,1,0:T(8,128)S(1)} custom-call(s32[4]{0:T(128)S(1)} %copy-done.4, f32[1,256]{1,0:T(1,128)S(1)} %copy-done.5, bf16[256,4096]{1,0:T(8,128)(2,1)S(1)} %copy-done.3, bf16[48,2048]{1,0:T(8,128)(2,1)S(1)} %pad_maximum_fusion.wtab_ref, bf16[48,2048]{1,0:T(8,128)(2,1)S(1)} %pad_maximum_fusion.1.dtab_ref, ...), custom_call_target="tpu_custom_call" | custom-call | flops 72477573120 | bytes 6291456 | tf_op jit(solution)/shard_map/pallas_call | solution.py:209
  91.1 4.1 %shard_map.108 = f32[1,8,128]{2,1,0:T(8,128)S(1)} custom-call(s32[4]{0:T(128)S(1)} %copy-done.4, f32[1,256]{1,0:T(1,128)S(1)} %copy-done.5, bf16[256,4096]{1,0:T(8,128)(2,1)S(1)} %copy-done.3, bf16[48,2048]{1,0:T(8,128)(2,1)S(1)} %pad_maximum_fusion.wtab_ref, bf16[48,2048]{1,0:T(8,128)(2,1)S(1)} %pad_maximum_fusion.1.dtab_ref, ...), custom_call_target="tpu_custom_call" | custom-call | flops 24159191040 | bytes 3145728 | tf_op jit(solution)/shard_map/pallas_call | solution.py:209
  95.2 0.0 collective-permute-done.9.refs_9_
  95.2 0.3 collective-permute-start.16
  95.6 1.6 %collective-permute-done.16.refs_11_ = bf16[1,64,4096]{2,1,0:T(8,128)(2,1)S(1)} collective-permute-done((bf16[1,64,4096]{2,1,0:T(8,128)(2,1)S(1)}, bf16[1,64,4096]{2,1,0:T(8,128)(2,1)S(1)}, u32[]{:S(2)}, u32[]{:S(2)}) %collective-permute-start.16) | collective-permute-done | bytes 524320 | tf_op jit(solution)/shard_map/ppermute | solution.py:54
  97.2 6.1 %shard_map.109 = f32[1,8,512]{2,1,0:T(8,128)S(1)} custom-call(s32[4]{0:T(128)S(1)} %copy-done.4, f32[1,256]{1,0:T(1,128)S(1)} %copy-done.5, bf16[256,4096]{1,0:T(8,128)(2,1)S(1)} %copy-done.3, bf16[48,2048]{1,0:T(8,128)(2,1)S(1)} %pad_maximum_fusion.wtab_ref, bf16[48,2048]{1,0:T(8,128)(2,1)S(1)} %pad_maximum_fusion.1.dtab_ref, ...), custom_call_target="tpu_custom_call" | custom-call | flops 72477573120 | bytes 6291456 | tf_op jit(solution)/shard_map/pallas_call | solution.py:209
  103.4 13.3 %collective-permute-start.19 = (f32[4,4,128]{2,1,0:T(4,128)S(1)}, f32[4,4,128]{2,1,0:T(4,128)S(1)}, u32[]{:S(2)}, u32[]{:S(2)}) collective-permute-start(f32[4,4,128]{2,1,0:T(4,128)S(1)} %pad_maximum_fusion.4), channel_id=1, source_target_pairs={{0,8},{4,12},{8,0},{12,4},{16,24},{20,28},{24,16},{28,20},{1,9},{5... | collective-permute-start | bytes 24584 | tf_op jit(solution)/shard_map/ppermute | solution.py:54
  116.8 0.1 collective-permute-start.18
  116.9 4.1 %shard_map.110 = f32[1,8,128]{2,1,0:T(8,128)S(1)} custom-call(s32[4]{0:T(128)S(1)} %copy-done.4, f32[1,256]{1,0:T(1,128)S(1)} %copy-done.5, bf16[256,4096]{1,0:T(8,128)(2,1)S(1)} %copy-done.3, bf16[48,2048]{1,0:T(8,128)(2,1)S(1)} %pad_maximum_fusion.wtab_ref, bf16[48,2048]{1,0:T(8,128)(2,1)S(1)} %pad_maximum_fusion.1.dtab_ref, ...), custom_call_target="tpu_custom_call" | custom-call | flops 24159191040 | bytes 3145728 | tf_op jit(solution)/shard_map/pallas_call | solution.py:209
  121.0 1.5 %collective-permute-start.17 = (f32[4,4,128]{2,1,0:T(4,128)S(1)}, f32[4,4,128]{2,1,0:T(4,128)S(1)}, u32[]{:S(2)}, u32[]{:S(2)}) collective-permute-start(f32[4,4,128]{2,1,0:T(4,128)S(1)} %pad_maximum_fusion.2), channel_id=1, source_target_pairs={{0,12},{4,8},{8,4},{12,0},{16,28},{20,24},{24,20},{28,16},{1,13},{... | collective-permute-start | bytes 24584 | tf_op jit(solution)/shard_map/ppermute | solution.py:54
  122.5 3.1 %collective-permute-done.17 = f32[4,4,128]{2,1,0:T(4,128)S(1)} collective-permute-done((f32[4,4,128]{2,1,0:T(4,128)S(1)}, f32[4,4,128]{2,1,0:T(4,128)S(1)}, u32[]{:S(2)}, u32[]{:S(2)}) %collective-permute-start.17) | collective-permute-done | bytes 8224 | tf_op jit(solution)/shard_map/ppermute | solution.py:54
  125.8 0.6 fusion.16
  126.4 0.6 pad_maximum_fusion.5
  (83 shorter events, 0.3 us)
Async XLA Ops:
  0.6 51.7 %copy-start = (bf16[2,64,4096]{2,1,0:T(8,128)(2,1)S(1)}, bf16[2,64,4096]{2,1,0:T(8,128)(2,1)}, u32[]{:S(2)}) copy-start(bf16[2,64,4096]{2,1,0:T(8,128)(2,1)} %refs_3_.1) | copy-start | bytes 3145732
  0.6 11.0 %copy-start.23 = (s32[128,2]{0,1:T(2,128)S(1)}, s32[128,2]{0,1:T(2,128)}, u32[]{:S(2)}) copy-start(s32[128,2]{0,1:T(2,128)} %param.10) | copy-start | bytes 3076
  0.7 12.2 %copy-start.7 = (f32[16,2048]{1,0:T(8,128)S(1)}, f32[16,2048]{1,0:T(8,128)}, u32[]{:S(2)}) copy-start(f32[16,2048]{1,0:T(8,128)} %param.13) | copy-start | bytes 393220
  0.7 12.2 %copy-start.9 = (f32[2048]{0:T(1024)S(1)}, f32[2048]{0:T(1024)}, u32[]{:S(2)}) copy-start(f32[2048]{0:T(1024)} %param.14) | copy-start | bytes 24580
  0.7 39.2 %copy-start.24 = (s32[128]{0:T(128)S(1)}, s32[128]{0:T(128)}, u32[]{:S(2)}) copy-start(s32[128]{0:T(128)} %param.11) | copy-start | bytes 1540
  0.7 41.8 %copy-start.8 = (s32[128,2,9]{0,1,2:T(2,128)S(1)}, s32[128,2,9]{0,1,2:T(2,128)}, u32[]{:S(2)}) copy-start(s32[128,2,9]{0,1,2:T(2,128)} %param.12) | copy-start | bytes 27652
  0.7 38.3 %collective-permute-start = (bf16[128,4096]{1,0:T(8,128)(2,1)}, bf16[128,4096]{1,0:T(8,128)(2,1)}, u32[]{:S(2)}, u32[]{:S(2)}) collective-permute-start(bf16[128,4096]{1,0:T(8,128)(2,1)} %refs_4_.7), channel_id=1, source_target_pairs={{0,4},{4,0},{8,12},{12,8},{16,20},{20,16},{24,28},{28,24},{1,5},{5... | collective-permute-start | bytes 3145736 | tf_op jit(solution)/shard_map/ppermute | solution.py:54
  3.7 36.2 %collective-permute-start.1 = (bf16[128,4096]{1,0:T(8,128)(2,1)}, bf16[128,4096]{1,0:T(8,128)(2,1)}, u32[]{:S(2)}, u32[]{:S(2)}) collective-permute-start(bf16[128,4096]{1,0:T(8,128)(2,1)} %refs_4_.7), channel_id=1, source_target_pairs={{0,8},{4,12},{8,0},{12,4},{16,24},{20,28},{24,16},{28,20},{1,9},{5... | collective-permute-start | bytes 3145736 | tf_op jit(solution)/shard_map/ppermute | solution.py:54
  5.3 34.6 %collective-permute-start.2 = (bf16[2,64,4096]{2,1,0:T(8,128)(2,1)}, bf16[2,64,4096]{2,1,0:T(8,128)(2,1)S(1)}, u32[]{:S(2)}, u32[]{:S(2)}) collective-permute-start(bf16[2,64,4096]{2,1,0:T(8,128)(2,1)} %refs_3_.1), channel_id=1, source_target_pairs={{0,2},{1,3},{2,0},{3,1},{4,6},{5,7},{6,4},{7,5},{8,10},{9,11},{10,... | collective-permute-start | bytes 3145736 | tf_op jit(solution)/shard_map/ppermute | solution.py:54
  6.8 33.1 %collective-permute-start.3 = (bf16[2,64,4096]{2,1,0:T(8,128)(2,1)}, bf16[2,64,4096]{2,1,0:T(8,128)(2,1)S(1)}, u32[]{:S(2)}, u32[]{:S(2)}) collective-permute-start(bf16[2,64,4096]{2,1,0:T(8,128)(2,1)} %refs_3_.1), channel_id=1, source_target_pairs={{0,1},{1,0},{2,3},{3,2},{4,5},{5,4},{6,7},{7,6},{8,9},{9,8},{10,11... | collective-permute-start | bytes 3145736 | tf_op jit(solution)/shard_map/ppermute | solution.py:54
  9.1 29.9 %collective-permute-start.4 = (bf16[1,64,4096]{2,1,0:T(8,128)(2,1)}, bf16[1,64,4096]{2,1,0:T(8,128)(2,1)}, u32[]{:S(2)}, u32[]{:S(2)}) collective-permute-start(bf16[1,64,4096]{2,1,0:T(8,128)(2,1)} %get-tuple-element.69), channel_id=1, source_target_pairs={{0,16},{4,20},{8,24},{12,28},{16,0},{20,4},{24,8},{28,12},{1,17},{... | collective-permute-start | bytes 1572872 | tf_op jit(solution)/shard_map/ppermute | solution.py:54
  39.9 12.4 %collective-permute-start.6 = (bf16[2,64,4096]{2,1,0:T(8,128)(2,1)S(1)}, bf16[2,64,4096]{2,1,0:T(8,128)(2,1)}, u32[]{:S(2)}, u32[]{:S(2)}) collective-permute-start(bf16[2,64,4096]{2,1,0:T(8,128)(2,1)S(1)} %collective-permute-done.2.refs_1_.refs_8_.refs_4_), channel_id=1, source_target_pairs={{0,1},{1,0},{2,3},{3,2},{4,5},{5,4},{6,7},{7,6},{8,9},{9,8},{10,11... | collective-permute-start | bytes 3145736 | tf_op jit(solution)/shard_map/ppermute | solution.py:54
  41.0 16.8 %collective-permute-start.12 = (bf16[1,64,4096]{2,1,0:T(8,128)(2,1)}, bf16[1,64,4096]{2,1,0:T(8,128)(2,1)}, u32[]{:S(2)}, u32[]{:S(2)}) collective-permute-start(bf16[1,64,4096]{2,1,0:T(8,128)(2,1)} %collective-permute-done.4.refs_8_), channel_id=1, source_target_pairs={{0,2},{1,3},{2,0},{3,1},{4,6},{5,7},{6,4},{7,5},{8,10},{9,11},{10,... | collective-permute-start | bytes 1572872 | tf_op jit(solution)/shard_map/ppermute | solution.py:54
  45.4 9.7 %collective-permute-start.7 = (bf16[32,128]{1,0:T(8,128)(2,1)S(1)}, bf16[32,128]{1,0:T(8,128)(2,1)S(1)}, u32[]{:S(2)}, u32[]{:S(2)}) collective-permute-start(bf16[32,128]{1,0:T(8,128)(2,1)S(1)} %pad.5.refs_1_.refs_0_), channel_id=1, source_target_pairs={{0,8},{4,12},{8,0},{12,4},{16,24},{20,28},{24,16},{28,20},{1,9},{5... | collective-permute-start | bytes 24584 | tf_op jit(solution)/shard_map/ppermute | solution.py:54
  48.1 8.9 %collective-permute-start.8 = (bf16[32,128]{1,0:T(8,128)(2,1)S(1)}, bf16[32,128]{1,0:T(8,128)(2,1)}, u32[]{:S(2)}, u32[]{:S(2)}) collective-permute-start(bf16[32,128]{1,0:T(8,128)(2,1)S(1)} %pad.5.refs_1_.refs_0_), channel_id=1, source_target_pairs={{0,4},{4,0},{8,12},{12,8},{16,20},{20,16},{24,28},{28,24},{1,5},{5... | collective-permute-start | bytes 24584 | tf_op jit(solution)/shard_map/ppermute | solution.py:54
  51.2 4.0 %copy-start.6 = (bf16[1,64,4096]{2,1,0:T(8,128)(2,1)S(1)}, bf16[1,64,4096]{2,1,0:T(8,128)(2,1)}, u32[]{:S(2)}) copy-start(bf16[1,64,4096]{2,1,0:T(8,128)(2,1)} %get-tuple-element.24) | copy-start | bytes 1572868
  51.2 6.6 %copy-start.2 = (bf16[128,4096]{1,0:T(8,128)(2,1)S(1)}, bf16[128,4096]{1,0:T(8,128)(2,1)}, u32[]{:S(2)}) copy-start(bf16[128,4096]{1,0:T(8,128)(2,1)} %refs_4_.7) | copy-start | bytes 3145732
  51.2 6.6 %copy-start.3 = (bf16[256,4096]{1,0:T(8,128)(2,1)S(1)}, bf16[256,4096]{1,0:T(8,128)(2,1)}, u32[]{:S(2)}) copy-start(bf16[256,4096]{1,0:T(8,128)(2,1)} %constant.73.clone.table_ref) | copy-start | bytes 6291460
  51.2 6.6 %copy-start.4 = (s32[4]{0:T(128)S(1)}, s32[4]{0:T(128)}, u32[]{:S(2)}) copy-start(s32[4]{0:T(128)} %add.52.ids_ref) | copy-start | bytes 52
  51.2 6.6 %copy-start.5 = (f32[1,256]{1,0:T(1,128)S(1)}, f32[1,256]{1,0:T(1,128)}, u32[]{:S(2)}) copy-start(f32[1,256]{1,0:T(1,128)} %constant.74.clone.label_ref) | copy-start | bytes 3076
  51.2 31.0 %collective-permute-start.10 = (bf16[32,128]{1,0:T(8,128)(2,1)S(1)}, bf16[32,128]{1,0:T(8,128)(2,1)S(1)}, u32[]{:S(2)}, u32[]{:S(2)}) collective-permute-start(bf16[32,128]{1,0:T(8,128)(2,1)S(1)} %pad.5.refs_1_.refs_0_), channel_id=1, source_target_pairs={{0,12},{4,8},{8,4},{12,0},{16,28},{20,24},{24,20},{28,16},{1,13},{... | collective-permute-start | bytes 24584 | tf_op jit(solution)/shard_map/ppermute | solution.py:54
  52.3 29.9 %collective-permute-start.13 = (bf16[1,64,4096]{2,1,0:T(8,128)(2,1)}, bf16[1,64,4096]{2,1,0:T(8,128)(2,1)S(1)}, u32[]{:S(2)}, u32[]{:S(2)}) collective-permute-start(bf16[1,64,4096]{2,1,0:T(8,128)(2,1)} %collective-permute-done.4.refs_8_), channel_id=1, source_target_pairs={{0,1},{1,0},{2,3},{3,2},{4,5},{5,4},{6,7},{7,6},{8,9},{9,8},{10,11... | collective-permute-start | bytes 1572872 | tf_op jit(solution)/shard_map/ppermute | solution.py:54
  55.1 26.5 %collective-permute-start.5 = (bf16[1,64,4096]{2,1,0:T(8,128)(2,1)S(1)}, bf16[1,64,4096]{2,1,0:T(8,128)(2,1)S(1)}, u32[]{:S(2)}, u32[]{:S(2)}) collective-permute-start(bf16[1,64,4096]{2,1,0:T(8,128)(2,1)S(1)} %copy-done.6), channel_id=1, source_target_pairs={{0,16},{4,20},{8,24},{12,28},{16,0},{20,4},{24,8},{28,12},{1,17},{... | collective-permute-start | bytes 1572872 | tf_op jit(solution)/shard_map/ppermute | solution.py:54
  57.0 25.5 %collective-permute-start.11 = (bf16[128,4096]{1,0:T(8,128)(2,1)}, bf16[128,4096]{1,0:T(8,128)(2,1)S(1)}, u32[]{:S(2)}, u32[]{:S(2)}) collective-permute-start(bf16[128,4096]{1,0:T(8,128)(2,1)} %collective-permute-done.1.refs_5_), channel_id=1, source_target_pairs={{0,4},{4,0},{8,12},{12,8},{16,20},{20,16},{24,28},{28,24},{1,5},{5... | collective-permute-start | bytes 3145736 | tf_op jit(solution)/shard_map/ppermute | solution.py:54
  57.8 24.8 %collective-permute-start.14 = (bf16[1,64,4096]{2,1,0:T(8,128)(2,1)}, bf16[1,64,4096]{2,1,0:T(8,128)(2,1)S(1)}, u32[]{:S(2)}, u32[]{:S(2)}) collective-permute-start(bf16[1,64,4096]{2,1,0:T(8,128)(2,1)} %collective-permute-done.12.refs_9_), channel_id=1, source_target_pairs={{0,1},{1,0},{2,3},{3,2},{4,5},{5,4},{6,7},{7,6},{8,9},{9,8},{10,11... | collective-permute-start | bytes 1572872 | tf_op jit(solution)/shard_map/ppermute | solution.py:54
  81.7 13.5 %collective-permute-start.9 = (bf16[1,64,4096]{2,1,0:T(8,128)(2,1)S(1)}, bf16[1,64,4096]{2,1,0:T(8,128)(2,1)S(1)}, u32[]{:S(2)}, u32[]{:S(2)}) collective-permute-start(bf16[1,64,4096]{2,1,0:T(8,128)(2,1)S(1)} %collective-permute-done.5.refs_8_), channel_id=1, source_target_pairs={{0,2},{1,3},{2,0},{3,1},{4,6},{5,7},{6,4},{7,5},{8,10},{9,11},{10,... | collective-permute-start | bytes 1572872 | tf_op jit(solution)/shard_map/ppermute | solution.py:54
  82.2 13.4 %collective-permute-start.15 = (bf16[1,64,4096]{2,1,0:T(8,128)(2,1)S(1)}, bf16[1,64,4096]{2,1,0:T(8,128)(2,1)S(1)}, u32[]{:S(2)}, u32[]{:S(2)}) collective-permute-start(bf16[1,64,4096]{2,1,0:T(8,128)(2,1)S(1)} %collective-permute-done.5.refs_8_), channel_id=1, source_target_pairs={{0,1},{1,0},{2,3},{3,2},{4,5},{5,4},{6,7},{7,6},{8,9},{9,8},{10,11... | collective-permute-start | bytes 1572872 | tf_op jit(solution)/shard_map/ppermute | solution.py:54
  91.1 4.4 %copy-start.17 = (pred[2,128]{1,0:T(4,128)(4,1)S(1)}, pred[2,128]{1,0:T(4,128)(4,1)}, u32[]{:S(2)}) copy-start(pred[2,128]{1,0:T(4,128)(4,1)} %get-tuple-element.57) | copy-start | bytes 772
  91.1 4.4 %copy-start.18 = (pred[2,128]{1,0:T(4,128)(4,1)S(1)}, pred[2,128]{1,0:T(4,128)(4,1)}, u32[]{:S(2)}) copy-start(pred[2,128]{1,0:T(4,128)(4,1)} %get-tuple-element.109) | copy-start | bytes 772
  91.1 4.4 %copy-start.19 = (pred[2,128]{1,0:T(4,128)(4,1)S(1)}, pred[2,128]{1,0:T(4,128)(4,1)}, u32[]{:S(2)}) copy-start(pred[2,128]{1,0:T(4,128)(4,1)} %get-tuple-element.111) | copy-start | bytes 772
  91.1 4.4 %copy-start.20 = (pred[2,128]{1,0:T(4,128)(4,1)S(1)}, pred[2,128]{1,0:T(4,128)(4,1)}, u32[]{:S(2)}) copy-start(pred[2,128]{1,0:T(4,128)(4,1)} %get-tuple-element.122) | copy-start | bytes 772
  91.1 4.4 %copy-start.21 = (pred[2,128]{1,0:T(4,128)(4,1)S(1)}, pred[2,128]{1,0:T(4,128)(4,1)}, u32[]{:S(2)}) copy-start(pred[2,128]{1,0:T(4,128)(4,1)} %get-tuple-element.124) | copy-start | bytes 772
  91.1 4.4 %copy-start.22 = (pred[2,128]{1,0:T(4,128)(4,1)S(1)}, pred[2,128]{1,0:T(4,128)(4,1)}, u32[]{:S(2)}) copy-start(pred[2,128]{1,0:T(4,128)(4,1)} %get-tuple-element.126) | copy-start | bytes 772
  95.2 8.1 %copy-start.1 = (f32[1,8,128]{2,1,0:T(8,128)}, f32[1,8,128]{2,1,0:T(8,128)S(1)}, u32[]{:S(2)}) copy-start(f32[1,8,128]{2,1,0:T(8,128)S(1)} %shard_map.108) | copy-start | bytes 12292
  95.2 2.0 %collective-permute-start.16 = (bf16[1,64,4096]{2,1,0:T(8,128)(2,1)S(1)}, bf16[1,64,4096]{2,1,0:T(8,128)(2,1)S(1)}, u32[]{:S(2)}, u32[]{:S(2)}) collective-permute-start(bf16[1,64,4096]{2,1,0:T(8,128)(2,1)S(1)} %collective-permute-done.9.refs_9_), channel_id=1, source_target_pairs={{0,1},{1,0},{2,3},{3,2},{4,5},{5,4},{6,7},{7,6},{8,9},{9,8},{10,11... | collective-permute-start | bytes 1572872 | tf_op jit(solution)/shard_map/ppermute | solution.py:54
  103.4 19.1 %collective-permute-start.19 = (f32[4,4,128]{2,1,0:T(4,128)S(1)}, f32[4,4,128]{2,1,0:T(4,128)S(1)}, u32[]{:S(2)}, u32[]{:S(2)}) collective-permute-start(f32[4,4,128]{2,1,0:T(4,128)S(1)} %pad_maximum_fusion.4), channel_id=1, source_target_pairs={{0,8},{4,12},{8,0},{12,4},{16,24},{20,28},{24,16},{28,20},{1,9},{5... | collective-permute-start | bytes 24584 | tf_op jit(solution)/shard_map/ppermute | solution.py:54
  116.7 4.2 %slice-start = ((f32[1,8,128]{2,1,0:T(8,128)}), f32[1,4,128]{2,1,0:T(4,128)S(1)}, s32[]{:S(2)}) async-start(f32[1,8,128]{2,1,0:T(8,128)} %copy-done.1), calls=%async_computation | async-start | bytes 4096 | tf_op jit(solution)/shard_map/slice | solution.py:323
  116.7 8.9 %copy-start.10 = (pred[2,128]{1,0:T(4,128)(4,1)S(1)}, pred[2,128]{1,0:T(4,128)(4,1)}, u32[]{:S(2)}) copy-start(pred[2,128]{1,0:T(4,128)(4,1)} %get-tuple-element.51) | copy-start | bytes 772
  116.7 8.9 %copy-start.11 = (pred[2,128]{1,0:T(4,128)(4,1)S(1)}, pred[2,128]{1,0:T(4,128)(4,1)}, u32[]{:S(2)}) copy-start(pred[2,128]{1,0:T(4,128)(4,1)} %get-tuple-element.56) | copy-start | bytes 772
  116.7 8.9 %copy-start.12 = (pred[2,128]{1,0:T(4,128)(4,1)S(1)}, pred[2,128]{1,0:T(4,128)(4,1)}, u32[]{:S(2)}) copy-start(pred[2,128]{1,0:T(4,128)(4,1)} %get-tuple-element.108) | copy-start | bytes 772
  116.7 8.9 %copy-start.13 = (pred[2,128]{1,0:T(4,128)(4,1)S(1)}, pred[2,128]{1,0:T(4,128)(4,1)}, u32[]{:S(2)}) copy-start(pred[2,128]{1,0:T(4,128)(4,1)} %get-tuple-element.110) | copy-start | bytes 772
  116.8 8.9 %copy-start.14 = (pred[2,128]{1,0:T(4,128)(4,1)S(1)}, pred[2,128]{1,0:T(4,128)(4,1)}, u32[]{:S(2)}) copy-start(pred[2,128]{1,0:T(4,128)(4,1)} %get-tuple-element.121) | copy-start | bytes 772
  116.8 8.9 %copy-start.15 = (pred[2,128]{1,0:T(4,128)(4,1)S(1)}, pred[2,128]{1,0:T(4,128)(4,1)}, u32[]{:S(2)}) copy-start(pred[2,128]{1,0:T(4,128)(4,1)} %get-tuple-element.123) | copy-start | bytes 772
  116.8 8.9 %copy-start.16 = (pred[2,128]{1,0:T(4,128)(4,1)S(1)}, pred[2,128]{1,0:T(4,128)(4,1)}, u32[]{:S(2)}) copy-start(pred[2,128]{1,0:T(4,128)(4,1)} %get-tuple-element.125) | copy-start | bytes 772
  116.8 5.7 %collective-permute-start.18 = (f32[4,4,128]{2,1,0:T(4,128)S(1)}, f32[4,4,128]{2,1,0:T(4,128)S(1)}, u32[]{:S(2)}, u32[]{:S(2)}) collective-permute-start(f32[4,4,128]{2,1,0:T(4,128)S(1)} %pad_maximum_fusion.3), channel_id=1, source_target_pairs={{0,4},{4,0},{8,12},{12,8},{16,20},{20,16},{24,28},{28,24},{1,5},{5... | collective-permute-start | bytes 24584 | tf_op jit(solution)/shard_map/ppermute | solution.py:54
  121.0 4.6 %collective-permute-start.17 = (f32[4,4,128]{2,1,0:T(4,128)S(1)}, f32[4,4,128]{2,1,0:T(4,128)S(1)}, u32[]{:S(2)}, u32[]{:S(2)}) collective-permute-start(f32[4,4,128]{2,1,0:T(4,128)S(1)} %pad_maximum_fusion.2), channel_id=1, source_target_pairs={{0,12},{4,8},{8,4},{12,0},{16,28},{20,24},{24,20},{28,16},{1,13},{... | collective-permute-start | bytes 24584 | tf_op jit(solution)/shard_map/ppermute | solution.py:54

commit v5 on v4

--- a/solution.py
+++ b/solution.py
@@ -106,11 +106,12 @@
                  dtab_ref, *refs):
     if have_penalty:
         penalty_ref, refs = refs[0], refs[1:]
-    meta_refs, refs = refs[:share], refs[share:]
     x_refs, refs = refs[:share], refs[share:]
     q_refs = refs[:len(spots)]
     out_ref, uv, pens, info, stats = refs[len(spots):]
     rows_all = out_ref.shape[2]
+    rows = rows_all // share
+    features = info.shape[1]
     slots = uv.shape[0]
     pixels = uv.shape[1] // 2
     ori = pens.shape[1]
@@ -118,10 +119,14 @@
     views = views_of(q_refs, spots)
 
     def particles(cols):
-        return jnp.concatenate([member[:, cols] for member in x_refs], axis=0)
-
-    meta = jnp.concatenate([member[...] for member in meta_refs], axis=1)
-    named = meta[3 * trans + 1:, :].astype(jnp.float32)
+        return jnp.concatenate([member[:rows, cols] for member in x_refs], axis=0)
+
+    below = [member[rows:rows + 8, :features // 8 * rows].astype(jnp.float32) for member in x_refs]
+    meta = jnp.concatenate(
+        [jnp.concatenate([block[:, at * rows:(at + 1) * rows] for at in range(features // 8)], axis=0)
+         for block in below], axis=1)
+    named = meta[3 * trans + 1:, :]
+    meta = meta.astype(jnp.bfloat16)
     wanted = ids_ref[index].astype(jnp.float32)
     names = jnp.max(jnp.where(named == wanted, 1.0, 0.0), axis=0, keepdims=True)
     before = lax.broadcasted_iota(jnp.int32, (rows_all, rows_all), 0)
@@ -198,8 +203,8 @@
     out_ref[0] = back[:8, :]
 
 
-def class_stats(index, ids, label, table, wtab, dtab, penalty, metas, x_parts, q_parts, trans, slots):
-    rows_all = sum(part.shape[0] for part in x_parts)
+def class_stats(index, ids, label, table, wtab, dtab, penalty, x_parts, q_parts, trans, slots, features):
+    rows_all = sum(part.shape[0] - 8 for part in x_parts)
     rows_q, width = q_parts[0][0].shape[1:]
     ori = rows_q * len(q_parts)
     arrays = [array for array, _ in q_parts]
@@ -210,12 +215,12 @@
         functools.partial(stats_kernel, trans, index, spots, len(x_parts), penalty is not None),
         out_shape=jax.ShapeDtypeStruct((1, 8, rows_all), jnp.float32),
         in_specs=[pl.BlockSpec(memory_space=pltpu.SMEM)]
-        + [vmem] * (4 + len(extra) + 2 * len(x_parts) + len(arrays)),
+        + [vmem] * (4 + len(extra) + len(x_parts) + len(arrays)),
         out_specs=vmem,
         scratch_shapes=[
             pltpu.VMEM((slots, width), jnp.float32),
             pltpu.VMEM((slots, ori), jnp.float32),
-            pltpu.VMEM((slots, metas[0].shape[0]), jnp.float32),
+            pltpu.VMEM((slots, features), jnp.float32),
             pltpu.VMEM((slots, 128), jnp.float32),
         ],
         compiler_params=pltpu.CompilerParams(vmem_limit_bytes=28 * 1024 * 1024),
@@ -224,7 +229,7 @@
             bytes_accessed=(rows_all + ori) * width * 2,
             transcendentals=0,
         ),
-    )(ids, label, table, wtab, dtab, *extra, *metas, *x_parts, *arrays)
+    )(ids, label, table, wtab, dtab, *extra, *x_parts, *arrays)
 
 
 def on_device(particles, candidates, ctf_ids, offsets, ctf_table, sigma_sq, projections):
@@ -252,39 +257,41 @@
 
     near = len([member for member in order if bin(member).count("1") < 2])
 
-    single = {bit: swap(particles, "pose", bit) for bit in share_bits[::-1]}
-    own_pieces = [projections] + [swap(projections, "dom", bit) for bit in dom_bits]
-    chunks = [projections[spot:spot + 1] for spot in range(local)]
-    far = [[swap(chunks[0], "pose", family * share)] for family in range(1, families)]
-
-    offsets, *_ = lax.optimization_barrier((offsets, own_pieces[-1]))
     offset_t = offsets.transpose(1, 2, 0).astype(jnp.float32)
     combo = (offset_t[0] + REACH) * (2 * REACH + 1) + (offset_t[1] + REACH)
     meta = jnp.concatenate(
         [combo, ctf_ids[None, :].astype(jnp.float32), offset_t[0], offset_t[1],
          candidates.T.astype(jnp.float32)], axis=0)
-    meta = jnp.pad(meta, ((0, -meta.shape[0] % 16), (0, 0)), constant_values=-1.0).astype(jnp.bfloat16)
-    metas = [swap(meta, "pose", member) if member else meta for member in order]
-
-    single, own_pieces, chunks, far = lax.optimization_barrier((single, own_pieces, chunks, far))
+    features = -(-meta.shape[0] // 16) * 16
+    meta = jnp.pad(meta, ((0, features - meta.shape[0]), (0, 0)), constant_values=-1.0)
+    meta = meta.reshape(features // 8, 8, rows).transpose(1, 0, 2).reshape(8, -1).astype(jnp.bfloat16)
+    meta = jnp.pad(meta, ((0, 0), (0, particles.shape[1] - meta.shape[1])))
+    block = jnp.concatenate([particles, meta], axis=0)
+
+    single = {bit: swap(block, "pose", bit) for bit in share_bits[::-1]}
+    own_pieces = [projections] + [swap(projections, "dom", bit) for bit in dom_bits]
+    own_pieces = own_pieces + [swap(own_pieces[1], "dom", bit) for bit in dom_bits[1:]]
+    chunks = [projections[spot:spot + 1] for spot in range(local)]
+    far = [[swap(chunks[0], "pose", family * share)] for family in range(1, families)]
+    weight = ctf_table / sigma_sq[None, :]
+    wtab = jnp.concatenate(split_three(weight), axis=0)
+    dtab = jnp.concatenate(split_three(weight * ctf_table), axis=0)
+    own_penalty = own_penalties(dtab, own_pieces)
+
+    owner = pose ^ (jnp.arange(families, dtype=jnp.int32) * share)
+    ids = (owner[:, None] * local + jnp.arange(local, dtype=jnp.int32)[None, :]).reshape(-1)
+    single, chunks, far, own_penalty, ids = lax.optimization_barrier(
+        (single, chunks, far, own_penalty, ids))
 
     x_parts = []
     for member in order:
         bits = [bit for bit in share_bits if member & bit]
-        part = single[bits[-1]] if bits else particles
+        part = single[bits[-1]] if bits else block
         for bit in bits[:-1]:
             part = swap(part, "pose", bit)
         x_parts.append(part)
     for family in range(1, families):
         far[family - 1] += [swap(chunk, "pose", family * share) for chunk in chunks[1:]]
-    own_pieces = own_pieces + [swap(own_pieces[1], "dom", bit) for bit in dom_bits[1:]]
-
-    weight = ctf_table / sigma_sq[None, :]
-    wtab = jnp.concatenate(split_three(weight), axis=0)
-    dtab = jnp.concatenate(split_three(weight * ctf_table), axis=0)
-    own_penalty = own_penalties(dtab, own_pieces)
-    owner = pose ^ (jnp.arange(families, dtype=jnp.int32) * share)
-    ids = (owner[:, None] * local + jnp.arange(local, dtype=jnp.int32)[None, :]).reshape(-1)
     table, label = phase_table(pixels)
     table, label = jnp.asarray(table), jnp.asarray(label)
     results = {}
@@ -295,8 +302,8 @@
         if latest:
             turn, results[latest[-1]] = lax.optimization_barrier((turn, results[latest[-1]]))
         results[(index, first)] = class_stats(
-            index, turn, label, table, wtab, dtab, penalty, metas[first:last], x_parts[first:last], members,
-            trans, slots_for(last - first))
+            index, turn, label, table, wtab, dtab, penalty, x_parts[first:last], members, trans,
+            slots_for(last - first), features)
         latest.append((index, first))
 
     own = [[(piece, spot) for piece in own_pieces] for spot in range(local)]
@@ -306,14 +313,16 @@
         for spot in range(local):
             pieces = [far[family - 1][spot]]
             for hop, bit in enumerate(dom_bits):
-                if spot:
-                    key = latest[-1] if hop else (spot, 0)
+                if spot or hop:
+                    key = (family * local + spot - 1, 0) if hop and spot else (local - 1, 0)
                     pieces[hop:], results[key] = lax.optimization_barrier((pieces[hop:], results[key]))
                 pieces = pieces + [swap(member, "dom", bit) for member in pieces]
             one_class(family * local + spot, [(member, 0) for member in pieces], None, 0, share)
-            if family == 1 and near < share:
-                one_class(spot, own[spot], own_penalty, near, share)
-
+            if family == 1 and spot == 0 and near < share:
+                for place in range(local):
+                    one_class(place, own[place], own_penalty, near, share)
+
+    results = dict(zip(results, lax.optimization_barrier(tuple(results.values()))))
     own = []
     for place, member in enumerate(order):
         block = []

time: 126 us -> 126 us (level); the launches traced: 127 us -> 125 us
  starting transfers between devices: 32.9 us -> 25.5 us
  local copies, waits for them, and re-layouts: 6.61 us -> 1.63 us
  Pallas kernels: 40.6 us -> 44.4 us
  other arithmetic: 5.48 us -> 9.02 us
  waiting for transfers between devices: 40.2 us -> 43.6 us
    ppermute x20 -> x17, starting transfers between devices: 32.9 us -> 25.5 us  [swap(): lax.ppermute(values, axis, [(index, index ^ bit) for index in range(count)])]
    ppermute x20 -> x17, waiting for transfers between devices: 40.2 us -> 43.6 us  [swap(): lax.ppermute(values, axis, [(index, index ^ bit) for index in range(count)])]
    pallas_call x6, Pallas kernels: 37.8 us -> 41.1 us  [class_stats(): pl.pallas_call(functools.partial(stats_kernel, trans, index, spots, len(x...]
    concatenate x1, local copies, waits for them, and re-layouts: 2.29 us -> 0.32 us  [on_device(): jnp.concatenate([combo, ctf_ids[None, :].astype(jnp.float32), offset_t[0]...]
    convert_element_type x1, other arithmetic: 0.07 us -> 1.59 us  [split_three(): parts.append(part.astype(jnp.bfloat16))]
    concatenate x0 -> x1, other arithmetic: none -> 1.32 us  [on_device(): block = jnp.concatenate([particles, meta], axis=0)]
  transfers between devices with their start and end apart: 20 -> 17, of which waited for: 6 -> 8; matrix products, arithmetic and copies ran while one was open for 8% -> 7% of each run, Pallas kernels for 27% -> 29%
where the time goes in v5:
time: 126 us; the launch traced here: 125 us
  Pallas kernels  44.4 us (35%)
  waiting for transfers between devices  43.6 us (35%)
  starting transfers between devices  25.5 us (20%)
  other arithmetic  9.02 us (7%)
  local copies, waits for them, and re-layouts  1.63 us (1%)
    ppermute x17, waiting for transfers between devices, swap(): lax.ppermute(values, axis, [(index, index ^ bit) for index in range(count)])  43.6 us
    pallas_call x6, Pallas kernels, class_stats(): pl.pallas_call(functools.partial(stats_kernel, trans, index, spots, len(x...  41.1 us
    ppermute x17, starting transfers between devices, swap(): lax.ppermute(values, axis, [(index, index ^ bit) for index in range(count)])  25.5 us
    pallas_call x1, Pallas kernels, own_penalties(): pl.pallas_call(functools.partial(penalty_kernel, len(pieces)), out_shape=...  3.23 us
  transfers between devices with their start and end apart: 17, of which 8 were waited for; matrix products, arithmetic and copies ran while one was open for 7% of the time, Pallas kernels for 29%

profile of v5, /device:TPU:0, one launch (start us, length us, event | category | flops | bytes accessed | tf_op | source)
XLA Modules:
  0.0 125.3 jit_solution(16202300091979661218)
XLA Ops:
  0.6 3.0 %collective-permute-start.3 = (bf16[2,64,4096]{2,1,0:T(8,128)(2,1)}, bf16[2,64,4096]{2,1,0:T(8,128)(2,1)S(1)}, u32[]{:S(2)}, u32[]{:S(2)}) collective-permute-start(bf16[2,64,4096]{2,1,0:T(8,128)(2,1)} %refs_2_.3), channel_id=1, source_target_pairs={{0,2},{1,3},{2,0},{3,1},{4,6},{5,7},{6,4},{7,5},{8,10},{9,11},{10,... | collective-permute-start | bytes 3145736 | tf_op jit(solution)/shard_map/ppermute | solution.py:54
  3.6 0.7 fusion.6
  4.4 0.7 convert_bitcast_fusion
  5.1 0.7 fusion.16
  5.8 0.3 concatenate.22
  6.1 1.3 %fusion.1.refs_1_.refs_0_ = bf16[136,4096]{1,0:T(8,128)(2,1)S(1)} fusion(bf16[8,512]{1,0:T(8,128)(2,1)S(1)} %pad_bitcast_fusion, bf16[128,4096]{1,0:T(8,128)(2,1)} %param.9), kind=kLoop, calls=%fused_computation.2 | loop fusion | flops 3342336 | bytes 2170880 | tf_op jit(solution)/shard_map/concatenate | solution.py:269
  7.4 0.0 copy-start.4
  7.5 1.6 %collective-permute-start = (bf16[136,4096]{1,0:T(8,128)(2,1)S(1)}, bf16[136,4096]{1,0:T(8,128)(2,1)}, u32[]{:S(2)}, u32[]{:S(2)}) collective-permute-start(bf16[136,4096]{1,0:T(8,128)(2,1)S(1)} %fusion.1.refs_1_.refs_0_), channel_id=1, source_target_pairs={{0,4},{4,0},{8,12},{12,8},{16,20},{20,16},{24,28},{28,24},{1,5},{5... | collective-permute-start | bytes 3342344 | tf_op jit(solution)/shard_map/ppermute | solution.py:54
  9.0 1.6 %collective-permute-start.1 = (bf16[136,4096]{1,0:T(8,128)(2,1)S(1)}, bf16[136,4096]{1,0:T(8,128)(2,1)}, u32[]{:S(2)}, u32[]{:S(2)}) collective-permute-start(bf16[136,4096]{1,0:T(8,128)(2,1)S(1)} %fusion.1.refs_1_.refs_0_), channel_id=1, source_target_pairs={{0,8},{4,12},{8,0},{12,4},{16,24},{20,28},{24,16},{28,20},{1,9},{5... | collective-permute-start | bytes 3342344 | tf_op jit(solution)/shard_map/ppermute | solution.py:54
  10.6 1.1 fusion.33
  11.7 2.6 %collective-permute-start.2 = (bf16[1,64,4096]{2,1,0:T(8,128)(2,1)}, bf16[1,64,4096]{2,1,0:T(8,128)(2,1)}, u32[]{:S(2)}, u32[]{:S(2)}) collective-permute-start(bf16[1,64,4096]{2,1,0:T(8,128)(2,1)} %get-tuple-element.81), channel_id=1, source_target_pairs={{0,16},{4,20},{8,24},{12,28},{16,0},{20,4},{24,8},{28,12},{1,17},{... | collective-permute-start | bytes 1572872 | tf_op jit(solution)/shard_map/ppermute | solution.py:54
  14.3 12.7 %collective-permute-done.3.refs_1_.refs_5_.refs_3_ = bf16[2,64,4096]{2,1,0:T(8,128)(2,1)S(1)} collective-permute-done((bf16[2,64,4096]{2,1,0:T(8,128)(2,1)}, bf16[2,64,4096]{2,1,0:T(8,128)(2,1)S(1)}, u32[]{:S(2)}, u32[]{:S(2)}) %collective-permute-start.3) | collective-permute-done | bytes 1048608 | tf_op jit(solution)/shard_map/ppermute | solution.py:54
  27.0 1.6 %reduce-precision_convert_fusion.1 = (bf16[16,2048]{1,0:T(8,128)(2,1)S(1)}, bf16[16,2048]{1,0:T(8,128)(2,1)S(1)}, bf16[16,2048]{1,0:T(8,128)(2,1)S(1)}, bf16[16,...) fusion(f32[16,2048]{1,0:T(8,128)} %param.13, f32[2048]{0:T(1024)S(1)} %copy-done.4), kind=kLoop, calls=%fused_computation.8 | loop fusion | flops 589824 | bytes 532480 | tf_op jit(solution)/shard_map/convert_element_type | solution.py:26
  28.6 0.1 iota_add_fusion
  28.7 0.1 add.57.ids_ref
  28.8 0.9 pad_maximum_fusion.dtab_ref
  29.6 0.0 copy-start.1
  29.6 0.0 copy-start.2
  29.7 0.0 collective-permute-done.4.refs_2_.refs_6_.refs_4_
  29.7 0.1 collective-permute-done.5.refs_3_.refs_7_.refs_5_
  29.8 3.2 %shard_map.104.refs_0_ = f32[2,16,256]{2,1,0:T(8,128)S(1)} custom-call(bf16[48,2048]{1,0:T(8,128)(2,1)S(1)} %pad_maximum_fusion.dtab_ref, bf16[2,64,4096]{2,1,0:T(8,128)(2,1)S(1)} %copy-done, bf16[2,64,4096]{2,1,0:T(8,128)(2,1)S(1)} %collective-permute-done.3.refs_1_.refs_5_.refs_3_, bf16[2,64,4096]{2,1,0:T(8,128)(2,1)} %collective-permute-done.4.refs_2_.refs_6_.refs_4_, ...), custom_call_target="tpu_custom_call" | custom-call | tf_op jit(solution)/shard_map/pallas_call | solution.py:96
  33.0 13.1 %collective-permute-done.2.refs_4_ = bf16[1,64,4096]{2,1,0:T(8,128)(2,1)} collective-permute-done((bf16[1,64,4096]{2,1,0:T(8,128)(2,1)}, bf16[1,64,4096]{2,1,0:T(8,128)(2,1)}, u32[]{:S(2)}, u32[]{:S(2)}) %collective-permute-start.2) | collective-permute-done | bytes 524320 | tf_op jit(solution)/shard_map/ppermute | solution.py:54
  46.2 0.9 collective-permute-done.1.refs_2_.refs_1_
  47.1 0.5 collective-permute-start.7
  47.6 0.4 collective-permute-start.9
  48.0 5.9 %shard_map.105 = f32[1,8,384]{2,1,0:T(8,128)S(1)} custom-call(s32[4]{0:T(128)S(1)} %add.57.ids_ref, f32[1,256]{1,0:T(1,128)S(1)} %copy-done.2, bf16[256,4096]{1,0:T(8,128)(2,1)S(1)} %copy-done.1, bf16[48,2048]{1,0:T(8,128)(2,1)S(1)} %pad_maximum_fusion.1.wtab_ref, bf16[48,2048]{1,0:T(8,128)(2,1)S(1)} %pad_maximum_fusion.dtab_ref, ...), custom_call_target="tpu_custom_call" | custom-call | flops 60397977600 | bytes 5242880 | tf_op jit(solution)/shard_map/pallas_call | solution.py:214
  53.9 0.0 copy-start.21
  53.9 4.7 %collective-permute-start.6 = (bf16[1,64,4096]{2,1,0:T(8,128)(2,1)S(1)}, bf16[1,64,4096]{2,1,0:T(8,128)(2,1)S(1)}, u32[]{:S(2)}, u32[]{:S(2)}) collective-permute-start(bf16[1,64,4096]{2,1,0:T(8,128)(2,1)S(1)} %copy-done.3), channel_id=1, source_target_pairs={{0,16},{4,20},{8,24},{12,28},{16,0},{20,4},{24,8},{28,12},{1,17},{... | collective-permute-start | bytes 1572872 | tf_op jit(solution)/shard_map/ppermute | solution.py:54
  58.6 7.8 %shard_map.106 = f32[1,8,384]{2,1,0:T(8,128)S(1)} custom-call(s32[4]{0:T(128)S(1)} %add.57.ids_ref, f32[1,256]{1,0:T(1,128)S(1)} %copy-done.2, bf16[256,4096]{1,0:T(8,128)(2,1)S(1)} %copy-done.1, bf16[48,2048]{1,0:T(8,128)(2,1)S(1)} %pad_maximum_fusion.1.wtab_ref, bf16[48,2048]{1,0:T(8,128)(2,1)S(1)} %pad_maximum_fusion.dtab_ref, ...), custom_call_target="tpu_custom_call" | custom-call | flops 60397977600 | bytes 5242880 | tf_op jit(solution)/shard_map/pallas_call | solution.py:214
  66.5 2.0 %collective-permute-start.11 = (bf16[1,64,4096]{2,1,0:T(8,128)(2,1)S(1)}, bf16[1,64,4096]{2,1,0:T(8,128)(2,1)S(1)}, u32[]{:S(2)}, u32[]{:S(2)}) collective-permute-start(bf16[1,64,4096]{2,1,0:T(8,128)(2,1)S(1)} %collective-permute-done.7.refs_5_), channel_id=1, source_target_pairs={{0,1},{1,0},{2,3},{3,2},{4,5},{5,4},{6,7},{7,6},{8,9},{9,8},{10,11... | collective-permute-start | bytes 1572872 | tf_op jit(solution)/shard_map/ppermute | solution.py:54
  68.4 0.5 fusion.25
  68.9 0.6 fusion.27
  69.6 0.6 fusion.38
  70.2 10.9 %collective-permute-done.6.refs_4_ = bf16[1,64,4096]{2,1,0:T(8,128)(2,1)S(1)} collective-permute-done((bf16[1,64,4096]{2,1,0:T(8,128)(2,1)S(1)}, bf16[1,64,4096]{2,1,0:T(8,128)(2,1)S(1)}, u32[]{:S(2)}, u32[]{:S(2)}) %collective-permute-start.6) | collective-permute-done | bytes 524320 | tf_op jit(solution)/shard_map/ppermute | solution.py:54
  81.1 2.6 %collective-permute-start.8 = (bf16[1,64,4096]{2,1,0:T(8,128)(2,1)S(1)}, bf16[1,64,4096]{2,1,0:T(8,128)(2,1)S(1)}, u32[]{:S(2)}, u32[]{:S(2)}) collective-permute-start(bf16[1,64,4096]{2,1,0:T(8,128)(2,1)S(1)} %collective-permute-done.6.refs_4_), channel_id=1, source_target_pairs={{0,2},{1,3},{2,0},{3,1},{4,6},{5,7},{6,4},{7,5},{8,10},{9,11},{10,... | collective-permute-start | bytes 1572872 | tf_op jit(solution)/shard_map/ppermute | solution.py:54
  83.7 10.4 %shard_map.107 = f32[1,8,512]{2,1,0:T(8,128)S(1)} custom-call(s32[4]{0:T(128)S(1)} %add.57.ids_ref, f32[1,256]{1,0:T(1,128)S(1)} %copy-done.2, bf16[256,4096]{1,0:T(8,128)(2,1)S(1)} %copy-done.1, bf16[48,2048]{1,0:T(8,128)(2,1)S(1)} %pad_maximum_fusion.1.wtab_ref, bf16[48,2048]{1,0:T(8,128)(2,1)S(1)} %pad_maximum_fusion.dtab_ref, ...), custom_call_target="tpu_custom_call" | custom-call | flops 72477573120 | bytes 6291456 | tf_op jit(solution)/shard_map/pallas_call | solution.py:214
  94.1 2.2 %collective-permute-done.8.refs_5_ = bf16[1,64,4096]{2,1,0:T(8,128)(2,1)S(1)} collective-permute-done((bf16[1,64,4096]{2,1,0:T(8,128)(2,1)S(1)}, bf16[1,64,4096]{2,1,0:T(8,128)(2,1)S(1)}, u32[]{:S(2)}, u32[]{:S(2)}) %collective-permute-start.8) | collective-permute-done | bytes 524320 | tf_op jit(solution)/shard_map/ppermute | solution.py:54
  96.3 4.4 %shard_map.108 = f32[1,8,128]{2,1,0:T(8,128)S(1)} custom-call(s32[4]{0:T(128)S(1)} %add.57.ids_ref, f32[1,256]{1,0:T(1,128)S(1)} %copy-done.2, bf16[256,4096]{1,0:T(8,128)(2,1)S(1)} %copy-done.1, bf16[48,2048]{1,0:T(8,128)(2,1)S(1)} %pad_maximum_fusion.1.wtab_ref, bf16[48,2048]{1,0:T(8,128)(2,1)S(1)} %pad_maximum_fusion.dtab_ref, ...), custom_call_target="tpu_custom_call" | custom-call | flops 24159191040 | bytes 3145728 | tf_op jit(solution)/shard_map/pallas_call | solution.py:214
  100.7 4.4 %shard_map.109 = f32[1,8,128]{2,1,0:T(8,128)S(1)} custom-call(s32[4]{0:T(128)S(1)} %add.57.ids_ref, f32[1,256]{1,0:T(1,128)S(1)} %copy-done.2, bf16[256,4096]{1,0:T(8,128)(2,1)S(1)} %copy-done.1, bf16[48,2048]{1,0:T(8,128)(2,1)S(1)} %pad_maximum_fusion.1.wtab_ref, bf16[48,2048]{1,0:T(8,128)(2,1)S(1)} %pad_maximum_fusion.dtab_ref, ...), custom_call_target="tpu_custom_call" | custom-call | flops 24159191040 | bytes 3145728 | tf_op jit(solution)/shard_map/pallas_call | solution.py:214
  105.1 0.0 copy-start.5
  105.1 0.0 copy-start.6
  105.3 8.2 %shard_map.110 = f32[1,8,512]{2,1,0:T(8,128)S(1)} custom-call(s32[4]{0:T(128)S(1)} %add.57.ids_ref, f32[1,256]{1,0:T(1,128)S(1)} %copy-done.2, bf16[256,4096]{1,0:T(8,128)(2,1)S(1)} %copy-done.1, bf16[48,2048]{1,0:T(8,128)(2,1)S(1)} %pad_maximum_fusion.1.wtab_ref, bf16[48,2048]{1,0:T(8,128)(2,1)S(1)} %pad_maximum_fusion.dtab_ref, ...), custom_call_target="tpu_custom_call" | custom-call | flops 72477573120 | bytes 6291456 | tf_op jit(solution)/shard_map/pallas_call | solution.py:214
  113.5 1.2 collective-permute-start.14
  114.7 5.5 %collective-permute-start.15 = (f32[4,4,128]{2,1,0:T(4,128)S(1)}, f32[4,4,128]{2,1,0:T(4,128)S(1)}, u32[]{:S(2)}, u32[]{:S(2)}) collective-permute-start(f32[4,4,128]{2,1,0:T(4,128)S(1)} %pad_maximum_fusion.3), channel_id=1, source_target_pairs={{0,4},{4,0},{8,12},{12,8},{16,20},{20,16},{24,28},{28,24},{1,5},{5... | collective-permute-start | bytes 24584 | tf_op jit(solution)/shard_map/ppermute | solution.py:54
  120.2 1.6 %collective-permute-done.15 = f32[4,4,128]{2,1,0:T(4,128)S(1)} collective-permute-done((f32[4,4,128]{2,1,0:T(4,128)S(1)}, f32[4,4,128]{2,1,0:T(4,128)S(1)}, u32[]{:S(2)}, u32[]{:S(2)}) %collective-permute-start.15) | collective-permute-done | bytes 8224 | tf_op jit(solution)/shard_map/ppermute | solution.py:54
  121.8 2.0 %collective-permute-done.16 = f32[4,4,128]{2,1,0:T(4,128)S(1)} collective-permute-done((f32[4,4,128]{2,1,0:T(4,128)S(1)}, f32[4,4,128]{2,1,0:T(4,128)S(1)}, u32[]{:S(2)}, u32[]{:S(2)}) %collective-permute-start.16) | collective-permute-done | bytes 8224 | tf_op jit(solution)/shard_map/ppermute | solution.py:54
  124.1 0.6 fusion.18
  124.7 0.6 pad_maximum_fusion.5
  (70 shorter events, 0.3 us)
Async XLA Ops:
  0.6 26.4 %collective-permute-start.3 = (bf16[2,64,4096]{2,1,0:T(8,128)(2,1)}, bf16[2,64,4096]{2,1,0:T(8,128)(2,1)S(1)}, u32[]{:S(2)}, u32[]{:S(2)}) collective-permute-start(bf16[2,64,4096]{2,1,0:T(8,128)(2,1)} %refs_2_.3), channel_id=1, source_target_pairs={{0,2},{1,3},{2,0},{3,1},{4,6},{5,7},{6,4},{7,5},{8,10},{9,11},{10,... | collective-permute-start | bytes 3145736 | tf_op jit(solution)/shard_map/ppermute | solution.py:54
  3.6 26.0 %collective-permute-start.4 = (bf16[2,64,4096]{2,1,0:T(8,128)(2,1)}, bf16[2,64,4096]{2,1,0:T(8,128)(2,1)}, u32[]{:S(2)}, u32[]{:S(2)}) collective-permute-start(bf16[2,64,4096]{2,1,0:T(8,128)(2,1)} %refs_2_.3), channel_id=1, source_target_pairs={{0,1},{1,0},{2,3},{3,2},{4,5},{5,4},{6,7},{7,6},{8,9},{9,8},{10,11... | collective-permute-start | bytes 3145736 | tf_op jit(solution)/shard_map/ppermute | solution.py:54
  4.3 6.3 %copy-start = (bf16[2,64,4096]{2,1,0:T(8,128)(2,1)S(1)}, bf16[2,64,4096]{2,1,0:T(8,128)(2,1)}, u32[]{:S(2)}) copy-start(bf16[2,64,4096]{2,1,0:T(8,128)(2,1)} %refs_2_.3) | copy-start | bytes 3145732
  7.4 19.6 %copy-start.4 = (f32[2048]{0:T(1024)S(1)}, f32[2048]{0:T(1024)}, u32[]{:S(2)}) copy-start(f32[2048]{0:T(1024)} %param.14) | copy-start | bytes 24580
  7.5 38.7 %collective-permute-start = (bf16[136,4096]{1,0:T(8,128)(2,1)S(1)}, bf16[136,4096]{1,0:T(8,128)(2,1)}, u32[]{:S(2)}, u32[]{:S(2)}) collective-permute-start(bf16[136,4096]{1,0:T(8,128)(2,1)S(1)} %fusion.1.refs_1_.refs_0_), channel_id=1, source_target_pairs={{0,4},{4,0},{8,12},{12,8},{16,20},{20,16},{24,28},{28,24},{1,5},{5... | collective-permute-start | bytes 3342344 | tf_op jit(solution)/shard_map/ppermute | solution.py:54
  9.0 38.0 %collective-permute-start.1 = (bf16[136,4096]{1,0:T(8,128)(2,1)S(1)}, bf16[136,4096]{1,0:T(8,128)(2,1)}, u32[]{:S(2)}, u32[]{:S(2)}) collective-permute-start(bf16[136,4096]{1,0:T(8,128)(2,1)S(1)} %fusion.1.refs_1_.refs_0_), channel_id=1, source_target_pairs={{0,8},{4,12},{8,0},{12,4},{16,24},{20,28},{24,16},{28,20},{1,9},{5... | collective-permute-start | bytes 3342344 | tf_op jit(solution)/shard_map/ppermute | solution.py:54
  11.7 34.5 %collective-permute-start.2 = (bf16[1,64,4096]{2,1,0:T(8,128)(2,1)}, bf16[1,64,4096]{2,1,0:T(8,128)(2,1)}, u32[]{:S(2)}, u32[]{:S(2)}) collective-permute-start(bf16[1,64,4096]{2,1,0:T(8,128)(2,1)} %get-tuple-element.81), channel_id=1, source_target_pairs={{0,16},{4,20},{8,24},{12,28},{16,0},{20,4},{24,8},{28,12},{1,17},{... | collective-permute-start | bytes 1572872 | tf_op jit(solution)/shard_map/ppermute | solution.py:54
  27.0 2.8 %collective-permute-start.5 = (bf16[2,64,4096]{2,1,0:T(8,128)(2,1)S(1)}, bf16[2,64,4096]{2,1,0:T(8,128)(2,1)}, u32[]{:S(2)}, u32[]{:S(2)}) collective-permute-start(bf16[2,64,4096]{2,1,0:T(8,128)(2,1)S(1)} %collective-permute-done.3.refs_1_.refs_5_.refs_3_), channel_id=1, source_target_pairs={{0,1},{1,0},{2,3},{3,2},{4,5},{5,4},{6,7},{7,6},{8,9},{9,8},{10,11... | collective-permute-start | bytes 3145736 | tf_op jit(solution)/shard_map/ppermute | solution.py:54
  29.6 18.4 %copy-start.1 = (bf16[256,4096]{1,0:T(8,128)(2,1)S(1)}, bf16[256,4096]{1,0:T(8,128)(2,1)}, u32[]{:S(2)}) copy-start(bf16[256,4096]{1,0:T(8,128)(2,1)} %constant.76.clone.table_ref) | copy-start | bytes 6291460
  29.6 18.3 %copy-start.2 = (f32[1,256]{1,0:T(1,128)S(1)}, f32[1,256]{1,0:T(1,128)}, u32[]{:S(2)}) copy-start(f32[1,256]{1,0:T(1,128)} %constant.77.clone.label_ref) | copy-start | bytes 3076
  47.1 6.8 %copy-start.3 = (bf16[1,64,4096]{2,1,0:T(8,128)(2,1)S(1)}, bf16[1,64,4096]{2,1,0:T(8,128)(2,1)}, u32[]{:S(2)}) copy-start(bf16[1,64,4096]{2,1,0:T(8,128)(2,1)} %get-tuple-element.35) | copy-start | bytes 1572868
  47.1 19.4 %collective-permute-start.7 = (bf16[1,64,4096]{2,1,0:T(8,128)(2,1)}, bf16[1,64,4096]{2,1,0:T(8,128)(2,1)S(1)}, u32[]{:S(2)}, u32[]{:S(2)}) collective-permute-start(bf16[1,64,4096]{2,1,0:T(8,128)(2,1)} %collective-permute-done.2.refs_4_), channel_id=1, source_target_pairs={{0,2},{1,3},{2,0},{3,1},{4,6},{5,7},{6,4},{7,5},{8,10},{9,11},{10,... | collective-permute-start | bytes 1572872 | tf_op jit(solution)/shard_map/ppermute | solution.py:54
  47.6 36.0 %collective-permute-start.10 = (bf16[1,64,4096]{2,1,0:T(8,128)(2,1)}, bf16[1,64,4096]{2,1,0:T(8,128)(2,1)S(1)}, u32[]{:S(2)}, u32[]{:S(2)}) collective-permute-start(bf16[1,64,4096]{2,1,0:T(8,128)(2,1)} %collective-permute-done.2.refs_4_), channel_id=1, source_target_pairs={{0,1},{1,0},{2,3},{3,2},{4,5},{5,4},{6,7},{7,6},{8,9},{9,8},{10,11... | collective-permute-start | bytes 1572872 | tf_op jit(solution)/shard_map/ppermute | solution.py:54
  47.6 36.0 %collective-permute-start.9 = (bf16[136,4096]{1,0:T(8,128)(2,1)}, bf16[136,4096]{1,0:T(8,128)(2,1)S(1)}, u32[]{:S(2)}, u32[]{:S(2)}) collective-permute-start(bf16[136,4096]{1,0:T(8,128)(2,1)} %collective-permute-done.1.refs_2_.refs_1_), channel_id=1, source_target_pairs={{0,4},{4,0},{8,12},{12,8},{16,20},{20,16},{24,28},{28,24},{1,5},{5... | collective-permute-start | bytes 3342344 | tf_op jit(solution)/shard_map/ppermute | solution.py:54
  53.9 14.5 %copy-start.21 = (s32[128,2]{0,1:T(2,128)S(1)}, s32[128,2]{0,1:T(2,128)}, u32[]{:S(2)}) copy-start(s32[128,2]{0,1:T(2,128)} %param.10) | copy-start | bytes 3076
  53.9 27.2 %collective-permute-start.6 = (bf16[1,64,4096]{2,1,0:T(8,128)(2,1)S(1)}, bf16[1,64,4096]{2,1,0:T(8,128)(2,1)S(1)}, u32[]{:S(2)}, u32[]{:S(2)}) collective-permute-start(bf16[1,64,4096]{2,1,0:T(8,128)(2,1)S(1)} %copy-done.3), channel_id=1, source_target_pairs={{0,16},{4,20},{8,24},{12,28},{16,0},{20,4},{24,8},{28,12},{1,17},{... | collective-permute-start | bytes 1572872 | tf_op jit(solution)/shard_map/ppermute | solution.py:54
  66.5 17.2 %collective-permute-start.11 = (bf16[1,64,4096]{2,1,0:T(8,128)(2,1)S(1)}, bf16[1,64,4096]{2,1,0:T(8,128)(2,1)S(1)}, u32[]{:S(2)}, u32[]{:S(2)}) collective-permute-start(bf16[1,64,4096]{2,1,0:T(8,128)(2,1)S(1)} %collective-permute-done.7.refs_5_), channel_id=1, source_target_pairs={{0,1},{1,0},{2,3},{3,2},{4,5},{5,4},{6,7},{7,6},{8,9},{9,8},{10,11... | collective-permute-start | bytes 1572872 | tf_op jit(solution)/shard_map/ppermute | solution.py:54
  81.1 15.2 %collective-permute-start.8 = (bf16[1,64,4096]{2,1,0:T(8,128)(2,1)S(1)}, bf16[1,64,4096]{2,1,0:T(8,128)(2,1)S(1)}, u32[]{:S(2)}, u32[]{:S(2)}) collective-permute-start(bf16[1,64,4096]{2,1,0:T(8,128)(2,1)S(1)} %collective-permute-done.6.refs_4_), channel_id=1, source_target_pairs={{0,2},{1,3},{2,0},{3,1},{4,6},{5,7},{6,4},{7,5},{8,10},{9,11},{10,... | collective-permute-start | bytes 1572872 | tf_op jit(solution)/shard_map/ppermute | solution.py:54
  83.7 21.6 %collective-permute-start.12 = (bf16[1,64,4096]{2,1,0:T(8,128)(2,1)S(1)}, bf16[1,64,4096]{2,1,0:T(8,128)(2,1)S(1)}, u32[]{:S(2)}, u32[]{:S(2)}) collective-permute-start(bf16[1,64,4096]{2,1,0:T(8,128)(2,1)S(1)} %collective-permute-done.6.refs_4_), channel_id=1, source_target_pairs={{0,1},{1,0},{2,3},{3,2},{4,5},{5,4},{6,7},{7,6},{8,9},{9,8},{10,11... | collective-permute-start | bytes 1572872 | tf_op jit(solution)/shard_map/ppermute | solution.py:54
  96.3 9.0 %collective-permute-start.13 = (bf16[1,64,4096]{2,1,0:T(8,128)(2,1)S(1)}, bf16[1,64,4096]{2,1,0:T(8,128)(2,1)S(1)}, u32[]{:S(2)}, u32[]{:S(2)}) collective-permute-start(bf16[1,64,4096]{2,1,0:T(8,128)(2,1)S(1)} %collective-permute-done.8.refs_5_), channel_id=1, source_target_pairs={{0,1},{1,0},{2,3},{3,2},{4,5},{5,4},{6,7},{7,6},{8,9},{9,8},{10,11... | collective-permute-start | bytes 1572872 | tf_op jit(solution)/shard_map/ppermute | solution.py:54
  105.1 18.8 %copy-start.5 = (pred[2,128]{1,0:T(4,128)(4,1)S(1)}, pred[2,128]{1,0:T(4,128)(4,1)}, u32[]{:S(2)}) copy-start(pred[2,128]{1,0:T(4,128)(4,1)} %get-tuple-element.63) | copy-start | bytes 772
  105.1 18.8 %copy-start.6 = (pred[2,128]{1,0:T(4,128)(4,1)S(1)}, pred[2,128]{1,0:T(4,128)(4,1)}, u32[]{:S(2)}) copy-start(pred[2,128]{1,0:T(4,128)(4,1)} %get-tuple-element.68) | copy-start | bytes 772
  105.1 18.8 %copy-start.7 = (pred[2,128]{1,0:T(4,128)(4,1)S(1)}, pred[2,128]{1,0:T(4,128)(4,1)}, u32[]{:S(2)}) copy-start(pred[2,128]{1,0:T(4,128)(4,1)} %get-tuple-element.120) | copy-start | bytes 772
  105.1 18.8 %copy-start.8 = (pred[2,128]{1,0:T(4,128)(4,1)S(1)}, pred[2,128]{1,0:T(4,128)(4,1)}, u32[]{:S(2)}) copy-start(pred[2,128]{1,0:T(4,128)(4,1)} %get-tuple-element.122) | copy-start | bytes 772
  105.1 18.8 %copy-start.9 = (pred[2,128]{1,0:T(4,128)(4,1)S(1)}, pred[2,128]{1,0:T(4,128)(4,1)}, u32[]{:S(2)}) copy-start(pred[2,128]{1,0:T(4,128)(4,1)} %get-tuple-element.133) | copy-start | bytes 772
  105.1 18.8 %copy-start.10 = (pred[2,128]{1,0:T(4,128)(4,1)S(1)}, pred[2,128]{1,0:T(4,128)(4,1)}, u32[]{:S(2)}) copy-start(pred[2,128]{1,0:T(4,128)(4,1)} %get-tuple-element.135) | copy-start | bytes 772
  105.1 18.8 %copy-start.11 = (pred[2,128]{1,0:T(4,128)(4,1)S(1)}, pred[2,128]{1,0:T(4,128)(4,1)}, u32[]{:S(2)}) copy-start(pred[2,128]{1,0:T(4,128)(4,1)} %get-tuple-element.137) | copy-start | bytes 772
  105.1 18.8 %copy-start.12 = (pred[2,128]{1,0:T(4,128)(4,1)S(1)}, pred[2,128]{1,0:T(4,128)(4,1)}, u32[]{:S(2)}) copy-start(pred[2,128]{1,0:T(4,128)(4,1)} %get-tuple-element.124) | copy-start | bytes 772
  105.2 18.8 %copy-start.13 = (pred[2,128]{1,0:T(4,128)(4,1)S(1)}, pred[2,128]{1,0:T(4,128)(4,1)}, u32[]{:S(2)}) copy-start(pred[2,128]{1,0:T(4,128)(4,1)} %get-tuple-element.125) | copy-start | bytes 772
  105.2 18.8 %copy-start.14 = (pred[2,128]{1,0:T(4,128)(4,1)S(1)}, pred[2,128]{1,0:T(4,128)(4,1)}, u32[]{:S(2)}) copy-start(pred[2,128]{1,0:T(4,128)(4,1)} %get-tuple-element.126) | copy-start | bytes 772
  105.2 18.8 %copy-start.15 = (pred[2,128]{1,0:T(4,128)(4,1)S(1)}, pred[2,128]{1,0:T(4,128)(4,1)}, u32[]{:S(2)}) copy-start(pred[2,128]{1,0:T(4,128)(4,1)} %get-tuple-element.127) | copy-start | bytes 772
  105.2 18.8 %copy-start.16 = (pred[2,128]{1,0:T(4,128)(4,1)S(1)}, pred[2,128]{1,0:T(4,128)(4,1)}, u32[]{:S(2)}) copy-start(pred[2,128]{1,0:T(4,128)(4,1)} %get-tuple-element.128) | copy-start | bytes 772
  105.2 18.8 %copy-start.17 = (pred[2,128]{1,0:T(4,128)(4,1)S(1)}, pred[2,128]{1,0:T(4,128)(4,1)}, u32[]{:S(2)}) copy-start(pred[2,128]{1,0:T(4,128)(4,1)} %get-tuple-element.129) | copy-start | bytes 772
  105.2 18.8 %copy-start.18 = (pred[2,128]{1,0:T(4,128)(4,1)S(1)}, pred[2,128]{1,0:T(4,128)(4,1)}, u32[]{:S(2)}) copy-start(pred[2,128]{1,0:T(4,128)(4,1)} %get-tuple-element.130) | copy-start | bytes 772
  105.2 18.8 %copy-start.19 = (pred[2,128]{1,0:T(4,128)(4,1)S(1)}, pred[2,128]{1,0:T(4,128)(4,1)}, u32[]{:S(2)}) copy-start(pred[2,128]{1,0:T(4,128)(4,1)} %get-tuple-element.131) | copy-start | bytes 772
  105.2 18.8 %copy-start.20 = (pred[2,128]{1,0:T(4,128)(4,1)S(1)}, pred[2,128]{1,0:T(4,128)(4,1)}, u32[]{:S(2)}) copy-start(pred[2,128]{1,0:T(4,128)(4,1)} %get-tuple-element.132) | copy-start | bytes 772
  113.5 6.7 %collective-permute-start.14 = (f32[4,4,128]{2,1,0:T(4,128)S(1)}, f32[4,4,128]{2,1,0:T(4,128)S(1)}, u32[]{:S(2)}, u32[]{:S(2)}) collective-permute-start(f32[4,4,128]{2,1,0:T(4,128)S(1)} %pad_maximum_fusion.2), channel_id=1, source_target_pairs={{0,12},{4,8},{8,4},{12,0},{16,28},{20,24},{24,20},{28,16},{1,13},{... | collective-permute-start | bytes 24584 | tf_op jit(solution)/shard_map/ppermute | solution.py:54
  114.7 7.1 %collective-permute-start.15 = (f32[4,4,128]{2,1,0:T(4,128)S(1)}, f32[4,4,128]{2,1,0:T(4,128)S(1)}, u32[]{:S(2)}, u32[]{:S(2)}) collective-permute-start(f32[4,4,128]{2,1,0:T(4,128)S(1)} %pad_maximum_fusion.3), channel_id=1, source_target_pairs={{0,4},{4,0},{8,12},{12,8},{16,20},{20,16},{24,28},{28,24},{1,5},{5... | collective-permute-start | bytes 24584 | tf_op jit(solution)/shard_map/ppermute | solution.py:54
  120.2 3.7 %collective-permute-start.16 = (f32[4,4,128]{2,1,0:T(4,128)S(1)}, f32[4,4,128]{2,1,0:T(4,128)S(1)}, u32[]{:S(2)}, u32[]{:S(2)}) collective-permute-start(f32[4,4,128]{2,1,0:T(4,128)S(1)} %pad_maximum_fusion.4), channel_id=1, source_target_pairs={{0,8},{4,12},{8,0},{12,4},{16,24},{20,28},{24,16},{28,20},{1,9},{5... | collective-permute-start | bytes 24584 | tf_op jit(solution)/shard_map/ppermute | solution.py:54

commit v6 on v5

--- a/solution.py
+++ b/solution.py
@@ -102,13 +102,13 @@
     )(dtab, *pieces)
 
 
-def stats_kernel(trans, index, spots, share, have_penalty, ids_ref, label_ref, table_ref, wtab_ref,
+def stats_kernel(trans, jobs, pieces, share, have_penalty, ids_ref, label_ref, table_ref, wtab_ref,
                  dtab_ref, *refs):
     if have_penalty:
         penalty_ref, refs = refs[0], refs[1:]
     x_refs, refs = refs[:share], refs[share:]
-    q_refs = refs[:len(spots)]
-    out_ref, uv, pens, info, stats = refs[len(spots):]
+    q_refs = refs[:pieces]
+    out_ref, uv, pens, info, stats = refs[pieces:]
     rows_all = out_ref.shape[2]
     rows = rows_all // share
     features = info.shape[1]
@@ -116,7 +116,6 @@
     pixels = uv.shape[1] // 2
     ori = pens.shape[1]
     groups = dtab_ref.shape[0] // 3
-    views = views_of(q_refs, spots)
 
     def particles(cols):
         return jnp.concatenate([member[:rows, cols] for member in x_refs], axis=0)
@@ -127,95 +126,96 @@
          for block in below], axis=1)
     named = meta[3 * trans + 1:, :]
     meta = meta.astype(jnp.bfloat16)
-    wanted = ids_ref[index].astype(jnp.float32)
-    names = jnp.max(jnp.where(named == wanted, 1.0, 0.0), axis=0, keepdims=True)
     before = lax.broadcasted_iota(jnp.int32, (rows_all, rows_all), 0)
     after = lax.broadcasted_iota(jnp.int32, (rows_all, rows_all), 1)
     upper = jnp.where(before <= after, 1.0, 0.0).astype(jnp.bfloat16)
-    ahead = jnp.dot(jnp.broadcast_to(names, (16, rows_all)).astype(jnp.bfloat16), upper,
-                    preferred_element_type=jnp.float32)[:1]
-    rank = jnp.where(names > 0.0, ahead - 1.0, -1.0).astype(jnp.int32)
-    tiles = (jnp.max(ahead).astype(jnp.int32) + (TILE - 1)) // TILE
-
-    row = lax.broadcasted_iota(jnp.int32, (slots, rows_all), 0)
-    pick = jnp.where(rank == row, 1.0, 0.0).astype(jnp.bfloat16)
-    info[...] = lax.dot_general(pick, meta, contract_last, preferred_element_type=jnp.float32)
-    lane = lax.broadcasted_iota(jnp.int32, (slots, 3 * groups), 1)
-    group_hot = jnp.where(info[:, trans:trans + 1] == (lane % groups).astype(jnp.float32), 1.0, 0.0)
-    group_hot = group_hot.astype(jnp.bfloat16)
-    stats[...] = jnp.zeros_like(stats)
-    for first in range(0, pixels, CHUNK):
-        weight = jnp.dot(group_hot, wtab_ref[:, first:first + CHUNK], preferred_element_type=jnp.float32)
-        for start in (first, pixels + first):
-            span = slice(start, start + CHUNK)
-            uv[:, span] = weight * jnp.dot(pick, particles(span), preferred_element_type=jnp.float32)
-    penalty = penalty_ref[spots[0]] if have_penalty else penalties_of(views, dtab_ref, ori, pixels)
-    pens[...] = jnp.dot(group_hot, jnp.concatenate(three(penalty), axis=0),
-                        preferred_element_type=jnp.float32)
     label = label_ref[...]
 
-    @pl.loop(0, tiles)
-    def _(tile):
-        mine = pl.ds(pl.multiple_of(tile * TILE, TILE), TILE)
-        here = info[mine, :]
-        hot = jnp.concatenate(
-            [jnp.where(here[:, t:t + 1] == label, 1.0, 0.0) for t in range(trans)], axis=0
-        ).astype(jnp.bfloat16)
-        scores = jnp.zeros((trans * TILE, ori), jnp.float32)
-        for first in range(0, pixels, PIECE):
-            cols = slice(first, first + PIECE)
-            icols = slice(pixels + first, pixels + first + PIECE)
-            cosine = jnp.dot(hot, table_ref[:, cols], preferred_element_type=jnp.float32)
-            sine = jnp.dot(hot, table_ref[:, icols], preferred_element_type=jnp.float32)
-            cosine = cosine.reshape(trans, TILE, PIECE)
-            sine = sine.reshape(trans, TILE, PIECE)
-            real = uv[mine, cols][None]
-            imag = uv[mine, icols][None]
-            shift_re = (real * cosine + imag * sine).astype(jnp.bfloat16)
-            shift_im = (imag * cosine - real * sine).astype(jnp.bfloat16)
-            scores += lax.dot_general(shift_re.reshape(trans * TILE, PIECE), views(cols), contract_last,
-                                      preferred_element_type=jnp.float32)
-            scores += lax.dot_general(shift_im.reshape(trans * TILE, PIECE), views(icols), contract_last,
-                                      preferred_element_type=jnp.float32)
-        full = scores.reshape(trans, TILE, ori) + pens[mine, :][None]
-        highest = jnp.max(jnp.max(full, axis=0), axis=1, keepdims=True)
-        total = jnp.zeros((TILE, ori), jnp.float32)
-        moment_x = jnp.zeros((TILE, ori), jnp.float32)
-        moment_y = jnp.zeros((TILE, ori), jnp.float32)
-        for t in range(trans):
-            term = jnp.exp(full[t] - highest)
-            total += term
-            moment_x += term * here[:, trans + 1 + t:trans + 2 + t]
-            moment_y += term * here[:, 2 * trans + 1 + t:2 * trans + 2 + t]
-        total = jnp.sum(total, axis=1, keepdims=True)
-        moment_x = jnp.sum(moment_x, axis=1, keepdims=True)
-        moment_y = jnp.sum(moment_y, axis=1, keepdims=True)
-        lanes = lax.broadcasted_iota(jnp.int32, (TILE, 128), 1)
-        stats[mine, :] = jnp.where(
-            lanes == 0, highest,
-            jnp.where(lanes == 1, total, jnp.where(lanes == 2, moment_x,
-                                                   jnp.where(lanes == 3, moment_y, 0.0))))
-
-    back = sum(
-        lax.dot_general(part, pick, (((0,), (0,)), ((), ())), preferred_element_type=jnp.float32)
-        for part in three(stats[...])
-    )
-    out_ref[0] = back[:8, :]
-
-
-def class_stats(index, ids, label, table, wtab, dtab, penalty, x_parts, q_parts, trans, slots, features):
+    for place, (index, spot) in enumerate(jobs):
+        views = views_of(q_refs, [spot] * pieces)
+        wanted = ids_ref[index].astype(jnp.float32)
+        names = jnp.max(jnp.where(named == wanted, 1.0, 0.0), axis=0, keepdims=True)
+        ahead = jnp.dot(jnp.broadcast_to(names, (16, rows_all)).astype(jnp.bfloat16), upper,
+                        preferred_element_type=jnp.float32)[:1]
+        rank = jnp.where(names > 0.0, ahead - 1.0, -1.0).astype(jnp.int32)
+        tiles = (jnp.max(ahead).astype(jnp.int32) + (TILE - 1)) // TILE
+
+        row = lax.broadcasted_iota(jnp.int32, (slots, rows_all), 0)
+        pick = jnp.where(rank == row, 1.0, 0.0).astype(jnp.bfloat16)
+        info[...] = lax.dot_general(pick, meta, contract_last, preferred_element_type=jnp.float32)
+        lane = lax.broadcasted_iota(jnp.int32, (slots, 3 * groups), 1)
+        group_hot = jnp.where(info[:, trans:trans + 1] == (lane % groups).astype(jnp.float32), 1.0, 0.0)
+        group_hot = group_hot.astype(jnp.bfloat16)
+        stats[...] = jnp.zeros_like(stats)
+        for first in range(0, pixels, CHUNK):
+            weight = jnp.dot(group_hot, wtab_ref[:, first:first + CHUNK], preferred_element_type=jnp.float32)
+            for start in (first, pixels + first):
+                span = slice(start, start + CHUNK)
+                uv[:, span] = weight * jnp.dot(pick, particles(span), preferred_element_type=jnp.float32)
+        penalty = penalty_ref[spot] if have_penalty else penalties_of(views, dtab_ref, ori, pixels)
+        pens[...] = jnp.dot(group_hot, jnp.concatenate(three(penalty), axis=0),
+                            preferred_element_type=jnp.float32)
+
+        @pl.loop(0, tiles)
+        def _(tile):
+            mine = pl.ds(pl.multiple_of(tile * TILE, TILE), TILE)
+            here = info[mine, :]
+            hot = jnp.concatenate(
+                [jnp.where(here[:, t:t + 1] == label, 1.0, 0.0) for t in range(trans)], axis=0
+            ).astype(jnp.bfloat16)
+            scores = jnp.zeros((trans * TILE, ori), jnp.float32)
+            for first in range(0, pixels, PIECE):
+                cols = slice(first, first + PIECE)
+                icols = slice(pixels + first, pixels + first + PIECE)
+                cosine = jnp.dot(hot, table_ref[:, cols], preferred_element_type=jnp.float32)
+                sine = jnp.dot(hot, table_ref[:, icols], preferred_element_type=jnp.float32)
+                cosine = cosine.reshape(trans, TILE, PIECE)
+                sine = sine.reshape(trans, TILE, PIECE)
+                real = uv[mine, cols][None]
+                imag = uv[mine, icols][None]
+                shift_re = (real * cosine + imag * sine).astype(jnp.bfloat16)
+                shift_im = (imag * cosine - real * sine).astype(jnp.bfloat16)
+                scores += lax.dot_general(shift_re.reshape(trans * TILE, PIECE), views(cols), contract_last,
+                                          preferred_element_type=jnp.float32)
+                scores += lax.dot_general(shift_im.reshape(trans * TILE, PIECE), views(icols), contract_last,
+                                          preferred_element_type=jnp.float32)
+            full = scores.reshape(trans, TILE, ori) + pens[mine, :][None]
+            highest = jnp.max(jnp.max(full, axis=0), axis=1, keepdims=True)
+            total = jnp.zeros((TILE, ori), jnp.float32)
+            moment_x = jnp.zeros((TILE, ori), jnp.float32)
+            moment_y = jnp.zeros((TILE, ori), jnp.float32)
+            for t in range(trans):
+                term = jnp.exp(full[t] - highest)
+                total += term
+                moment_x += term * here[:, trans + 1 + t:trans + 2 + t]
+                moment_y += term * here[:, 2 * trans + 1 + t:2 * trans + 2 + t]
+            total = jnp.sum(total, axis=1, keepdims=True)
+            moment_x = jnp.sum(moment_x, axis=1, keepdims=True)
+            moment_y = jnp.sum(moment_y, axis=1, keepdims=True)
+            lanes = lax.broadcasted_iota(jnp.int32, (TILE, 128), 1)
+            stats[mine, :] = jnp.where(
+                lanes == 0, highest,
+                jnp.where(lanes == 1, total, jnp.where(lanes == 2, moment_x,
+                                                       jnp.where(lanes == 3, moment_y, 0.0))))
+
+        back = sum(
+            lax.dot_general(part, pick, (((0,), (0,)), ((), ())), preferred_element_type=jnp.float32)
+            for part in three(stats[...])
+        )
+        out_ref[place] = back[:8, :]
+
+
+def class_stats(jobs, ids, label, table, wtab, dtab, penalty, x_parts, q_parts, trans, slots, features):
     rows_all = sum(part.shape[0] - 8 for part in x_parts)
-    rows_q, width = q_parts[0][0].shape[1:]
+    rows_q, width = q_parts[0].shape[1:]
     ori = rows_q * len(q_parts)
-    arrays = [array for array, _ in q_parts]
-    spots = [spot for _, spot in q_parts]
     extra = [] if penalty is None else [penalty]
     vmem = pl.BlockSpec(memory_space=pltpu.VMEM)
     return pl.pallas_call(
-        functools.partial(stats_kernel, trans, index, spots, len(x_parts), penalty is not None),
-        out_shape=jax.ShapeDtypeStruct((1, 8, rows_all), jnp.float32),
+        functools.partial(stats_kernel, trans, jobs, len(q_parts), len(x_parts), penalty is not None),
+        out_shape=jax.ShapeDtypeStruct((len(jobs), 8, rows_all), jnp.float32),
         in_specs=[pl.BlockSpec(memory_space=pltpu.SMEM)]
-        + [vmem] * (4 + len(extra) + len(x_parts) + len(arrays)),
+        + [vmem] * (4 + len(extra) + len(x_parts) + len(q_parts)),
         out_specs=vmem,
         scratch_shapes=[
             pltpu.VMEM((slots, width), jnp.float32),
@@ -225,11 +225,11 @@
         ],
         compiler_params=pltpu.CompilerParams(vmem_limit_bytes=28 * 1024 * 1024),
         cost_estimate=pl.CostEstimate(
-            flops=20 * slots * trans * width * (ori + 256),
+            flops=20 * len(jobs) * slots * trans * width * (ori + 256),
             bytes_accessed=(rows_all + ori) * width * 2,
             transcendentals=0,
         ),
-    )(ids, label, table, wtab, dtab, *extra, *x_parts, *arrays)
+    )(ids, label, table, wtab, dtab, *extra, *x_parts, *q_parts)
 
 
 def on_device(particles, candidates, ctf_ids, offsets, ctf_table, sigma_sq, projections):
@@ -297,39 +297,39 @@
     results = {}
     latest = []
 
-    def one_class(index, members, penalty, first, last):
+    def run(key, jobs, members, penalty, first, last):
         turn = ids
         if latest:
             turn, results[latest[-1]] = lax.optimization_barrier((turn, results[latest[-1]]))
-        results[(index, first)] = class_stats(
-            index, turn, label, table, wtab, dtab, penalty, x_parts[first:last], members, trans,
-            slots_for(last - first), features)
-        latest.append((index, first))
-
-    own = [[(piece, spot) for piece in own_pieces] for spot in range(local)]
-    for spot in range(local):
-        one_class(spot, own[spot], own_penalty, 0, near)
+        results[key] = class_stats(jobs, turn, label, table, wtab, dtab, penalty, x_parts[first:last],
+                                   members, trans, slots_for(last - first), features)
+        latest.append(key)
+
+    own_jobs = [(spot, spot) for spot in range(local)]
+    run("near", own_jobs, own_pieces, own_penalty, 0, near)
     for family in range(1, families):
         for spot in range(local):
             pieces = [far[family - 1][spot]]
             for hop, bit in enumerate(dom_bits):
                 if spot or hop:
-                    key = (family * local + spot - 1, 0) if hop and spot else (local - 1, 0)
+                    key = "last" if hop and spot else "near"
                     pieces[hop:], results[key] = lax.optimization_barrier((pieces[hop:], results[key]))
                 pieces = pieces + [swap(member, "dom", bit) for member in pieces]
-            one_class(family * local + spot, [(member, 0) for member in pieces], None, 0, share)
-            if family == 1 and spot == 0 and near < share:
-                for place in range(local):
-                    one_class(place, own[place], own_penalty, near, share)
+            index = family * local + spot
+            run(index, [(index, 0)], pieces, None, 0, share)
+            if "last" not in results:
+                run("last", own_jobs, own_pieces, own_penalty, near, share)
 
     results = dict(zip(results, lax.optimization_barrier(tuple(results.values()))))
     own = []
     for place, member in enumerate(order):
         block = []
         for spot in range(families * local):
-            first = near if spot < local and place >= near else 0
-            start = (place - first) * rows
-            block.append(results[(spot, first)][:, :4, start:start + rows])
+            key, at = spot, 0
+            if spot < local:
+                key, at = ("near" if place < near else "last"), spot
+            start = (place - (near if key == "last" else 0)) * rows
+            block.append(results[key][at:at + 1, :4, start:start + rows])
         block = jnp.concatenate(block, axis=0)
         block = swap(block, "pose", member) if member else block
         own += [(member, spot, block[spot]) for spot in range(families * local)]

time: 126 us -> 118 us (0.937)
  the two profiles are of different devices: /device:TPU:0 before, /device:TPU:18 now
where the time goes in v6:
time: 118 us; the launch traced here: 116 us
  waiting for transfers between devices  45.4 us (38%)
  Pallas kernels  40.3 us (34%)
  starting transfers between devices  21 us (18%)
  other arithmetic  7.29 us (6%)
  local copies, waits for them, and re-layouts  1.57 us (1%)
    ppermute x17, waiting for transfers between devices, swap(): lax.ppermute(values, axis, [(index, index ^ bit) for index in range(count)])  45.4 us
    pallas_call x4, Pallas kernels, class_stats(): pl.pallas_call(functools.partial(stats_kernel, trans, jobs, len(q_parts),...  37 us
    ppermute x17, starting transfers between devices, swap(): lax.ppermute(values, axis, [(index, index ^ bit) for index in range(count)])  21 us
    pallas_call x1, Pallas kernels, own_penalties(): pl.pallas_call(functools.partial(penalty_kernel, len(pieces)), out_shape=...  3.26 us
  transfers between devices with their start and end apart: 17, of which 8 were waited for; matrix products, arithmetic and copies ran while one was open for 7% of the time, Pallas kernels for 28%

profile of v6, /device:TPU:18, one launch (start us, length us, event | category | flops | bytes accessed | tf_op | source)
XLA Modules:
  0.0 116.4 jit_solution(8167382779647465338)
XLA Ops:
  0.6 0.6 collective-permute-start.3
  1.2 0.0 collective-permute-start.4
  1.2 0.7 fusion.6
  2.0 0.7 convert_bitcast_fusion
  2.7 0.7 fusion.16
  3.4 0.3 concatenate.25
  3.7 1.3 %fusion.1.refs_1_.refs_0_ = bf16[136,4096]{1,0:T(8,128)(2,1)S(1)} fusion(bf16[8,512]{1,0:T(8,128)(2,1)S(1)} %pad_bitcast_fusion, bf16[128,4096]{1,0:T(8,128)(2,1)} %param.9), kind=kLoop, calls=%fused_computation.2 | loop fusion | flops 3342336 | bytes 2170880 | tf_op jit(solution)/shard_map/concatenate | solution.py:269
  5.0 0.0 copy-start.4
  5.1 1.6 %collective-permute-start = (bf16[136,4096]{1,0:T(8,128)(2,1)S(1)}, bf16[136,4096]{1,0:T(8,128)(2,1)}, u32[]{:S(2)}, u32[]{:S(2)}) collective-permute-start(bf16[136,4096]{1,0:T(8,128)(2,1)S(1)} %fusion.1.refs_1_.refs_0_), channel_id=1, source_target_pairs={{0,4},{4,0},{8,12},{12,8},{16,20},{20,16},{24,28},{28,24},{1,5},{5... | collective-permute-start | bytes 3342344 | tf_op jit(solution)/shard_map/ppermute | solution.py:54
  6.6 1.6 %collective-permute-start.1 = (bf16[136,4096]{1,0:T(8,128)(2,1)S(1)}, bf16[136,4096]{1,0:T(8,128)(2,1)}, u32[]{:S(2)}, u32[]{:S(2)}) collective-permute-start(bf16[136,4096]{1,0:T(8,128)(2,1)S(1)} %fusion.1.refs_1_.refs_0_), channel_id=1, source_target_pairs={{0,8},{4,12},{8,0},{12,4},{16,24},{20,28},{24,16},{28,20},{1,9},{5... | collective-permute-start | bytes 3342344 | tf_op jit(solution)/shard_map/ppermute | solution.py:54
  8.2 1.1 fusion.33
  9.3 0.3 collective-permute-start.2
  9.7 16.1 %collective-permute-done.3.refs_1_.refs_5_.refs_3_ = bf16[2,64,4096]{2,1,0:T(8,128)(2,1)S(1)} collective-permute-done((bf16[2,64,4096]{2,1,0:T(8,128)(2,1)}, bf16[2,64,4096]{2,1,0:T(8,128)(2,1)S(1)}, u32[]{:S(2)}, u32[]{:S(2)}) %collective-permute-start.3) | collective-permute-done | bytes 1048608 | tf_op jit(solution)/shard_map/ppermute | solution.py:54
  25.8 1.6 %reduce-precision_convert_fusion.1 = (bf16[16,2048]{1,0:T(8,128)(2,1)S(1)}, bf16[16,2048]{1,0:T(8,128)(2,1)S(1)}, bf16[16,2048]{1,0:T(8,128)(2,1)S(1)}, bf16[16,...) fusion(f32[16,2048]{1,0:T(8,128)} %param.13, f32[2048]{0:T(1024)S(1)} %copy-done.4), kind=kLoop, calls=%fused_computation.8 | loop fusion | flops 589824 | bytes 532480 | tf_op jit(solution)/shard_map/convert_element_type | solution.py:26
  27.4 0.1 iota_add_fusion
  27.5 0.1 add.57.ids_ref
  27.6 0.9 pad_maximum_fusion.dtab_ref
  28.4 0.0 copy-start.1
  28.5 0.0 copy-start.2
  28.5 0.1 collective-permute-done.5.refs_3_.refs_7_.refs_5_
  28.6 3.3 %shard_map.104.refs_0_ = f32[2,16,256]{2,1,0:T(8,128)S(1)} custom-call(bf16[48,2048]{1,0:T(8,128)(2,1)S(1)} %pad_maximum_fusion.dtab_ref, bf16[2,64,4096]{2,1,0:T(8,128)(2,1)S(1)} %copy-done, bf16[2,64,4096]{2,1,0:T(8,128)(2,1)S(1)} %collective-permute-done.3.refs_1_.refs_5_.refs_3_, bf16[2,64,4096]{2,1,0:T(8,128)(2,1)} %collective-permute-done.4.refs_2_.refs_6_.refs_4_, ...), custom_call_target="tpu_custom_call" | custom-call | tf_op jit(solution)/shard_map/pallas_call | solution.py:96
  31.9 12.7 %collective-permute-done.2.refs_4_ = bf16[1,64,4096]{2,1,0:T(8,128)(2,1)} collective-permute-done((bf16[1,64,4096]{2,1,0:T(8,128)(2,1)}, bf16[1,64,4096]{2,1,0:T(8,128)(2,1)}, u32[]{:S(2)}, u32[]{:S(2)}) %collective-permute-start.2) | collective-permute-done | bytes 524320 | tf_op jit(solution)/shard_map/ppermute | solution.py:54
  44.6 0.0 collective-permute-done.refs_3_.refs_2_
  44.6 0.0 collective-permute-done.1.refs_2_.refs_1_
  44.6 1.5 %collective-permute-start.7 = (bf16[1,64,4096]{2,1,0:T(8,128)(2,1)}, bf16[1,64,4096]{2,1,0:T(8,128)(2,1)S(1)}, u32[]{:S(2)}, u32[]{:S(2)}) collective-permute-start(bf16[1,64,4096]{2,1,0:T(8,128)(2,1)} %collective-permute-done.2.refs_4_), channel_id=1, source_target_pairs={{0,2},{1,3},{2,0},{3,1},{4,6},{5,7},{6,4},{7,5},{8,10},{9,11},{10,... | collective-permute-start | bytes 1572872 | tf_op jit(solution)/shard_map/ppermute | solution.py:54
  46.1 0.0 collective-permute-start.9
  46.1 0.5 collective-permute-start.8
  46.6 0.4 collective-permute-start.6
  47.0 13.3 %shard_map.105 = f32[2,8,384]{2,1,0:T(8,128)S(1)} custom-call(s32[4]{0:T(128)S(1)} %add.57.ids_ref, f32[1,256]{1,0:T(1,128)S(1)} %copy-done.2, bf16[256,4096]{1,0:T(8,128)(2,1)S(1)} %copy-done.1, bf16[48,2048]{1,0:T(8,128)(2,1)S(1)} %pad_maximum_fusion.1.wtab_ref, bf16[48,2048]{1,0:T(8,128)(2,1)S(1)} %pad_maximum_fusion.dtab_ref, ...), custom_call_target="tpu_custom_call" | custom-call | flops 120795955200 | bytes 5242880 | tf_op jit(solution)/shard_map/pallas_call | solution.py:214
  60.3 0.0 collective-permute-done.7.refs_5_
  60.3 0.1 collective-permute-start.10
  60.4 9.4 %collective-permute-done.6.refs_4_ = bf16[1,64,4096]{2,1,0:T(8,128)(2,1)S(1)} collective-permute-done((bf16[1,64,4096]{2,1,0:T(8,128)(2,1)S(1)}, bf16[1,64,4096]{2,1,0:T(8,128)(2,1)S(1)}, u32[]{:S(2)}, u32[]{:S(2)}) %collective-permute-start.6) | collective-permute-done | bytes 524320 | tf_op jit(solution)/shard_map/ppermute | solution.py:54
  69.8 0.4 collective-permute-start.11
  70.2 0.0 collective-permute-start.12
  70.2 3.0 %collective-permute-done.8.refs_3_.refs_1_ = bf16[136,4096]{1,0:T(8,128)(2,1)S(1)} collective-permute-done((bf16[136,4096]{1,0:T(8,128)(2,1)}, bf16[136,4096]{1,0:T(8,128)(2,1)S(1)}, u32[]{:S(2)}, u32[]{:S(2)}) %collective-permute-start.8) | collective-permute-done | bytes 1114144 | tf_op jit(solution)/shard_map/ppermute | solution.py:54
  73.3 8.5 %shard_map.106 = f32[1,8,512]{2,1,0:T(8,128)S(1)} custom-call(s32[4]{0:T(128)S(1)} %add.57.ids_ref, f32[1,256]{1,0:T(1,128)S(1)} %copy-done.2, bf16[256,4096]{1,0:T(8,128)(2,1)S(1)} %copy-done.1, bf16[48,2048]{1,0:T(8,128)(2,1)S(1)} %pad_maximum_fusion.1.wtab_ref, bf16[48,2048]{1,0:T(8,128)(2,1)S(1)} %pad_maximum_fusion.dtab_ref, ...), custom_call_target="tpu_custom_call" | custom-call | flops 72477573120 | bytes 6291456 | tf_op jit(solution)/shard_map/pallas_call | solution.py:214
  81.8 0.0 copy-start.5
  81.8 7.0 %shard_map.107 = f32[2,8,128]{2,1,0:T(8,128)S(1)} custom-call(s32[4]{0:T(128)S(1)} %add.57.ids_ref, f32[1,256]{1,0:T(1,128)S(1)} %copy-done.2, bf16[256,4096]{1,0:T(8,128)(2,1)S(1)} %copy-done.1, bf16[48,2048]{1,0:T(8,128)(2,1)S(1)} %pad_maximum_fusion.1.wtab_ref, bf16[48,2048]{1,0:T(8,128)(2,1)S(1)} %pad_maximum_fusion.dtab_ref, ...), custom_call_target="tpu_custom_call" | custom-call | flops 48318382080 | bytes 3145728 | tf_op jit(solution)/shard_map/pallas_call | solution.py:214
  88.8 0.1 collective-permute-start.13
  89.0 1.8 %collective-permute-done.13.refs_7_ = bf16[1,64,4096]{2,1,0:T(8,128)(2,1)S(1)} collective-permute-done((bf16[1,64,4096]{2,1,0:T(8,128)(2,1)S(1)}, bf16[1,64,4096]{2,1,0:T(8,128)(2,1)S(1)}, u32[]{:S(2)}, u32[]{:S(2)}) %collective-permute-start.13) | collective-permute-done | bytes 524320 | tf_op jit(solution)/shard_map/ppermute | solution.py:54
  90.8 8.2 %shard_map.108 = f32[1,8,512]{2,1,0:T(8,128)S(1)} custom-call(s32[4]{0:T(128)S(1)} %add.57.ids_ref, f32[1,256]{1,0:T(1,128)S(1)} %copy-done.2, bf16[256,4096]{1,0:T(8,128)(2,1)S(1)} %copy-done.1, bf16[48,2048]{1,0:T(8,128)(2,1)S(1)} %pad_maximum_fusion.1.wtab_ref, bf16[48,2048]{1,0:T(8,128)(2,1)S(1)} %pad_maximum_fusion.dtab_ref, ...), custom_call_target="tpu_custom_call" | custom-call | flops 72477573120 | bytes 6291456 | tf_op jit(solution)/shard_map/pallas_call | solution.py:214
  99.1 6.5 %collective-permute-start.14 = (f32[4,4,128]{2,1,0:T(4,128)S(1)}, f32[4,4,128]{2,1,0:T(4,128)S(1)}, u32[]{:S(2)}, u32[]{:S(2)}) collective-permute-start(f32[4,4,128]{2,1,0:T(4,128)S(1)} %pad_maximum_fusion.2), channel_id=1, source_target_pairs={{0,12},{4,8},{8,4},{12,0},{16,28},{20,24},{24,20},{28,16},{1,13},{... | collective-permute-start | bytes 24584 | tf_op jit(solution)/shard_map/ppermute | solution.py:54
  105.6 5.9 %collective-permute-start.15 = (f32[4,4,128]{2,1,0:T(4,128)S(1)}, f32[4,4,128]{2,1,0:T(4,128)S(1)}, u32[]{:S(2)}, u32[]{:S(2)}) collective-permute-start(f32[4,4,128]{2,1,0:T(4,128)S(1)} %pad_maximum_fusion.3), channel_id=1, source_target_pairs={{0,4},{4,0},{8,12},{12,8},{16,20},{20,16},{24,28},{28,24},{1,5},{5... | collective-permute-start | bytes 24584 | tf_op jit(solution)/shard_map/ppermute | solution.py:54
  111.5 1.5 %collective-permute-start.16 = (f32[4,4,128]{2,1,0:T(4,128)S(1)}, f32[4,4,128]{2,1,0:T(4,128)S(1)}, u32[]{:S(2)}, u32[]{:S(2)}) collective-permute-start(f32[4,4,128]{2,1,0:T(4,128)S(1)} %pad_maximum_fusion.4), channel_id=1, source_target_pairs={{0,8},{4,12},{8,0},{12,4},{16,24},{20,28},{24,16},{28,20},{1,9},{5... | collective-permute-start | bytes 24584 | tf_op jit(solution)/shard_map/ppermute | solution.py:54
  113.0 0.2 collective-permute-done.15
  113.2 2.0 %collective-permute-done.16 = f32[4,4,128]{2,1,0:T(4,128)S(1)} collective-permute-done((f32[4,4,128]{2,1,0:T(4,128)S(1)}, f32[4,4,128]{2,1,0:T(4,128)S(1)}, u32[]{:S(2)}, u32[]{:S(2)}) %collective-permute-start.16) | collective-permute-done | bytes 8224 | tf_op jit(solution)/shard_map/ppermute | solution.py:54
  115.3 0.6 fusion.18
  115.8 0.6 pad_maximum_fusion.5
  (36 shorter events, 0.3 us)
Async XLA Ops:
  0.6 25.2 %collective-permute-start.3 = (bf16[2,64,4096]{2,1,0:T(8,128)(2,1)}, bf16[2,64,4096]{2,1,0:T(8,128)(2,1)S(1)}, u32[]{:S(2)}, u32[]{:S(2)}) collective-permute-start(bf16[2,64,4096]{2,1,0:T(8,128)(2,1)} %refs_2_.1), channel_id=1, source_target_pairs={{0,2},{1,3},{2,0},{3,1},{4,6},{5,7},{6,4},{7,5},{8,10},{9,11},{10,... | collective-permute-start | bytes 3145736 | tf_op jit(solution)/shard_map/ppermute | solution.py:54
  1.2 27.2 %collective-permute-start.4 = (bf16[2,64,4096]{2,1,0:T(8,128)(2,1)}, bf16[2,64,4096]{2,1,0:T(8,128)(2,1)}, u32[]{:S(2)}, u32[]{:S(2)}) collective-permute-start(bf16[2,64,4096]{2,1,0:T(8,128)(2,1)} %refs_2_.1), channel_id=1, source_target_pairs={{0,1},{1,0},{2,3},{3,2},{4,5},{5,4},{6,7},{7,6},{8,9},{9,8},{10,11... | collective-permute-start | bytes 3145736 | tf_op jit(solution)/shard_map/ppermute | solution.py:54
  1.9 6.3 %copy-start = (bf16[2,64,4096]{2,1,0:T(8,128)(2,1)S(1)}, bf16[2,64,4096]{2,1,0:T(8,128)(2,1)}, u32[]{:S(2)}) copy-start(bf16[2,64,4096]{2,1,0:T(8,128)(2,1)} %refs_2_.1) | copy-start | bytes 3145732
  5.0 20.8 %copy-start.4 = (f32[2048]{0:T(1024)S(1)}, f32[2048]{0:T(1024)}, u32[]{:S(2)}) copy-start(f32[2048]{0:T(1024)} %param.14) | copy-start | bytes 24580
  5.1 39.5 %collective-permute-start = (bf16[136,4096]{1,0:T(8,128)(2,1)S(1)}, bf16[136,4096]{1,0:T(8,128)(2,1)}, u32[]{:S(2)}, u32[]{:S(2)}) collective-permute-start(bf16[136,4096]{1,0:T(8,128)(2,1)S(1)} %fusion.1.refs_1_.refs_0_), channel_id=1, source_target_pairs={{0,4},{4,0},{8,12},{12,8},{16,20},{20,16},{24,28},{28,24},{1,5},{5... | collective-permute-start | bytes 3342344 | tf_op jit(solution)/shard_map/ppermute | solution.py:54
  6.6 37.9 %collective-permute-start.1 = (bf16[136,4096]{1,0:T(8,128)(2,1)S(1)}, bf16[136,4096]{1,0:T(8,128)(2,1)}, u32[]{:S(2)}, u32[]{:S(2)}) collective-permute-start(bf16[136,4096]{1,0:T(8,128)(2,1)S(1)} %fusion.1.refs_1_.refs_0_), channel_id=1, source_target_pairs={{0,8},{4,12},{8,0},{12,4},{16,24},{20,28},{24,16},{28,20},{1,9},{5... | collective-permute-start | bytes 3342344 | tf_op jit(solution)/shard_map/ppermute | solution.py:54
  9.3 35.2 %collective-permute-start.2 = (bf16[1,64,4096]{2,1,0:T(8,128)(2,1)}, bf16[1,64,4096]{2,1,0:T(8,128)(2,1)}, u32[]{:S(2)}, u32[]{:S(2)}) collective-permute-start(bf16[1,64,4096]{2,1,0:T(8,128)(2,1)} %get-tuple-element.69), channel_id=1, source_target_pairs={{0,16},{4,20},{8,24},{12,28},{16,0},{20,4},{24,8},{28,12},{1,17},{... | collective-permute-start | bytes 1572872 | tf_op jit(solution)/shard_map/ppermute | solution.py:54
  25.8 2.8 %collective-permute-start.5 = (bf16[2,64,4096]{2,1,0:T(8,128)(2,1)S(1)}, bf16[2,64,4096]{2,1,0:T(8,128)(2,1)}, u32[]{:S(2)}, u32[]{:S(2)}) collective-permute-start(bf16[2,64,4096]{2,1,0:T(8,128)(2,1)S(1)} %collective-permute-done.3.refs_1_.refs_5_.refs_3_), channel_id=1, source_target_pairs={{0,1},{1,0},{2,3},{3,2},{4,5},{5,4},{6,7},{7,6},{8,9},{9,8},{10,11... | collective-permute-start | bytes 3145736 | tf_op jit(solution)/shard_map/ppermute | solution.py:54
  28.4 18.1 %copy-start.3 = (bf16[1,64,4096]{2,1,0:T(8,128)(2,1)S(1)}, bf16[1,64,4096]{2,1,0:T(8,128)(2,1)}, u32[]{:S(2)}) copy-start(bf16[1,64,4096]{2,1,0:T(8,128)(2,1)} %get-tuple-element.24) | copy-start | bytes 1572868
  28.4 18.6 %copy-start.1 = (bf16[256,4096]{1,0:T(8,128)(2,1)S(1)}, bf16[256,4096]{1,0:T(8,128)(2,1)}, u32[]{:S(2)}) copy-start(bf16[256,4096]{1,0:T(8,128)(2,1)} %constant.76.clone.table_ref) | copy-start | bytes 6291460
  28.5 18.6 %copy-start.2 = (f32[1,256]{1,0:T(1,128)S(1)}, f32[1,256]{1,0:T(1,128)}, u32[]{:S(2)}) copy-start(f32[1,256]{1,0:T(1,128)} %constant.77.clone.label_ref) | copy-start | bytes 3076
  44.6 15.8 %collective-permute-start.7 = (bf16[1,64,4096]{2,1,0:T(8,128)(2,1)}, bf16[1,64,4096]{2,1,0:T(8,128)(2,1)S(1)}, u32[]{:S(2)}, u32[]{:S(2)}) collective-permute-start(bf16[1,64,4096]{2,1,0:T(8,128)(2,1)} %collective-permute-done.2.refs_4_), channel_id=1, source_target_pairs={{0,2},{1,3},{2,0},{3,1},{4,6},{5,7},{6,4},{7,5},{8,10},{9,11},{10,... | collective-permute-start | bytes 1572872 | tf_op jit(solution)/shard_map/ppermute | solution.py:54
  46.1 24.2 %collective-permute-start.9 = (bf16[1,64,4096]{2,1,0:T(8,128)(2,1)}, bf16[1,64,4096]{2,1,0:T(8,128)(2,1)S(1)}, u32[]{:S(2)}, u32[]{:S(2)}) collective-permute-start(bf16[1,64,4096]{2,1,0:T(8,128)(2,1)} %collective-permute-done.2.refs_4_), channel_id=1, source_target_pairs={{0,1},{1,0},{2,3},{3,2},{4,5},{5,4},{6,7},{7,6},{8,9},{9,8},{10,11... | collective-permute-start | bytes 1572872 | tf_op jit(solution)/shard_map/ppermute | solution.py:54
  46.1 27.2 %collective-permute-start.8 = (bf16[136,4096]{1,0:T(8,128)(2,1)}, bf16[136,4096]{1,0:T(8,128)(2,1)S(1)}, u32[]{:S(2)}, u32[]{:S(2)}) collective-permute-start(bf16[136,4096]{1,0:T(8,128)(2,1)} %collective-permute-done.1.refs_2_.refs_1_), channel_id=1, source_target_pairs={{0,4},{4,0},{8,12},{12,8},{16,20},{20,16},{24,28},{28,24},{1,5},{5... | collective-permute-start | bytes 3342344 | tf_op jit(solution)/shard_map/ppermute | solution.py:54
  46.6 23.3 %collective-permute-start.6 = (bf16[1,64,4096]{2,1,0:T(8,128)(2,1)S(1)}, bf16[1,64,4096]{2,1,0:T(8,128)(2,1)S(1)}, u32[]{:S(2)}, u32[]{:S(2)}) collective-permute-start(bf16[1,64,4096]{2,1,0:T(8,128)(2,1)S(1)} %copy-done.3), channel_id=1, source_target_pairs={{0,16},{4,20},{8,24},{12,28},{16,0},{20,4},{24,8},{28,12},{1,17},{... | collective-permute-start | bytes 1572872 | tf_op jit(solution)/shard_map/ppermute | solution.py:54
  60.3 9.9 %collective-permute-start.10 = (bf16[1,64,4096]{2,1,0:T(8,128)(2,1)S(1)}, bf16[1,64,4096]{2,1,0:T(8,128)(2,1)S(1)}, u32[]{:S(2)}, u32[]{:S(2)}) collective-permute-start(bf16[1,64,4096]{2,1,0:T(8,128)(2,1)S(1)} %collective-permute-done.7.refs_5_), channel_id=1, source_target_pairs={{0,1},{1,0},{2,3},{3,2},{4,5},{5,4},{6,7},{7,6},{8,9},{9,8},{10,11... | collective-permute-start | bytes 1572872 | tf_op jit(solution)/shard_map/ppermute | solution.py:54
  69.8 19.0 %collective-permute-start.11 = (bf16[1,64,4096]{2,1,0:T(8,128)(2,1)S(1)}, bf16[1,64,4096]{2,1,0:T(8,128)(2,1)S(1)}, u32[]{:S(2)}, u32[]{:S(2)}) collective-permute-start(bf16[1,64,4096]{2,1,0:T(8,128)(2,1)S(1)} %collective-permute-done.6.refs_4_), channel_id=1, source_target_pairs={{0,2},{1,3},{2,0},{3,1},{4,6},{5,7},{6,4},{7,5},{8,10},{9,11},{10,... | collective-permute-start | bytes 1572872 | tf_op jit(solution)/shard_map/ppermute | solution.py:54
  70.2 18.8 %collective-permute-start.12 = (bf16[1,64,4096]{2,1,0:T(8,128)(2,1)S(1)}, bf16[1,64,4096]{2,1,0:T(8,128)(2,1)S(1)}, u32[]{:S(2)}, u32[]{:S(2)}) collective-permute-start(bf16[1,64,4096]{2,1,0:T(8,128)(2,1)S(1)} %collective-permute-done.6.refs_4_), channel_id=1, source_target_pairs={{0,1},{1,0},{2,3},{3,2},{4,5},{5,4},{6,7},{7,6},{8,9},{9,8},{10,11... | collective-permute-start | bytes 1572872 | tf_op jit(solution)/shard_map/ppermute | solution.py:54
  81.8 7.1 %copy-start.5 = (s32[128,2]{0,1:T(2,128)S(1)}, s32[128,2]{0,1:T(2,128)}, u32[]{:S(2)}) copy-start(s32[128,2]{0,1:T(2,128)} %param.10) | copy-start | bytes 3076
  88.8 2.0 %collective-permute-start.13 = (bf16[1,64,4096]{2,1,0:T(8,128)(2,1)S(1)}, bf16[1,64,4096]{2,1,0:T(8,128)(2,1)S(1)}, u32[]{:S(2)}, u32[]{:S(2)}) collective-permute-start(bf16[1,64,4096]{2,1,0:T(8,128)(2,1)S(1)} %collective-permute-done.11.refs_5_), channel_id=1, source_target_pairs={{0,1},{1,0},{2,3},{3,2},{4,5},{5,4},{6,7},{7,6},{8,9},{9,8},{10,11... | collective-permute-start | bytes 1572872 | tf_op jit(solution)/shard_map/ppermute | solution.py:54
  99.1 13.9 %collective-permute-start.14 = (f32[4,4,128]{2,1,0:T(4,128)S(1)}, f32[4,4,128]{2,1,0:T(4,128)S(1)}, u32[]{:S(2)}, u32[]{:S(2)}) collective-permute-start(f32[4,4,128]{2,1,0:T(4,128)S(1)} %pad_maximum_fusion.2), channel_id=1, source_target_pairs={{0,12},{4,8},{8,4},{12,0},{16,28},{20,24},{24,20},{28,16},{1,13},{... | collective-permute-start | bytes 24584 | tf_op jit(solution)/shard_map/ppermute | solution.py:54
  105.6 7.6 %collective-permute-start.15 = (f32[4,4,128]{2,1,0:T(4,128)S(1)}, f32[4,4,128]{2,1,0:T(4,128)S(1)}, u32[]{:S(2)}, u32[]{:S(2)}) collective-permute-start(f32[4,4,128]{2,1,0:T(4,128)S(1)} %pad_maximum_fusion.3), channel_id=1, source_target_pairs={{0,4},{4,0},{8,12},{12,8},{16,20},{20,16},{24,28},{28,24},{1,5},{5... | collective-permute-start | bytes 24584 | tf_op jit(solution)/shard_map/ppermute | solution.py:54
  111.5 3.7 %collective-permute-start.16 = (f32[4,4,128]{2,1,0:T(4,128)S(1)}, f32[4,4,128]{2,1,0:T(4,128)S(1)}, u32[]{:S(2)}, u32[]{:S(2)}) collective-permute-start(f32[4,4,128]{2,1,0:T(4,128)S(1)} %pad_maximum_fusion.4), channel_id=1, source_target_pairs={{0,8},{4,12},{8,0},{12,4},{16,24},{20,28},{24,16},{28,20},{1,9},{5... | collective-permute-start | bytes 24584 | tf_op jit(solution)/shard_map/ppermute | solution.py:54

commit v7 on v6

--- a/solution.py
+++ b/solution.py
@@ -14,6 +14,7 @@
 REACH = 3
 SHARE = 4
 TILE = 32
+HALF = 16
 CHUNK = 512
 PIECE = 256
 HIGHEST = lax.Precision.HIGHEST
@@ -102,7 +103,7 @@
     )(dtab, *pieces)
 
 
-def stats_kernel(trans, jobs, pieces, share, have_penalty, ids_ref, label_ref, table_ref, wtab_ref,
+def stats_kernel(trans, jobs, pieces, share, size, have_penalty, ids_ref, label_ref, table_ref, wtab_ref,
                  dtab_ref, *refs):
     if have_penalty:
         penalty_ref, refs = refs[0], refs[1:]
@@ -138,7 +139,7 @@
         ahead = jnp.dot(jnp.broadcast_to(names, (16, rows_all)).astype(jnp.bfloat16), upper,
                         preferred_element_type=jnp.float32)[:1]
         rank = jnp.where(names > 0.0, ahead - 1.0, -1.0).astype(jnp.int32)
-        tiles = (jnp.max(ahead).astype(jnp.int32) + (TILE - 1)) // TILE
+        tiles = (jnp.max(ahead).astype(jnp.int32) + (size - 1)) // size
 
         row = lax.broadcasted_iota(jnp.int32, (slots, rows_all), 0)
         pick = jnp.where(rank == row, 1.0, 0.0).astype(jnp.bfloat16)
@@ -158,32 +159,32 @@
 
         @pl.loop(0, tiles)
         def _(tile):
-            mine = pl.ds(pl.multiple_of(tile * TILE, TILE), TILE)
+            mine = pl.ds(pl.multiple_of(tile * size, size), size)
             here = info[mine, :]
             hot = jnp.concatenate(
                 [jnp.where(here[:, t:t + 1] == label, 1.0, 0.0) for t in range(trans)], axis=0
             ).astype(jnp.bfloat16)
-            scores = jnp.zeros((trans * TILE, ori), jnp.float32)
+            scores = jnp.zeros((trans * size, ori), jnp.float32)
             for first in range(0, pixels, PIECE):
                 cols = slice(first, first + PIECE)
                 icols = slice(pixels + first, pixels + first + PIECE)
                 cosine = jnp.dot(hot, table_ref[:, cols], preferred_element_type=jnp.float32)
                 sine = jnp.dot(hot, table_ref[:, icols], preferred_element_type=jnp.float32)
-                cosine = cosine.reshape(trans, TILE, PIECE)
-                sine = sine.reshape(trans, TILE, PIECE)
+                cosine = cosine.reshape(trans, size, PIECE)
+                sine = sine.reshape(trans, size, PIECE)
                 real = uv[mine, cols][None]
                 imag = uv[mine, icols][None]
                 shift_re = (real * cosine + imag * sine).astype(jnp.bfloat16)
                 shift_im = (imag * cosine - real * sine).astype(jnp.bfloat16)
-                scores += lax.dot_general(shift_re.reshape(trans * TILE, PIECE), views(cols), contract_last,
+                scores += lax.dot_general(shift_re.reshape(trans * size, PIECE), views(cols), contract_last,
                                           preferred_element_type=jnp.float32)
-                scores += lax.dot_general(shift_im.reshape(trans * TILE, PIECE), views(icols), contract_last,
+                scores += lax.dot_general(shift_im.reshape(trans * size, PIECE), views(icols), contract_last,
                                           preferred_element_type=jnp.float32)
-            full = scores.reshape(trans, TILE, ori) + pens[mine, :][None]
+            full = scores.reshape(trans, size, ori) + pens[mine, :][None]
             highest = jnp.max(jnp.max(full, axis=0), axis=1, keepdims=True)
-            total = jnp.zeros((TILE, ori), jnp.float32)
-            moment_x = jnp.zeros((TILE, ori), jnp.float32)
-            moment_y = jnp.zeros((TILE, ori), jnp.float32)
+            total = jnp.zeros((size, ori), jnp.float32)
+            moment_x = jnp.zeros((size, ori), jnp.float32)
+            moment_y = jnp.zeros((size, ori), jnp.float32)
             for t in range(trans):
                 term = jnp.exp(full[t] - highest)
                 total += term
@@ -192,7 +193,7 @@
             total = jnp.sum(total, axis=1, keepdims=True)
             moment_x = jnp.sum(moment_x, axis=1, keepdims=True)
             moment_y = jnp.sum(moment_y, axis=1, keepdims=True)
-            lanes = lax.broadcasted_iota(jnp.int32, (TILE, 128), 1)
+            lanes = lax.broadcasted_iota(jnp.int32, (size, 128), 1)
             stats[mine, :] = jnp.where(
                 lanes == 0, highest,
                 jnp.where(lanes == 1, total, jnp.where(lanes == 2, moment_x,
@@ -212,7 +213,8 @@
     extra = [] if penalty is None else [penalty]
     vmem = pl.BlockSpec(memory_space=pltpu.VMEM)
     return pl.pallas_call(
-        functools.partial(stats_kernel, trans, jobs, len(q_parts), len(x_parts), penalty is not None),
+        functools.partial(stats_kernel, trans, jobs, len(q_parts), len(x_parts), HALF if len(x_parts) == 1 else TILE,
+                          penalty is not None),
         out_shape=jax.ShapeDtypeStruct((len(jobs), 8, rows_all), jnp.float32),
         in_specs=[pl.BlockSpec(memory_space=pltpu.SMEM)]
         + [vmem] * (4 + len(extra) + len(x_parts) + len(q_parts)),
@@ -223,7 +225,7 @@
             pltpu.VMEM((slots, features), jnp.float32),
             pltpu.VMEM((slots, 128), jnp.float32),
         ],
-        compiler_params=pltpu.CompilerParams(vmem_limit_bytes=28 * 1024 * 1024),
+        compiler_params=pltpu.CompilerParams(vmem_limit_bytes=20 * 1024 * 1024),
         cost_estimate=pl.CostEstimate(
             flops=20 * len(jobs) * slots * trans * width * (ori + 256),
             bytes_accessed=(rows_all + ori) * width * 2,

time: 118 us -> 118 us (level)
  the two profiles are of different devices: /device:TPU:18 before, /device:TPU:0 now
where the time goes in v7:
time: 118 us
  Pallas kernels  49.9 us (42%)
  waiting for transfers between devices  40.1 us (34%)
  starting transfers between devices  18.1 us (15%)
  other arithmetic  7.29 us (6%)
  local copies, waits for them, and re-layouts  1.57 us (1%)
    pallas_call x4, Pallas kernels, class_stats(): pl.pallas_call(functools.partial(stats_kernel, trans, jobs, len(q_parts),...  46.6 us
    ppermute x17, waiting for transfers between devices, swap(): lax.ppermute(values, axis, [(index, index ^ bit) for index in range(count)])  40.1 us
    ppermute x17, starting transfers between devices, swap(): lax.ppermute(values, axis, [(index, index ^ bit) for index in range(count)])  18.1 us
    pallas_call x1, Pallas kernels, own_penalties(): pl.pallas_call(functools.partial(penalty_kernel, len(pieces)), out_shape=...  3.27 us
  transfers between devices with their start and end apart: 17, of which 8 were waited for; matrix products, arithmetic and copies ran while one was open for 6% of the time, Pallas kernels for 37%

profile of v7, /device:TPU:0, one launch (start us, length us, event | category | flops | bytes accessed | tf_op | source)
XLA Modules:
  0.0 117.8 jit_solution(8136259752417036225)
XLA Ops:
  0.6 3.0 %collective-permute-start.3 = (bf16[2,64,4096]{2,1,0:T(8,128)(2,1)}, bf16[2,64,4096]{2,1,0:T(8,128)(2,1)S(1)}, u32[]{:S(2)}, u32[]{:S(2)}) collective-permute-start(bf16[2,64,4096]{2,1,0:T(8,128)(2,1)} %refs_2_.1), channel_id=1, source_target_pairs={{0,2},{1,3},{2,0},{3,1},{4,6},{5,7},{6,4},{7,5},{8,10},{9,11},{10,... | collective-permute-start | bytes 3145736 | tf_op jit(solution)/shard_map/ppermute | solution.py:55
  3.6 0.0 collective-permute-start.4
  3.6 0.7 fusion.6
  4.4 0.7 convert_bitcast_fusion
  5.1 0.7 fusion.16
  5.8 0.3 concatenate.25
  6.1 1.3 %fusion.1.refs_1_.refs_0_ = bf16[136,4096]{1,0:T(8,128)(2,1)S(1)} fusion(bf16[8,512]{1,0:T(8,128)(2,1)S(1)} %pad_bitcast_fusion, bf16[128,4096]{1,0:T(8,128)(2,1)} %param.9), kind=kLoop, calls=%fused_computation.2 | loop fusion | flops 3342336 | bytes 2170880 | tf_op jit(solution)/shard_map/concatenate | solution.py:271
  7.4 0.0 copy-start.4
  7.5 1.6 %collective-permute-start = (bf16[136,4096]{1,0:T(8,128)(2,1)S(1)}, bf16[136,4096]{1,0:T(8,128)(2,1)}, u32[]{:S(2)}, u32[]{:S(2)}) collective-permute-start(bf16[136,4096]{1,0:T(8,128)(2,1)S(1)} %fusion.1.refs_1_.refs_0_), channel_id=1, source_target_pairs={{0,4},{4,0},{8,12},{12,8},{16,20},{20,16},{24,28},{28,24},{1,5},{5... | collective-permute-start | bytes 3342344 | tf_op jit(solution)/shard_map/ppermute | solution.py:55
  9.0 1.6 %collective-permute-start.1 = (bf16[136,4096]{1,0:T(8,128)(2,1)S(1)}, bf16[136,4096]{1,0:T(8,128)(2,1)}, u32[]{:S(2)}, u32[]{:S(2)}) collective-permute-start(bf16[136,4096]{1,0:T(8,128)(2,1)S(1)} %fusion.1.refs_1_.refs_0_), channel_id=1, source_target_pairs={{0,8},{4,12},{8,0},{12,4},{16,24},{20,28},{24,16},{28,20},{1,9},{5... | collective-permute-start | bytes 3342344 | tf_op jit(solution)/shard_map/ppermute | solution.py:55
  10.6 1.1 fusion.33
  11.7 2.6 %collective-permute-start.2 = (bf16[1,64,4096]{2,1,0:T(8,128)(2,1)}, bf16[1,64,4096]{2,1,0:T(8,128)(2,1)}, u32[]{:S(2)}, u32[]{:S(2)}) collective-permute-start(bf16[1,64,4096]{2,1,0:T(8,128)(2,1)} %get-tuple-element.69), channel_id=1, source_target_pairs={{0,16},{4,20},{8,24},{12,28},{16,0},{20,4},{24,8},{28,12},{1,17},{... | collective-permute-start | bytes 1572872 | tf_op jit(solution)/shard_map/ppermute | solution.py:55
  14.3 12.7 %collective-permute-done.3.refs_1_.refs_5_.refs_3_ = bf16[2,64,4096]{2,1,0:T(8,128)(2,1)S(1)} collective-permute-done((bf16[2,64,4096]{2,1,0:T(8,128)(2,1)}, bf16[2,64,4096]{2,1,0:T(8,128)(2,1)S(1)}, u32[]{:S(2)}, u32[]{:S(2)}) %collective-permute-start.3) | collective-permute-done | bytes 1048608 | tf_op jit(solution)/shard_map/ppermute | solution.py:55
  27.0 1.6 %reduce-precision_convert_fusion.1 = (bf16[16,2048]{1,0:T(8,128)(2,1)S(1)}, bf16[16,2048]{1,0:T(8,128)(2,1)S(1)}, bf16[16,2048]{1,0:T(8,128)(2,1)S(1)}, bf16[16,...) fusion(f32[16,2048]{1,0:T(8,128)} %param.13, f32[2048]{0:T(1024)S(1)} %copy-done.4), kind=kLoop, calls=%fused_computation.8 | loop fusion | flops 589824 | bytes 532480 | tf_op jit(solution)/shard_map/convert_element_type | solution.py:27
  28.6 0.1 iota_add_fusion
  28.7 0.1 add.57.ids_ref
  28.8 0.9 pad_maximum_fusion.dtab_ref
  29.6 0.0 copy-start.1
  29.7 0.0 copy-start.2
  29.7 0.1 collective-permute-done.5.refs_3_.refs_7_.refs_5_
  29.8 3.3 %shard_map.104.refs_0_ = f32[2,16,256]{2,1,0:T(8,128)S(1)} custom-call(bf16[48,2048]{1,0:T(8,128)(2,1)S(1)} %pad_maximum_fusion.dtab_ref, bf16[2,64,4096]{2,1,0:T(8,128)(2,1)S(1)} %copy-done, bf16[2,64,4096]{2,1,0:T(8,128)(2,1)S(1)} %collective-permute-done.3.refs_1_.refs_5_.refs_3_, bf16[2,64,4096]{2,1,0:T(8,128)(2,1)} %collective-permute-done.4.refs_2_.refs_6_.refs_4_, ...), custom_call_target="tpu_custom_call" | custom-call | tf_op jit(solution)/shard_map/pallas_call | solution.py:97
  33.1 13.1 %collective-permute-done.2.refs_4_ = bf16[1,64,4096]{2,1,0:T(8,128)(2,1)} collective-permute-done((bf16[1,64,4096]{2,1,0:T(8,128)(2,1)}, bf16[1,64,4096]{2,1,0:T(8,128)(2,1)}, u32[]{:S(2)}, u32[]{:S(2)}) %collective-permute-start.2) | collective-permute-done | bytes 524320 | tf_op jit(solution)/shard_map/ppermute | solution.py:55
  46.2 0.0 collective-permute-done.refs_3_.refs_2_
  46.2 0.9 collective-permute-done.1.refs_2_.refs_1_
  47.1 0.5 collective-permute-start.7
  47.6 0.0 collective-permute-start.9
  47.6 0.4 collective-permute-start.8
  48.0 2.6 %collective-permute-start.6 = (bf16[1,64,4096]{2,1,0:T(8,128)(2,1)S(1)}, bf16[1,64,4096]{2,1,0:T(8,128)(2,1)S(1)}, u32[]{:S(2)}, u32[]{:S(2)}) collective-permute-start(bf16[1,64,4096]{2,1,0:T(8,128)(2,1)S(1)} %copy-done.3), channel_id=1, source_target_pairs={{0,16},{4,20},{8,24},{12,28},{16,0},{20,4},{24,8},{28,12},{1,17},{... | collective-permute-start | bytes 1572872 | tf_op jit(solution)/shard_map/ppermute | solution.py:55
  50.6 13.3 %shard_map.105 = f32[2,8,384]{2,1,0:T(8,128)S(1)} custom-call(s32[4]{0:T(128)S(1)} %add.57.ids_ref, f32[1,256]{1,0:T(1,128)S(1)} %copy-done.2, bf16[256,4096]{1,0:T(8,128)(2,1)S(1)} %copy-done.1, bf16[48,2048]{1,0:T(8,128)(2,1)S(1)} %pad_maximum_fusion.1.wtab_ref, bf16[48,2048]{1,0:T(8,128)(2,1)S(1)} %pad_maximum_fusion.dtab_ref, ...), custom_call_target="tpu_custom_call" | custom-call | flops 120795955200 | bytes 5242880 | tf_op jit(solution)/shard_map/pallas_call | solution.py:215
  63.9 0.1 collective-permute-start.10
  64.0 10.2 %collective-permute-done.6.refs_4_ = bf16[1,64,4096]{2,1,0:T(8,128)(2,1)S(1)} collective-permute-done((bf16[1,64,4096]{2,1,0:T(8,128)(2,1)S(1)}, bf16[1,64,4096]{2,1,0:T(8,128)(2,1)S(1)}, u32[]{:S(2)}, u32[]{:S(2)}) %collective-permute-start.6) | collective-permute-done | bytes 524320 | tf_op jit(solution)/shard_map/ppermute | solution.py:55
  74.2 1.6 %collective-permute-start.11 = (bf16[1,64,4096]{2,1,0:T(8,128)(2,1)S(1)}, bf16[1,64,4096]{2,1,0:T(8,128)(2,1)S(1)}, u32[]{:S(2)}, u32[]{:S(2)}) collective-permute-start(bf16[1,64,4096]{2,1,0:T(8,128)(2,1)S(1)} %collective-permute-done.6.refs_4_), channel_id=1, source_target_pairs={{0,2},{1,3},{2,0},{3,1},{4,6},{5,7},{6,4},{7,5},{8,10},{9,11},{10,... | collective-permute-start | bytes 1572872 | tf_op jit(solution)/shard_map/ppermute | solution.py:55
  75.8 0.0 collective-permute-done.9.refs_6_
  75.8 0.0 collective-permute-done.10.refs_7_
  75.8 16.4 %shard_map.106 = f32[1,8,512]{2,1,0:T(8,128)S(1)} custom-call(s32[4]{0:T(128)S(1)} %add.57.ids_ref, f32[1,256]{1,0:T(1,128)S(1)} %copy-done.2, bf16[256,4096]{1,0:T(8,128)(2,1)S(1)} %copy-done.1, bf16[48,2048]{1,0:T(8,128)(2,1)S(1)} %pad_maximum_fusion.1.wtab_ref, bf16[48,2048]{1,0:T(8,128)(2,1)S(1)} %pad_maximum_fusion.dtab_ref, ...), custom_call_target="tpu_custom_call" | custom-call | flops 72477573120 | bytes 6291456 | tf_op jit(solution)/shard_map/pallas_call | solution.py:215
  92.2 0.0 copy-start.5
  92.2 10.7 %shard_map.107 = f32[2,8,128]{2,1,0:T(8,128)S(1)} custom-call(s32[4]{0:T(128)S(1)} %add.57.ids_ref, f32[1,256]{1,0:T(1,128)S(1)} %copy-done.2, bf16[256,4096]{1,0:T(8,128)(2,1)S(1)} %copy-done.1, bf16[48,2048]{1,0:T(8,128)(2,1)S(1)} %pad_maximum_fusion.1.wtab_ref, bf16[48,2048]{1,0:T(8,128)(2,1)S(1)} %pad_maximum_fusion.dtab_ref, ...), custom_call_target="tpu_custom_call" | custom-call | flops 48318382080 | bytes 3145728 | tf_op jit(solution)/shard_map/pallas_call | solution.py:215
  103.0 0.0 collective-permute-done.11.refs_5_
  103.0 0.6 collective-permute-start.13
  103.6 1.5 %collective-permute-done.13.refs_7_ = bf16[1,64,4096]{2,1,0:T(8,128)(2,1)S(1)} collective-permute-done((bf16[1,64,4096]{2,1,0:T(8,128)(2,1)S(1)}, bf16[1,64,4096]{2,1,0:T(8,128)(2,1)S(1)}, u32[]{:S(2)}, u32[]{:S(2)}) %collective-permute-start.13) | collective-permute-done | bytes 524320 | tf_op jit(solution)/shard_map/ppermute | solution.py:55
  105.1 6.2 %shard_map.108 = f32[1,8,512]{2,1,0:T(8,128)S(1)} custom-call(s32[4]{0:T(128)S(1)} %add.57.ids_ref, f32[1,256]{1,0:T(1,128)S(1)} %copy-done.2, bf16[256,4096]{1,0:T(8,128)(2,1)S(1)} %copy-done.1, bf16[48,2048]{1,0:T(8,128)(2,1)S(1)} %pad_maximum_fusion.1.wtab_ref, bf16[48,2048]{1,0:T(8,128)(2,1)S(1)} %pad_maximum_fusion.dtab_ref, ...), custom_call_target="tpu_custom_call" | custom-call | flops 72477573120 | bytes 6291456 | tf_op jit(solution)/shard_map/pallas_call | solution.py:215
  111.4 0.1 collective-permute-start.14
  111.4 0.1 collective-permute-start.15
  111.5 3.4 %collective-permute-start.16 = (f32[4,4,128]{2,1,0:T(4,128)S(1)}, f32[4,4,128]{2,1,0:T(4,128)S(1)}, u32[]{:S(2)}, u32[]{:S(2)}) collective-permute-start(f32[4,4,128]{2,1,0:T(4,128)S(1)} %pad_maximum_fusion.4), channel_id=1, source_target_pairs={{0,8},{4,12},{8,0},{12,4},{16,24},{20,28},{24,16},{28,20},{1,9},{5... | collective-permute-start | bytes 24584 | tf_op jit(solution)/shard_map/ppermute | solution.py:55
  114.9 1.0 collective-permute-done.14
  116.0 0.6 collective-permute-done.16
  116.6 0.6 fusion.18
  117.2 0.6 pad_maximum_fusion.5
  (36 shorter events, 0.2 us)
Async XLA Ops:
  0.6 26.4 %collective-permute-start.3 = (bf16[2,64,4096]{2,1,0:T(8,128)(2,1)}, bf16[2,64,4096]{2,1,0:T(8,128)(2,1)S(1)}, u32[]{:S(2)}, u32[]{:S(2)}) collective-permute-start(bf16[2,64,4096]{2,1,0:T(8,128)(2,1)} %refs_2_.1), channel_id=1, source_target_pairs={{0,2},{1,3},{2,0},{3,1},{4,6},{5,7},{6,4},{7,5},{8,10},{9,11},{10,... | collective-permute-start | bytes 3145736 | tf_op jit(solution)/shard_map/ppermute | solution.py:55
  3.6 26.0 %collective-permute-start.4 = (bf16[2,64,4096]{2,1,0:T(8,128)(2,1)}, bf16[2,64,4096]{2,1,0:T(8,128)(2,1)}, u32[]{:S(2)}, u32[]{:S(2)}) collective-permute-start(bf16[2,64,4096]{2,1,0:T(8,128)(2,1)} %refs_2_.1), channel_id=1, source_target_pairs={{0,1},{1,0},{2,3},{3,2},{4,5},{5,4},{6,7},{7,6},{8,9},{9,8},{10,11... | collective-permute-start | bytes 3145736 | tf_op jit(solution)/shard_map/ppermute | solution.py:55
  4.3 6.3 %copy-start = (bf16[2,64,4096]{2,1,0:T(8,128)(2,1)S(1)}, bf16[2,64,4096]{2,1,0:T(8,128)(2,1)}, u32[]{:S(2)}) copy-start(bf16[2,64,4096]{2,1,0:T(8,128)(2,1)} %refs_2_.1) | copy-start | bytes 3145732
  7.4 19.6 %copy-start.4 = (f32[2048]{0:T(1024)S(1)}, f32[2048]{0:T(1024)}, u32[]{:S(2)}) copy-start(f32[2048]{0:T(1024)} %param.14) | copy-start | bytes 24580
  7.5 38.7 %collective-permute-start = (bf16[136,4096]{1,0:T(8,128)(2,1)S(1)}, bf16[136,4096]{1,0:T(8,128)(2,1)}, u32[]{:S(2)}, u32[]{:S(2)}) collective-permute-start(bf16[136,4096]{1,0:T(8,128)(2,1)S(1)} %fusion.1.refs_1_.refs_0_), channel_id=1, source_target_pairs={{0,4},{4,0},{8,12},{12,8},{16,20},{20,16},{24,28},{28,24},{1,5},{5... | collective-permute-start | bytes 3342344 | tf_op jit(solution)/shard_map/ppermute | solution.py:55
  9.0 38.0 %collective-permute-start.1 = (bf16[136,4096]{1,0:T(8,128)(2,1)S(1)}, bf16[136,4096]{1,0:T(8,128)(2,1)}, u32[]{:S(2)}, u32[]{:S(2)}) collective-permute-start(bf16[136,4096]{1,0:T(8,128)(2,1)S(1)} %fusion.1.refs_1_.refs_0_), channel_id=1, source_target_pairs={{0,8},{4,12},{8,0},{12,4},{16,24},{20,28},{24,16},{28,20},{1,9},{5... | collective-permute-start | bytes 3342344 | tf_op jit(solution)/shard_map/ppermute | solution.py:55
  11.7 34.5 %collective-permute-start.2 = (bf16[1,64,4096]{2,1,0:T(8,128)(2,1)}, bf16[1,64,4096]{2,1,0:T(8,128)(2,1)}, u32[]{:S(2)}, u32[]{:S(2)}) collective-permute-start(bf16[1,64,4096]{2,1,0:T(8,128)(2,1)} %get-tuple-element.69), channel_id=1, source_target_pairs={{0,16},{4,20},{8,24},{12,28},{16,0},{20,4},{24,8},{28,12},{1,17},{... | collective-permute-start | bytes 1572872 | tf_op jit(solution)/shard_map/ppermute | solution.py:55
  27.0 2.8 %collective-permute-start.5 = (bf16[2,64,4096]{2,1,0:T(8,128)(2,1)S(1)}, bf16[2,64,4096]{2,1,0:T(8,128)(2,1)}, u32[]{:S(2)}, u32[]{:S(2)}) collective-permute-start(bf16[2,64,4096]{2,1,0:T(8,128)(2,1)S(1)} %collective-permute-done.3.refs_1_.refs_5_.refs_3_), channel_id=1, source_target_pairs={{0,1},{1,0},{2,3},{3,2},{4,5},{5,4},{6,7},{7,6},{8,9},{9,8},{10,11... | collective-permute-start | bytes 3145736 | tf_op jit(solution)/shard_map/ppermute | solution.py:55
  29.6 18.4 %copy-start.3 = (bf16[1,64,4096]{2,1,0:T(8,128)(2,1)S(1)}, bf16[1,64,4096]{2,1,0:T(8,128)(2,1)}, u32[]{:S(2)}) copy-start(bf16[1,64,4096]{2,1,0:T(8,128)(2,1)} %get-tuple-element.24) | copy-start | bytes 1572868
  29.6 21.0 %copy-start.1 = (bf16[256,4096]{1,0:T(8,128)(2,1)S(1)}, bf16[256,4096]{1,0:T(8,128)(2,1)}, u32[]{:S(2)}) copy-start(bf16[256,4096]{1,0:T(8,128)(2,1)} %constant.76.clone.table_ref) | copy-start | bytes 6291460
  29.7 21.0 %copy-start.2 = (f32[1,256]{1,0:T(1,128)S(1)}, f32[1,256]{1,0:T(1,128)}, u32[]{:S(2)}) copy-start(f32[1,256]{1,0:T(1,128)} %constant.77.clone.label_ref) | copy-start | bytes 3076
  47.1 16.8 %collective-permute-start.7 = (bf16[1,64,4096]{2,1,0:T(8,128)(2,1)}, bf16[1,64,4096]{2,1,0:T(8,128)(2,1)S(1)}, u32[]{:S(2)}, u32[]{:S(2)}) collective-permute-start(bf16[1,64,4096]{2,1,0:T(8,128)(2,1)} %collective-permute-done.2.refs_4_), channel_id=1, source_target_pairs={{0,2},{1,3},{2,0},{3,1},{4,6},{5,7},{6,4},{7,5},{8,10},{9,11},{10,... | collective-permute-start | bytes 1572872 | tf_op jit(solution)/shard_map/ppermute | solution.py:55
  47.6 28.2 %collective-permute-start.9 = (bf16[1,64,4096]{2,1,0:T(8,128)(2,1)}, bf16[1,64,4096]{2,1,0:T(8,128)(2,1)S(1)}, u32[]{:S(2)}, u32[]{:S(2)}) collective-permute-start(bf16[1,64,4096]{2,1,0:T(8,128)(2,1)} %collective-permute-done.2.refs_4_), channel_id=1, source_target_pairs={{0,1},{1,0},{2,3},{3,2},{4,5},{5,4},{6,7},{7,6},{8,9},{9,8},{10,11... | collective-permute-start | bytes 1572872 | tf_op jit(solution)/shard_map/ppermute | solution.py:55
  47.6 28.2 %collective-permute-start.8 = (bf16[136,4096]{1,0:T(8,128)(2,1)}, bf16[136,4096]{1,0:T(8,128)(2,1)S(1)}, u32[]{:S(2)}, u32[]{:S(2)}) collective-permute-start(bf16[136,4096]{1,0:T(8,128)(2,1)} %collective-permute-done.1.refs_2_.refs_1_), channel_id=1, source_target_pairs={{0,4},{4,0},{8,12},{12,8},{16,20},{20,16},{24,28},{28,24},{1,5},{5... | collective-permute-start | bytes 3342344 | tf_op jit(solution)/shard_map/ppermute | solution.py:55
  48.0 26.2 %collective-permute-start.6 = (bf16[1,64,4096]{2,1,0:T(8,128)(2,1)S(1)}, bf16[1,64,4096]{2,1,0:T(8,128)(2,1)S(1)}, u32[]{:S(2)}, u32[]{:S(2)}) collective-permute-start(bf16[1,64,4096]{2,1,0:T(8,128)(2,1)S(1)} %copy-done.3), channel_id=1, source_target_pairs={{0,16},{4,20},{8,24},{12,28},{16,0},{20,4},{24,8},{28,12},{1,17},{... | collective-permute-start | bytes 1572872 | tf_op jit(solution)/shard_map/ppermute | solution.py:55
  63.9 11.9 %collective-permute-start.10 = (bf16[1,64,4096]{2,1,0:T(8,128)(2,1)S(1)}, bf16[1,64,4096]{2,1,0:T(8,128)(2,1)S(1)}, u32[]{:S(2)}, u32[]{:S(2)}) collective-permute-start(bf16[1,64,4096]{2,1,0:T(8,128)(2,1)S(1)} %collective-permute-done.7.refs_5_), channel_id=1, source_target_pairs={{0,1},{1,0},{2,3},{3,2},{4,5},{5,4},{6,7},{7,6},{8,9},{9,8},{10,11... | collective-permute-start | bytes 1572872 | tf_op jit(solution)/shard_map/ppermute | solution.py:55
  74.2 28.8 %collective-permute-start.11 = (bf16[1,64,4096]{2,1,0:T(8,128)(2,1)S(1)}, bf16[1,64,4096]{2,1,0:T(8,128)(2,1)S(1)}, u32[]{:S(2)}, u32[]{:S(2)}) collective-permute-start(bf16[1,64,4096]{2,1,0:T(8,128)(2,1)S(1)} %collective-permute-done.6.refs_4_), channel_id=1, source_target_pairs={{0,2},{1,3},{2,0},{3,1},{4,6},{5,7},{6,4},{7,5},{8,10},{9,11},{10,... | collective-permute-start | bytes 1572872 | tf_op jit(solution)/shard_map/ppermute | solution.py:55
  75.8 27.8 %collective-permute-start.12 = (bf16[1,64,4096]{2,1,0:T(8,128)(2,1)S(1)}, bf16[1,64,4096]{2,1,0:T(8,128)(2,1)S(1)}, u32[]{:S(2)}, u32[]{:S(2)}) collective-permute-start(bf16[1,64,4096]{2,1,0:T(8,128)(2,1)S(1)} %collective-permute-done.6.refs_4_), channel_id=1, source_target_pairs={{0,1},{1,0},{2,3},{3,2},{4,5},{5,4},{6,7},{7,6},{8,9},{9,8},{10,11... | collective-permute-start | bytes 1572872 | tf_op jit(solution)/shard_map/ppermute | solution.py:55
  92.2 11.3 %copy-start.5 = (s32[128,2]{0,1:T(2,128)S(1)}, s32[128,2]{0,1:T(2,128)}, u32[]{:S(2)}) copy-start(s32[128,2]{0,1:T(2,128)} %param.10) | copy-start | bytes 3076
  103.0 2.1 %collective-permute-start.13 = (bf16[1,64,4096]{2,1,0:T(8,128)(2,1)S(1)}, bf16[1,64,4096]{2,1,0:T(8,128)(2,1)S(1)}, u32[]{:S(2)}, u32[]{:S(2)}) collective-permute-start(bf16[1,64,4096]{2,1,0:T(8,128)(2,1)S(1)} %collective-permute-done.11.refs_5_), channel_id=1, source_target_pairs={{0,1},{1,0},{2,3},{3,2},{4,5},{5,4},{6,7},{7,6},{8,9},{9,8},{10,11... | collective-permute-start | bytes 1572872 | tf_op jit(solution)/shard_map/ppermute | solution.py:55
  111.4 4.6 %collective-permute-start.14 = (f32[4,4,128]{2,1,0:T(4,128)S(1)}, f32[4,4,128]{2,1,0:T(4,128)S(1)}, u32[]{:S(2)}, u32[]{:S(2)}) collective-permute-start(f32[4,4,128]{2,1,0:T(4,128)S(1)} %pad_maximum_fusion.2), channel_id=1, source_target_pairs={{0,12},{4,8},{8,4},{12,0},{16,28},{20,24},{24,20},{28,16},{1,13},{... | collective-permute-start | bytes 24584 | tf_op jit(solution)/shard_map/ppermute | solution.py:55
  111.4 4.5 %collective-permute-start.15 = (f32[4,4,128]{2,1,0:T(4,128)S(1)}, f32[4,4,128]{2,1,0:T(4,128)S(1)}, u32[]{:S(2)}, u32[]{:S(2)}) collective-permute-start(f32[4,4,128]{2,1,0:T(4,128)S(1)} %pad_maximum_fusion.3), channel_id=1, source_target_pairs={{0,4},{4,0},{8,12},{12,8},{16,20},{20,16},{24,28},{28,24},{1,5},{5... | collective-permute-start | bytes 24584 | tf_op jit(solution)/shard_map/ppermute | solution.py:55
  111.5 5.0 %collective-permute-start.16 = (f32[4,4,128]{2,1,0:T(4,128)S(1)}, f32[4,4,128]{2,1,0:T(4,128)S(1)}, u32[]{:S(2)}, u32[]{:S(2)}) collective-permute-start(f32[4,4,128]{2,1,0:T(4,128)S(1)} %pad_maximum_fusion.4), channel_id=1, source_target_pairs={{0,8},{4,12},{8,0},{12,4},{16,24},{20,28},{24,16},{28,20},{1,9},{5... | collective-permute-start | bytes 24584 | tf_op jit(solution)/shard_map/ppermute | solution.py:55

commit v8 on v7

--- a/solution.py
+++ b/solution.py
@@ -14,7 +14,6 @@
 REACH = 3
 SHARE = 4
 TILE = 32
-HALF = 16
 CHUNK = 512
 PIECE = 256
 HIGHEST = lax.Precision.HIGHEST
@@ -103,7 +102,7 @@
     )(dtab, *pieces)
 
 
-def stats_kernel(trans, jobs, pieces, share, size, have_penalty, ids_ref, label_ref, table_ref, wtab_ref,
+def stats_kernel(trans, jobs, pieces, share, have_penalty, ids_ref, label_ref, table_ref, wtab_ref,
                  dtab_ref, *refs):
     if have_penalty:
         penalty_ref, refs = refs[0], refs[1:]
@@ -139,7 +138,7 @@
         ahead = jnp.dot(jnp.broadcast_to(names, (16, rows_all)).astype(jnp.bfloat16), upper,
                         preferred_element_type=jnp.float32)[:1]
         rank = jnp.where(names > 0.0, ahead - 1.0, -1.0).astype(jnp.int32)
-        tiles = (jnp.max(ahead).astype(jnp.int32) + (size - 1)) // size
+        tiles = (jnp.max(ahead).astype(jnp.int32) + (TILE - 1)) // TILE
 
         row = lax.broadcasted_iota(jnp.int32, (slots, rows_all), 0)
         pick = jnp.where(rank == row, 1.0, 0.0).astype(jnp.bfloat16)
@@ -157,9 +156,8 @@
         pens[...] = jnp.dot(group_hot, jnp.concatenate(three(penalty), axis=0),
                             preferred_element_type=jnp.float32)
 
-        @pl.loop(0, tiles)
-        def _(tile):
-            mine = pl.ds(pl.multiple_of(tile * size, size), size)
+        def one_tile(start, size):
+            mine = pl.ds(pl.multiple_of(start, TILE), size)
             here = info[mine, :]
             hot = jnp.concatenate(
                 [jnp.where(here[:, t:t + 1] == label, 1.0, 0.0) for t in range(trans)], axis=0
@@ -199,6 +197,19 @@
                 jnp.where(lanes == 1, total, jnp.where(lanes == 2, moment_x,
                                                        jnp.where(lanes == 3, moment_y, 0.0))))
 
+        if share > 1 and slots >= 2 * TILE:
+            @pl.loop(0, tiles // 2)
+            def _(pair):
+                one_tile(pair * (2 * TILE), 2 * TILE)
+
+            @pl.when(tiles % 2 == 1)
+            def _():
+                one_tile((tiles - 1) * TILE, TILE)
+        else:
+            @pl.loop(0, tiles)
+            def _(tile):
+                one_tile(tile * TILE, TILE)
+
         back = sum(
             lax.dot_general(part, pick, (((0,), (0,)), ((), ())), preferred_element_type=jnp.float32)
             for part in three(stats[...])
@@ -213,8 +224,7 @@
     extra = [] if penalty is None else [penalty]
     vmem = pl.BlockSpec(memory_space=pltpu.VMEM)
     return pl.pallas_call(
-        functools.partial(stats_kernel, trans, jobs, len(q_parts), len(x_parts), HALF if len(x_parts) == 1 else TILE,
-                          penalty is not None),
+        functools.partial(stats_kernel, trans, jobs, len(q_parts), len(x_parts), penalty is not None),
         out_shape=jax.ShapeDtypeStruct((len(jobs), 8, rows_all), jnp.float32),
         in_specs=[pl.BlockSpec(memory_space=pltpu.SMEM)]
         + [vmem] * (4 + len(extra) + len(x_parts) + len(q_parts)),
@@ -225,7 +235,7 @@
             pltpu.VMEM((slots, features), jnp.float32),
             pltpu.VMEM((slots, 128), jnp.float32),
         ],
-        compiler_params=pltpu.CompilerParams(vmem_limit_bytes=20 * 1024 * 1024),
+        compiler_params=pltpu.CompilerParams(vmem_limit_bytes=28 * 1024 * 1024),
         cost_estimate=pl.CostEstimate(
             flops=20 * len(jobs) * slots * trans * width * (ori + 256),
             bytes_accessed=(rows_all + ori) * width * 2,

time: 118 us -> 115 us (0.975)
  Pallas kernels: 49.9 us -> 47.3 us
    pallas_call x4, Pallas kernels: 46.6 us -> 44 us  [class_stats(): pl.pallas_call(functools.partial(stats_kernel, trans, jobs, len(q_parts),...]
  transfers between devices with their start and end apart: 17 -> 17, of which waited for: 8 -> 8; matrix products, arithmetic and copies ran while one was open for 6% -> 7% of each run, Pallas kernels for 37% -> 36%
where the time goes in v8:
time: 115 us; the launch traced here: 114 us
  Pallas kernels  47.3 us (41%)
  waiting for transfers between devices  39.1 us (34%)
  starting transfers between devices  18.1 us (16%)
  other arithmetic  7.29 us (6%)
  local copies, waits for them, and re-layouts  1.57 us (1%)
    pallas_call x4, Pallas kernels, class_stats(): pl.pallas_call(functools.partial(stats_kernel, trans, jobs, len(q_parts),...  44 us
    ppermute x17, waiting for transfers between devices, swap(): lax.ppermute(values, axis, [(index, index ^ bit) for index in range(count)])  39.1 us
    ppermute x17, starting transfers between devices, swap(): lax.ppermute(values, axis, [(index, index ^ bit) for index in range(count)])  18.1 us
    pallas_call x1, Pallas kernels, own_penalties(): pl.pallas_call(functools.partial(penalty_kernel, len(pieces)), out_shape=...  3.27 us
  transfers between devices with their start and end apart: 17, of which 8 were waited for; matrix products, arithmetic and copies ran while one was open for 7% of the time, Pallas kernels for 36%

profile of v8, /device:TPU:0, one launch (start us, length us, event | category | flops | bytes accessed | tf_op | source)
XLA Modules:
  0.0 114.3 jit_solution(17018514504297390626)
XLA Ops:
  0.6 3.0 %collective-permute-start.3 = (bf16[2,64,4096]{2,1,0:T(8,128)(2,1)}, bf16[2,64,4096]{2,1,0:T(8,128)(2,1)S(1)}, u32[]{:S(2)}, u32[]{:S(2)}) collective-permute-start(bf16[2,64,4096]{2,1,0:T(8,128)(2,1)} %refs_2_.1), channel_id=1, source_target_pairs={{0,2},{1,3},{2,0},{3,1},{4,6},{5,7},{6,4},{7,5},{8,10},{9,11},{10,... | collective-permute-start | bytes 3145736 | tf_op jit(solution)/shard_map/ppermute | solution.py:54
  3.6 0.7 fusion.6
  4.4 0.7 convert_bitcast_fusion
  5.1 0.7 fusion.16
  5.8 0.3 concatenate.25
  6.1 1.3 %fusion.1.refs_1_.refs_0_ = bf16[136,4096]{1,0:T(8,128)(2,1)S(1)} fusion(bf16[8,512]{1,0:T(8,128)(2,1)S(1)} %pad_bitcast_fusion, bf16[128,4096]{1,0:T(8,128)(2,1)} %param.9), kind=kLoop, calls=%fused_computation.2 | loop fusion | flops 3342336 | bytes 2170880 | tf_op jit(solution)/shard_map/concatenate | solution.py:281
  7.4 0.0 copy-start.4
  7.5 1.6 %collective-permute-start = (bf16[136,4096]{1,0:T(8,128)(2,1)S(1)}, bf16[136,4096]{1,0:T(8,128)(2,1)}, u32[]{:S(2)}, u32[]{:S(2)}) collective-permute-start(bf16[136,4096]{1,0:T(8,128)(2,1)S(1)} %fusion.1.refs_1_.refs_0_), channel_id=1, source_target_pairs={{0,4},{4,0},{8,12},{12,8},{16,20},{20,16},{24,28},{28,24},{1,5},{5... | collective-permute-start | bytes 3342344 | tf_op jit(solution)/shard_map/ppermute | solution.py:54
  9.0 1.6 %collective-permute-start.1 = (bf16[136,4096]{1,0:T(8,128)(2,1)S(1)}, bf16[136,4096]{1,0:T(8,128)(2,1)}, u32[]{:S(2)}, u32[]{:S(2)}) collective-permute-start(bf16[136,4096]{1,0:T(8,128)(2,1)S(1)} %fusion.1.refs_1_.refs_0_), channel_id=1, source_target_pairs={{0,8},{4,12},{8,0},{12,4},{16,24},{20,28},{24,16},{28,20},{1,9},{5... | collective-permute-start | bytes 3342344 | tf_op jit(solution)/shard_map/ppermute | solution.py:54
  10.6 1.1 fusion.33
  11.7 2.6 %collective-permute-start.2 = (bf16[1,64,4096]{2,1,0:T(8,128)(2,1)}, bf16[1,64,4096]{2,1,0:T(8,128)(2,1)}, u32[]{:S(2)}, u32[]{:S(2)}) collective-permute-start(bf16[1,64,4096]{2,1,0:T(8,128)(2,1)} %get-tuple-element.69), channel_id=1, source_target_pairs={{0,16},{4,20},{8,24},{12,28},{16,0},{20,4},{24,8},{28,12},{1,17},{... | collective-permute-start | bytes 1572872 | tf_op jit(solution)/shard_map/ppermute | solution.py:54
  14.3 12.7 %collective-permute-done.3.refs_1_.refs_5_.refs_3_ = bf16[2,64,4096]{2,1,0:T(8,128)(2,1)S(1)} collective-permute-done((bf16[2,64,4096]{2,1,0:T(8,128)(2,1)}, bf16[2,64,4096]{2,1,0:T(8,128)(2,1)S(1)}, u32[]{:S(2)}, u32[]{:S(2)}) %collective-permute-start.3) | collective-permute-done | bytes 1048608 | tf_op jit(solution)/shard_map/ppermute | solution.py:54
  27.0 1.6 %reduce-precision_convert_fusion.1 = (bf16[16,2048]{1,0:T(8,128)(2,1)S(1)}, bf16[16,2048]{1,0:T(8,128)(2,1)S(1)}, bf16[16,2048]{1,0:T(8,128)(2,1)S(1)}, bf16[16,...) fusion(f32[16,2048]{1,0:T(8,128)} %param.13, f32[2048]{0:T(1024)S(1)} %copy-done.4), kind=kLoop, calls=%fused_computation.8 | loop fusion | flops 589824 | bytes 532480 | tf_op jit(solution)/shard_map/convert_element_type | solution.py:26
  28.6 0.1 iota_add_fusion
  28.7 0.1 add.57.ids_ref
  28.8 0.9 pad_maximum_fusion.dtab_ref
  29.6 0.0 copy-start.1
  29.7 0.0 copy-start.2
  29.7 0.0 collective-permute-done.4.refs_2_.refs_6_.refs_4_
  29.7 0.1 collective-permute-done.5.refs_3_.refs_7_.refs_5_
  29.8 3.3 %shard_map.104.refs_0_ = f32[2,16,256]{2,1,0:T(8,128)S(1)} custom-call(bf16[48,2048]{1,0:T(8,128)(2,1)S(1)} %pad_maximum_fusion.dtab_ref, bf16[2,64,4096]{2,1,0:T(8,128)(2,1)S(1)} %copy-done, bf16[2,64,4096]{2,1,0:T(8,128)(2,1)S(1)} %collective-permute-done.3.refs_1_.refs_5_.refs_3_, bf16[2,64,4096]{2,1,0:T(8,128)(2,1)} %collective-permute-done.4.refs_2_.refs_6_.refs_4_, ...), custom_call_target="tpu_custom_call" | custom-call | tf_op jit(solution)/shard_map/pallas_call | solution.py:96
  33.1 13.1 %collective-permute-done.2.refs_4_ = bf16[1,64,4096]{2,1,0:T(8,128)(2,1)} collective-permute-done((bf16[1,64,4096]{2,1,0:T(8,128)(2,1)}, bf16[1,64,4096]{2,1,0:T(8,128)(2,1)}, u32[]{:S(2)}, u32[]{:S(2)}) %collective-permute-start.2) | collective-permute-done | bytes 524320 | tf_op jit(solution)/shard_map/ppermute | solution.py:54
  46.2 0.0 collective-permute-done.refs_3_.refs_2_
  46.2 0.9 collective-permute-done.1.refs_2_.refs_1_
  47.1 0.5 collective-permute-start.7
  47.6 0.0 collective-permute-start.9
  47.6 0.4 collective-permute-start.8
  48.0 2.6 %collective-permute-start.6 = (bf16[1,64,4096]{2,1,0:T(8,128)(2,1)S(1)}, bf16[1,64,4096]{2,1,0:T(8,128)(2,1)S(1)}, u32[]{:S(2)}, u32[]{:S(2)}) collective-permute-start(bf16[1,64,4096]{2,1,0:T(8,128)(2,1)S(1)} %copy-done.3), channel_id=1, source_target_pairs={{0,16},{4,20},{8,24},{12,28},{16,0},{20,4},{24,8},{28,12},{1,17},{... | collective-permute-start | bytes 1572872 | tf_op jit(solution)/shard_map/ppermute | solution.py:54
  50.6 14.2 %shard_map.105 = f32[2,8,384]{2,1,0:T(8,128)S(1)} custom-call(s32[4]{0:T(128)S(1)} %add.57.ids_ref, f32[1,256]{1,0:T(1,128)S(1)} %copy-done.2, bf16[256,4096]{1,0:T(8,128)(2,1)S(1)} %copy-done.1, bf16[48,2048]{1,0:T(8,128)(2,1)S(1)} %pad_maximum_fusion.1.wtab_ref, bf16[48,2048]{1,0:T(8,128)(2,1)S(1)} %pad_maximum_fusion.dtab_ref, ...), custom_call_target="tpu_custom_call" | custom-call | flops 120795955200 | bytes 5242880 | tf_op jit(solution)/shard_map/pallas_call | solution.py:226
  64.9 0.0 collective-permute-done.7.refs_5_
  64.9 0.1 collective-permute-start.10
  65.0 9.2 %collective-permute-done.6.refs_4_ = bf16[1,64,4096]{2,1,0:T(8,128)(2,1)S(1)} collective-permute-done((bf16[1,64,4096]{2,1,0:T(8,128)(2,1)S(1)}, bf16[1,64,4096]{2,1,0:T(8,128)(2,1)S(1)}, u32[]{:S(2)}, u32[]{:S(2)}) %collective-permute-start.6) | collective-permute-done | bytes 524320 | tf_op jit(solution)/shard_map/ppermute | solution.py:54
  74.2 1.6 %collective-permute-start.11 = (bf16[1,64,4096]{2,1,0:T(8,128)(2,1)S(1)}, bf16[1,64,4096]{2,1,0:T(8,128)(2,1)S(1)}, u32[]{:S(2)}, u32[]{:S(2)}) collective-permute-start(bf16[1,64,4096]{2,1,0:T(8,128)(2,1)S(1)} %collective-permute-done.6.refs_4_), channel_id=1, source_target_pairs={{0,2},{1,3},{2,0},{3,1},{4,6},{5,7},{6,4},{7,5},{8,10},{9,11},{10,... | collective-permute-start | bytes 1572872 | tf_op jit(solution)/shard_map/ppermute | solution.py:54
  75.8 0.0 collective-permute-start.12
  75.8 0.0 collective-permute-done.9.refs_6_
  75.8 14.6 %shard_map.106 = f32[1,8,512]{2,1,0:T(8,128)S(1)} custom-call(s32[4]{0:T(128)S(1)} %add.57.ids_ref, f32[1,256]{1,0:T(1,128)S(1)} %copy-done.2, bf16[256,4096]{1,0:T(8,128)(2,1)S(1)} %copy-done.1, bf16[48,2048]{1,0:T(8,128)(2,1)S(1)} %pad_maximum_fusion.1.wtab_ref, bf16[48,2048]{1,0:T(8,128)(2,1)S(1)} %pad_maximum_fusion.dtab_ref, ...), custom_call_target="tpu_custom_call" | custom-call | flops 72477573120 | bytes 6291456 | tf_op jit(solution)/shard_map/pallas_call | solution.py:226
  90.4 0.0 copy-start.5
  90.4 9.0 %shard_map.107 = f32[2,8,128]{2,1,0:T(8,128)S(1)} custom-call(s32[4]{0:T(128)S(1)} %add.57.ids_ref, f32[1,256]{1,0:T(1,128)S(1)} %copy-done.2, bf16[256,4096]{1,0:T(8,128)(2,1)S(1)} %copy-done.1, bf16[48,2048]{1,0:T(8,128)(2,1)S(1)} %pad_maximum_fusion.1.wtab_ref, bf16[48,2048]{1,0:T(8,128)(2,1)S(1)} %pad_maximum_fusion.dtab_ref, ...), custom_call_target="tpu_custom_call" | custom-call | flops 48318382080 | bytes 3145728 | tf_op jit(solution)/shard_map/pallas_call | solution.py:226
  99.4 0.6 collective-permute-start.13
  100.1 1.5 %collective-permute-done.13.refs_7_ = bf16[1,64,4096]{2,1,0:T(8,128)(2,1)S(1)} collective-permute-done((bf16[1,64,4096]{2,1,0:T(8,128)(2,1)S(1)}, bf16[1,64,4096]{2,1,0:T(8,128)(2,1)S(1)}, u32[]{:S(2)}, u32[]{:S(2)}) %collective-permute-start.13) | collective-permute-done | bytes 524320 | tf_op jit(solution)/shard_map/ppermute | solution.py:54
  101.5 6.2 %shard_map.108 = f32[1,8,512]{2,1,0:T(8,128)S(1)} custom-call(s32[4]{0:T(128)S(1)} %add.57.ids_ref, f32[1,256]{1,0:T(1,128)S(1)} %copy-done.2, bf16[256,4096]{1,0:T(8,128)(2,1)S(1)} %copy-done.1, bf16[48,2048]{1,0:T(8,128)(2,1)S(1)} %pad_maximum_fusion.1.wtab_ref, bf16[48,2048]{1,0:T(8,128)(2,1)S(1)} %pad_maximum_fusion.dtab_ref, ...), custom_call_target="tpu_custom_call" | custom-call | flops 72477573120 | bytes 6291456 | tf_op jit(solution)/shard_map/pallas_call | solution.py:226
  107.9 0.1 collective-permute-start.14
  108.0 0.1 collective-permute-start.15
  108.0 3.4 %collective-permute-start.16 = (f32[4,4,128]{2,1,0:T(4,128)S(1)}, f32[4,4,128]{2,1,0:T(4,128)S(1)}, u32[]{:S(2)}, u32[]{:S(2)}) collective-permute-start(f32[4,4,128]{2,1,0:T(4,128)S(1)} %pad_maximum_fusion.4), channel_id=1, source_target_pairs={{0,8},{4,12},{8,0},{12,4},{16,24},{20,28},{24,16},{28,20},{1,9},{5... | collective-permute-start | bytes 24584 | tf_op jit(solution)/shard_map/ppermute | solution.py:54
  111.4 1.1 collective-permute-done.14
  112.5 0.5 collective-permute-done.16
  113.1 0.6 fusion.18
  113.7 0.6 pad_maximum_fusion.5
  (36 shorter events, 0.2 us)
Async XLA Ops:
  0.6 26.4 %collective-permute-start.3 = (bf16[2,64,4096]{2,1,0:T(8,128)(2,1)}, bf16[2,64,4096]{2,1,0:T(8,128)(2,1)S(1)}, u32[]{:S(2)}, u32[]{:S(2)}) collective-permute-start(bf16[2,64,4096]{2,1,0:T(8,128)(2,1)} %refs_2_.1), channel_id=1, source_target_pairs={{0,2},{1,3},{2,0},{3,1},{4,6},{5,7},{6,4},{7,5},{8,10},{9,11},{10,... | collective-permute-start | bytes 3145736 | tf_op jit(solution)/shard_map/ppermute | solution.py:54
  3.6 26.0 %collective-permute-start.4 = (bf16[2,64,4096]{2,1,0:T(8,128)(2,1)}, bf16[2,64,4096]{2,1,0:T(8,128)(2,1)}, u32[]{:S(2)}, u32[]{:S(2)}) collective-permute-start(bf16[2,64,4096]{2,1,0:T(8,128)(2,1)} %refs_2_.1), channel_id=1, source_target_pairs={{0,1},{1,0},{2,3},{3,2},{4,5},{5,4},{6,7},{7,6},{8,9},{9,8},{10,11... | collective-permute-start | bytes 3145736 | tf_op jit(solution)/shard_map/ppermute | solution.py:54
  4.3 6.3 %copy-start = (bf16[2,64,4096]{2,1,0:T(8,128)(2,1)S(1)}, bf16[2,64,4096]{2,1,0:T(8,128)(2,1)}, u32[]{:S(2)}) copy-start(bf16[2,64,4096]{2,1,0:T(8,128)(2,1)} %refs_2_.1) | copy-start | bytes 3145732
  7.4 19.6 %copy-start.4 = (f32[2048]{0:T(1024)S(1)}, f32[2048]{0:T(1024)}, u32[]{:S(2)}) copy-start(f32[2048]{0:T(1024)} %param.14) | copy-start | bytes 24580
  7.5 38.7 %collective-permute-start = (bf16[136,4096]{1,0:T(8,128)(2,1)S(1)}, bf16[136,4096]{1,0:T(8,128)(2,1)}, u32[]{:S(2)}, u32[]{:S(2)}) collective-permute-start(bf16[136,4096]{1,0:T(8,128)(2,1)S(1)} %fusion.1.refs_1_.refs_0_), channel_id=1, source_target_pairs={{0,4},{4,0},{8,12},{12,8},{16,20},{20,16},{24,28},{28,24},{1,5},{5... | collective-permute-start | bytes 3342344 | tf_op jit(solution)/shard_map/ppermute | solution.py:54
  9.0 38.0 %collective-permute-start.1 = (bf16[136,4096]{1,0:T(8,128)(2,1)S(1)}, bf16[136,4096]{1,0:T(8,128)(2,1)}, u32[]{:S(2)}, u32[]{:S(2)}) collective-permute-start(bf16[136,4096]{1,0:T(8,128)(2,1)S(1)} %fusion.1.refs_1_.refs_0_), channel_id=1, source_target_pairs={{0,8},{4,12},{8,0},{12,4},{16,24},{20,28},{24,16},{28,20},{1,9},{5... | collective-permute-start | bytes 3342344 | tf_op jit(solution)/shard_map/ppermute | solution.py:54
  11.7 34.5 %collective-permute-start.2 = (bf16[1,64,4096]{2,1,0:T(8,128)(2,1)}, bf16[1,64,4096]{2,1,0:T(8,128)(2,1)}, u32[]{:S(2)}, u32[]{:S(2)}) collective-permute-start(bf16[1,64,4096]{2,1,0:T(8,128)(2,1)} %get-tuple-element.69), channel_id=1, source_target_pairs={{0,16},{4,20},{8,24},{12,28},{16,0},{20,4},{24,8},{28,12},{1,17},{... | collective-permute-start | bytes 1572872 | tf_op jit(solution)/shard_map/ppermute | solution.py:54
  27.0 2.8 %collective-permute-start.5 = (bf16[2,64,4096]{2,1,0:T(8,128)(2,1)S(1)}, bf16[2,64,4096]{2,1,0:T(8,128)(2,1)}, u32[]{:S(2)}, u32[]{:S(2)}) collective-permute-start(bf16[2,64,4096]{2,1,0:T(8,128)(2,1)S(1)} %collective-permute-done.3.refs_1_.refs_5_.refs_3_), channel_id=1, source_target_pairs={{0,1},{1,0},{2,3},{3,2},{4,5},{5,4},{6,7},{7,6},{8,9},{9,8},{10,11... | collective-permute-start | bytes 3145736 | tf_op jit(solution)/shard_map/ppermute | solution.py:54
  29.6 18.4 %copy-start.3 = (bf16[1,64,4096]{2,1,0:T(8,128)(2,1)S(1)}, bf16[1,64,4096]{2,1,0:T(8,128)(2,1)}, u32[]{:S(2)}) copy-start(bf16[1,64,4096]{2,1,0:T(8,128)(2,1)} %get-tuple-element.24) | copy-start | bytes 1572868
  29.6 21.0 %copy-start.1 = (bf16[256,4096]{1,0:T(8,128)(2,1)S(1)}, bf16[256,4096]{1,0:T(8,128)(2,1)}, u32[]{:S(2)}) copy-start(bf16[256,4096]{1,0:T(8,128)(2,1)} %constant.76.clone.table_ref) | copy-start | bytes 6291460
  29.7 21.0 %copy-start.2 = (f32[1,256]{1,0:T(1,128)S(1)}, f32[1,256]{1,0:T(1,128)}, u32[]{:S(2)}) copy-start(f32[1,256]{1,0:T(1,128)} %constant.77.clone.label_ref) | copy-start | bytes 3076
  47.1 17.8 %collective-permute-start.7 = (bf16[1,64,4096]{2,1,0:T(8,128)(2,1)}, bf16[1,64,4096]{2,1,0:T(8,128)(2,1)S(1)}, u32[]{:S(2)}, u32[]{:S(2)}) collective-permute-start(bf16[1,64,4096]{2,1,0:T(8,128)(2,1)} %collective-permute-done.2.refs_4_), channel_id=1, source_target_pairs={{0,2},{1,3},{2,0},{3,1},{4,6},{5,7},{6,4},{7,5},{8,10},{9,11},{10,... | collective-permute-start | bytes 1572872 | tf_op jit(solution)/shard_map/ppermute | solution.py:54
  47.6 28.2 %collective-permute-start.9 = (bf16[1,64,4096]{2,1,0:T(8,128)(2,1)}, bf16[1,64,4096]{2,1,0:T(8,128)(2,1)S(1)}, u32[]{:S(2)}, u32[]{:S(2)}) collective-permute-start(bf16[1,64,4096]{2,1,0:T(8,128)(2,1)} %collective-permute-done.2.refs_4_), channel_id=1, source_target_pairs={{0,1},{1,0},{2,3},{3,2},{4,5},{5,4},{6,7},{7,6},{8,9},{9,8},{10,11... | collective-permute-start | bytes 1572872 | tf_op jit(solution)/shard_map/ppermute | solution.py:54
  47.6 28.2 %collective-permute-start.8 = (bf16[136,4096]{1,0:T(8,128)(2,1)}, bf16[136,4096]{1,0:T(8,128)(2,1)S(1)}, u32[]{:S(2)}, u32[]{:S(2)}) collective-permute-start(bf16[136,4096]{1,0:T(8,128)(2,1)} %collective-permute-done.1.refs_2_.refs_1_), channel_id=1, source_target_pairs={{0,4},{4,0},{8,12},{12,8},{16,20},{20,16},{24,28},{28,24},{1,5},{5... | collective-permute-start | bytes 3342344 | tf_op jit(solution)/shard_map/ppermute | solution.py:54
  48.0 26.2 %collective-permute-start.6 = (bf16[1,64,4096]{2,1,0:T(8,128)(2,1)S(1)}, bf16[1,64,4096]{2,1,0:T(8,128)(2,1)S(1)}, u32[]{:S(2)}, u32[]{:S(2)}) collective-permute-start(bf16[1,64,4096]{2,1,0:T(8,128)(2,1)S(1)} %copy-done.3), channel_id=1, source_target_pairs={{0,16},{4,20},{8,24},{12,28},{16,0},{20,4},{24,8},{28,12},{1,17},{... | collective-permute-start | bytes 1572872 | tf_op jit(solution)/shard_map/ppermute | solution.py:54
  64.9 10.9 %collective-permute-start.10 = (bf16[1,64,4096]{2,1,0:T(8,128)(2,1)S(1)}, bf16[1,64,4096]{2,1,0:T(8,128)(2,1)S(1)}, u32[]{:S(2)}, u32[]{:S(2)}) collective-permute-start(bf16[1,64,4096]{2,1,0:T(8,128)(2,1)S(1)} %collective-permute-done.7.refs_5_), channel_id=1, source_target_pairs={{0,1},{1,0},{2,3},{3,2},{4,5},{5,4},{6,7},{7,6},{8,9},{9,8},{10,11... | collective-permute-start | bytes 1572872 | tf_op jit(solution)/shard_map/ppermute | solution.py:54
  74.2 25.3 %collective-permute-start.11 = (bf16[1,64,4096]{2,1,0:T(8,128)(2,1)S(1)}, bf16[1,64,4096]{2,1,0:T(8,128)(2,1)S(1)}, u32[]{:S(2)}, u32[]{:S(2)}) collective-permute-start(bf16[1,64,4096]{2,1,0:T(8,128)(2,1)S(1)} %collective-permute-done.6.refs_4_), channel_id=1, source_target_pairs={{0,2},{1,3},{2,0},{3,1},{4,6},{5,7},{6,4},{7,5},{8,10},{9,11},{10,... | collective-permute-start | bytes 1572872 | tf_op jit(solution)/shard_map/ppermute | solution.py:54
  75.8 24.3 %collective-permute-start.12 = (bf16[1,64,4096]{2,1,0:T(8,128)(2,1)S(1)}, bf16[1,64,4096]{2,1,0:T(8,128)(2,1)S(1)}, u32[]{:S(2)}, u32[]{:S(2)}) collective-permute-start(bf16[1,64,4096]{2,1,0:T(8,128)(2,1)S(1)} %collective-permute-done.6.refs_4_), channel_id=1, source_target_pairs={{0,1},{1,0},{2,3},{3,2},{4,5},{5,4},{6,7},{7,6},{8,9},{9,8},{10,11... | collective-permute-start | bytes 1572872 | tf_op jit(solution)/shard_map/ppermute | solution.py:54
  90.4 9.6 %copy-start.5 = (s32[128,2]{0,1:T(2,128)S(1)}, s32[128,2]{0,1:T(2,128)}, u32[]{:S(2)}) copy-start(s32[128,2]{0,1:T(2,128)} %param.10) | copy-start | bytes 3076
  99.4 2.1 %collective-permute-start.13 = (bf16[1,64,4096]{2,1,0:T(8,128)(2,1)S(1)}, bf16[1,64,4096]{2,1,0:T(8,128)(2,1)S(1)}, u32[]{:S(2)}, u32[]{:S(2)}) collective-permute-start(bf16[1,64,4096]{2,1,0:T(8,128)(2,1)S(1)} %collective-permute-done.11.refs_5_), channel_id=1, source_target_pairs={{0,1},{1,0},{2,3},{3,2},{4,5},{5,4},{6,7},{7,6},{8,9},{9,8},{10,11... | collective-permute-start | bytes 1572872 | tf_op jit(solution)/shard_map/ppermute | solution.py:54
  107.9 4.6 %collective-permute-start.14 = (f32[4,4,128]{2,1,0:T(4,128)S(1)}, f32[4,4,128]{2,1,0:T(4,128)S(1)}, u32[]{:S(2)}, u32[]{:S(2)}) collective-permute-start(f32[4,4,128]{2,1,0:T(4,128)S(1)} %pad_maximum_fusion.2), channel_id=1, source_target_pairs={{0,12},{4,8},{8,4},{12,0},{16,28},{20,24},{24,20},{28,16},{1,13},{... | collective-permute-start | bytes 24584 | tf_op jit(solution)/shard_map/ppermute | solution.py:54
  108.0 4.6 %collective-permute-start.15 = (f32[4,4,128]{2,1,0:T(4,128)S(1)}, f32[4,4,128]{2,1,0:T(4,128)S(1)}, u32[]{:S(2)}, u32[]{:S(2)}) collective-permute-start(f32[4,4,128]{2,1,0:T(4,128)S(1)} %pad_maximum_fusion.3), channel_id=1, source_target_pairs={{0,4},{4,0},{8,12},{12,8},{16,20},{20,16},{24,28},{28,24},{1,5},{5... | collective-permute-start | bytes 24584 | tf_op jit(solution)/shard_map/ppermute | solution.py:54
  108.0 5.0 %collective-permute-start.16 = (f32[4,4,128]{2,1,0:T(4,128)S(1)}, f32[4,4,128]{2,1,0:T(4,128)S(1)}, u32[]{:S(2)}, u32[]{:S(2)}) collective-permute-start(f32[4,4,128]{2,1,0:T(4,128)S(1)} %pad_maximum_fusion.4), channel_id=1, source_target_pairs={{0,8},{4,12},{8,0},{12,4},{16,24},{20,28},{24,16},{28,20},{1,9},{5... | collective-permute-start | bytes 24584 | tf_op jit(solution)/shard_map/ppermute | solution.py:54
